TPU v7x, 32 devices: a whole 2x2x4 slice. The times are simulated.
32 devices in a mesh: groups: 2 (over y), dom: 4 (over z), probe: 2 (over x), orb: 2 (over core).
Axes of the slice: x: 2, y: 2, z: 4, core: 2. Of those that a mesh axis runs over, the one named last changes fastest.
Arguments:
- probes: float32 [1024, 16, 256], P(('groups', 'dom', 'orb'), None, 'probe'), parts along dimension 0, may hold values from -6 to 6
- blocks: bfloat16 [20480, 16, 16], P(('groups', 'dom', 'orb')), parts along dimension 0, may hold values from -0.0625 to 0.0625
- block_rows: int32 [20480], P(('groups', 'dom', 'orb')), parts along dimension 0, may hold values from 0 to 63
- block_cols: int32 [20480], P(('groups', 'dom', 'orb')), parts along dimension 0, may hold values from 0 to 95
- counts: int32 [16], P(('groups', 'dom', 'orb')), parts along dimension 0, may hold values from 640 to 1280, as said below
Outputs:
- last_vector: float32 [1024, 16, 256], P(('groups', 'dom', 'orb'), None, 'probe'), parts along dimension 0
- moments: float32 [18, 256], P('groups', 'probe'), parts along dimension 0
There are 2 independent parts, one for each index of `groups`. A program takes and returns all parts, laid end to end along the dimension named above; each array names one. Nothing has to cross between parts.
Inputs may be any that keep to these rules, and one draw needn't show every extreme that they name: `counts`: some domain uses all 1280 slots in every draw.
All inputs are finite; a program needn't handle non-finite values.
Results may differ from a plain program's by a relative error of at most 0.0085.
Values may be sent and summed in bfloat16 or wider, within the bound.
No kernel may reach another device: no remote copies, remote signals or barrier semaphores. Data moves between devices by JAX's collectives and lax.ppermute only.
A program may use at most 192 MiB of HBM per device.

v0:
```python
import jax
import jax.numpy as jnp
from jax import lax
from jax.sharding import PartitionSpec as P

ORB = 16
STEPS = 8


def from_behind(block, axis, distance):
    devices = range(lax.axis_size(axis))
    route = [((i - distance) % len(devices), i) for i in devices]
    return lax.ppermute(block, axis, route)


def two_part(high, low, right):
    return jnp.dot(high, right, preferred_element_type=jnp.float32) + jnp.dot(
        low, right, preferred_element_type=jnp.float32
    )


def two_part_t(high, low, right):
    return jnp.einsum("ac,ap->cp", high, right, preferred_element_type=jnp.float32) + jnp.einsum(
        "ac,ap->cp", low, right, preferred_element_type=jnp.float32
    )


def per_device(probes, blocks, block_rows, block_cols, counts):
    atoms = probes.shape[0]
    orbits = probes.shape[1]
    width = probes.shape[2]
    halo_rows = atoms // 2
    columns = atoms + halo_rows
    slots = jnp.arange(blocks.shape[0], dtype=jnp.int32)
    used = slots < counts[0]
    flat_blocks = jnp.where(
        used[:, None], blocks.astype(jnp.float32).reshape(blocks.shape[0], -1), jnp.float32(0.0)
    )
    pair_index = block_rows * columns + block_cols
    summed = jax.ops.segment_sum(flat_blocks, pair_index, num_segments=atoms * columns)
    dense = summed.reshape(atoms, columns, orbits, orbits).transpose(0, 2, 1, 3)
    dense = dense.reshape(atoms * orbits, columns * orbits)
    high = dense.astype(jnp.bfloat16)
    low = (dense - high.astype(jnp.float32)).astype(jnp.bfloat16)
    local_width = atoms * orbits
    scale = jnp.float32(1.0 / (atoms * ORB * lax.axis_size(("dom", "orb"))))

    def apply_ham(vector):
        rounded = vector.astype(jnp.bfloat16)
        edge = from_behind(rounded[:halo_rows], ("dom", "orb"), -1)
        extended = jnp.concatenate([rounded, edge], axis=0).reshape(columns * orbits, width)
        flat_local = rounded.reshape(local_width, width)
        forward = two_part(high, low, extended)
        backward = two_part_t(high, low, flat_local)
        totals = forward + backward[:local_width]
        back_terms = from_behind(backward[local_width:], ("dom", "orb"), 1)
        totals = totals.at[: halo_rows * orbits].add(back_terms)
        return totals.reshape(atoms, orbits, width)

    def moment(vector):
        local_term = jnp.sum(probes * vector, axis=(0, 1)) * scale
        return lax.psum(local_term, ("dom", "orb"))

    moments = jnp.zeros((STEPS + 1, width), jnp.float32)
    moments = moments.at[0].set(moment(probes))
    current = apply_ham(probes)
    moments = moments.at[1].set(moment(current))

    def one_turn(index, carry):
        previous, present, table = carry
        following_vec = 2.0 * apply_ham(present) - previous
        table = lax.dynamic_update_slice_in_dim(table, moment(following_vec)[None], index + 1, 0)
        return (present, following_vec, table)

    previous, current, moments = lax.fori_loop(1, STEPS, one_turn, (probes, current, moments))
    return (current, moments)


def solution(mesh):
    in_specs = (
        P(("groups", "dom", "orb"), None, "probe"),
        P(("groups", "dom", "orb"), None, None),
        P(("groups", "dom", "orb")),
        P(("groups", "dom", "orb")),
        P(("groups", "dom", "orb")),
    )
    out_specs = (P(("groups", "dom", "orb"), None, "probe"), P("groups", "probe"))
    return jax.shard_map(
        per_device, mesh=mesh, in_specs=in_specs, out_specs=out_specs, check_vma=False
    )
```

profile of v0, /device:TPU:0, one launch (start us, length us, event | category | flops | bytes accessed | tf_op | source)
XLA Modules:
  0.0 542.8 jit_solution(17154623070789735047)
XLA Ops:
  1.8 4.5 collective-permute-start.2
  8.6 13.9 %scatter_custom_fusion = f32[6144,256]{1,0:T(8,128)} fusion(s32[1280]{0:T(1024)S(1)} %multiply_add_fusion, f32[]{:T(128)} %constant.247.clone.1, f32[1280,256]{1,0:T(8,128)S(1)} %copy.16, pred[1280]{0:T(1024)(128)(4,1)S(1)} %iota_compare_fusion), kind=kCustom, calls=%fused_computation.13 | custom fusion | flops 655360 | bytes 7605248 | tf_op jit(solution)/shard_map/scatter-add | solution.py:40
  22.5 6.6 %copy.17 = f32[6144,256]{0,1:T(8,128)} copy(f32[6144,256]{1,0:T(8,128)} %scatter_custom_fusion) | data formatting | bytes 12582912 | tf_op jit(solution)/shard_map/scatter-add | solution.py:40
  29.1 9.0 %reshape.208 = f32[64,96,16,16]{1,0,3,2:T(8,128)} reshape(f32[6144,256]{0,1:T(8,128)} %copy.17) | data formatting | bytes 12582912 | tf_op jit(solution)/shard_map/reshape | solution.py:41
  38.1 6.6 %bitcast_convert_fusion.1 = bf16[64,16,96,16]{2,0,3,1:T(8,128)(2,1)} fusion(f32[64,96,16,16]{1,0,3,2:T(8,128)} %reshape.208), kind=kLoop, calls=%fused_computation.31 | loop fusion | flops 1572864 | bytes 9437184 | tf_op jit(solution)/shard_map/convert_element_type | solution.py:43
  47.9 21.0 %copy.18 = bf16[64,16,96,16]{3,2,1,0:T(8,128)(2,1)} copy(bf16[64,16,96,16]{2,0,3,1:T(8,128)(2,1)} %bitcast_convert_fusion.1) | data formatting | bytes 6291456 | tf_op jit(solution)/shard_map/convert_element_type | solution.py:43
  68.8 41.3 %convert_element_type.48 = bf16[1024,1536]{1,0:T(8,128)(2,1)S(1)} reshape(bf16[64,16,96,16]{3,2,1,0:T(8,128)(2,1)} %copy.18) | data formatting | bytes 6291456 | tf_op jit(solution)/shard_map/convert_element_type | solution.py:43
  110.1 21.2 %copy.19 = bf16[64,16,96,16]{3,2,1,0:T(8,128)(2,1)} copy(bf16[64,16,96,16]{2,0,3,1:T(8,128)(2,1)} %subtract_convert_fusion) | data formatting | bytes 6291456 | tf_op jit(solution)/shard_map/convert_element_type | solution.py:44
  131.3 42.1 %convert_element_type.52 = bf16[1024,1536]{1,0:T(8,128)(2,1)} reshape(bf16[64,16,96,16]{3,2,1,0:T(8,128)(2,1)} %copy.19) | data formatting | bytes 6291456 | tf_op jit(solution)/shard_map/convert_element_type | solution.py:44
  178.0 28.8 %copy.20 = f32[64,16,96,16]{3,2,1,0:T(8,128)} copy(f32[64,16,96,16]{2,0,3,1:T(8,128)} %bitcast.78) | data formatting | bytes 12582912 | tf_op jit(solution)/shard_map/transpose | solution.py:41
  206.7 41.2 %reshape.214 = f32[1024,1536]{1,0:T(8,128)} reshape(f32[64,16,96,16]{3,2,1,0:T(8,128)} %copy.20) | data formatting | bytes 12582912 | tf_op jit(solution)/shard_map/reshape | solution.py:42
  247.9 8.0 %subtract_convert_fusion.1 = (bf16[1024,1536]{1,0:T(8,128)(2,1)S(1)}, bf16[1024,1536]{1,0:T(8,128)(2,1)}) fusion(f32[1024,1536]{1,0:T(8,128)} %reshape.214), kind=kLoop, calls=%fused_computation.12 | loop fusion | flops 6291456 | bytes 12582912 | tf_op jit(solution)/shard_map/convert_element_type | solution.py:44
  263.7 17.1 %all-reduce.1 = (f32[1,128]{1,0:T(1,128)S(1)}, f32[1,128]{1,0:T(1,128)S(1)}) all-reduce(f32[1,128]{1,0:T(1,128)S(1)} %get-tuple-element.377, f32[1,128]{1,0:T(1,128)S(1)} %get-tuple-element.376), channel_id=1, replica_groups=mesh['groups'=2,'dom'=4,'probe'=2,'orb'=2] {'dom','orb'}, use_global_device_ids=true, to_apply=%region_2.3 | all-reduce | flops 256 | bytes 2048 | tf_op jit(solution)/shard_map/psum | solution.py:62
  280.9 261.3 %while.27 = (s32[]{:T(128)}, f32[64,16,128]{2,1,0:T(8,128)}, f32[64,16,128]{2,1,0:T(8,128)}, f32[9,128]{1,0:T(8,128)S(1)}, bf16[1024,1536]{1,0:T(8,128)(2,1)}, /...) while((s32[]{:T(128)}, f32[64,16,128]{2,1,0:T(8,128)}, ...), condition=%wide.region_8.9_spmd, body=%wide.region_5.8_spmd.sunk | while | flops 1611989120 | bytes 48238400 | solution.py:75
  302.8 13.6 %psum.37 = f32[1,128]{1,0:T(1,128)S(1)} all-reduce(f32[1,128]{1,0:T(1,128)S(1)} %multiply_bitcast_fusion.4), channel_id=1, replica_groups=mesh['groups'=2,'dom'=4,'probe'=2,'orb'=2] {'dom','orb'}, use_global_device_ids=true, to_apply=%region_7.7 | all-reduce | flops 128 | bytes 1024 | tf_op jit(solution)/shard_map/while/body/eval_jaxpr/psum | solution.py:62
  328.1 4.0 collective-permute-done.1
  340.1 13.6 %psum.37 = f32[1,128]{1,0:T(1,128)S(1)} all-reduce(f32[1,128]{1,0:T(1,128)S(1)} %multiply_bitcast_fusion.4), channel_id=1, replica_groups=mesh['groups'=2,'dom'=4,'probe'=2,'orb'=2] {'dom','orb'}, use_global_device_ids=true, to_apply=%region_7.7 | all-reduce | flops 128 | bytes 1024 | tf_op jit(solution)/shard_map/while/body/eval_jaxpr/psum | solution.py:62
  365.5 4.0 collective-permute-done.1
  377.4 13.6 %psum.37 = f32[1,128]{1,0:T(1,128)S(1)} all-reduce(f32[1,128]{1,0:T(1,128)S(1)} %multiply_bitcast_fusion.4), channel_id=1, replica_groups=mesh['groups'=2,'dom'=4,'probe'=2,'orb'=2] {'dom','orb'}, use_global_device_ids=true, to_apply=%region_7.7 | all-reduce | flops 128 | bytes 1024 | tf_op jit(solution)/shard_map/while/body/eval_jaxpr/psum | solution.py:62
  414.8 13.6 %psum.37 = f32[1,128]{1,0:T(1,128)S(1)} all-reduce(f32[1,128]{1,0:T(1,128)S(1)} %multiply_bitcast_fusion.4), channel_id=1, replica_groups=mesh['groups'=2,'dom'=4,'probe'=2,'orb'=2] {'dom','orb'}, use_global_device_ids=true, to_apply=%region_7.7 | all-reduce | flops 128 | bytes 1024 | tf_op jit(solution)/shard_map/while/body/eval_jaxpr/psum | solution.py:62
  452.1 13.6 %psum.37 = f32[1,128]{1,0:T(1,128)S(1)} all-reduce(f32[1,128]{1,0:T(1,128)S(1)} %multiply_bitcast_fusion.4), channel_id=1, replica_groups=mesh['groups'=2,'dom'=4,'probe'=2,'orb'=2] {'dom','orb'}, use_global_device_ids=true, to_apply=%region_7.7 | all-reduce | flops 128 | bytes 1024 | tf_op jit(solution)/shard_map/while/body/eval_jaxpr/psum | solution.py:62
  477.4 4.0 collective-permute-done.1
  489.4 13.6 %psum.37 = f32[1,128]{1,0:T(1,128)S(1)} all-reduce(f32[1,128]{1,0:T(1,128)S(1)} %multiply_bitcast_fusion.4), channel_id=1, replica_groups=mesh['groups'=2,'dom'=4,'probe'=2,'orb'=2] {'dom','orb'}, use_global_device_ids=true, to_apply=%region_7.7 | all-reduce | flops 128 | bytes 1024 | tf_op jit(solution)/shard_map/while/body/eval_jaxpr/psum | solution.py:62
  526.7 13.6 %psum.37 = f32[1,128]{1,0:T(1,128)S(1)} all-reduce(f32[1,128]{1,0:T(1,128)S(1)} %multiply_bitcast_fusion.4), channel_id=1, replica_groups=mesh['groups'=2,'dom'=4,'probe'=2,'orb'=2] {'dom','orb'}, use_global_device_ids=true, to_apply=%region_7.7 | all-reduce | flops 128 | bytes 1024 | tf_op jit(solution)/shard_map/while/body/eval_jaxpr/psum | solution.py:62
  (225 shorter events, 172.4 us)
Async XLA Ops:
  0.6 7.9 %copy-start.13 = (s32[1280]{0:T(1024)S(1)}, s32[1280]{0:T(1024)}, u32[]{:S(2)}) copy-start(s32[1280]{0:T(1024)} %param.17) | copy-start | bytes 15364
  0.6 7.9 %copy-start.12 = (s32[1280]{0:T(1024)S(1)}, s32[1280]{0:T(1024)}, u32[]{:S(2)}) copy-start(s32[1280]{0:T(1024)} %param.18) | copy-start | bytes 15364
  1.8 255.0 %collective-permute-start.2 = (bf16[32,16,128]{2,1,0:T(8,128)(2,1)S(1)}, bf16[32,16,128]{2,1,0:T(8,128)(2,1)}, u32[]{:S(2)}, u32[]{:S(2)}) collective-permute-start(bf16[32,16,128]{2,1,0:T(8,128)(2,1)S(1)} %slice.154), channel_id=1, source_target_pairs={{1,0},{4,1},{5,4},{8,5},{9,8},{12,9},{13,12},{0,13},{3,2},{6,3},{7... | collective-permute-start | bytes 393224 | tf_op jit(solution)/shard_map/ppermute | solution.py:13
  38.1 6.6 %copy-start.1 = (f32[64,96,16,16]{1,0,3,2:T(8,128)S(1)}, f32[64,96,16,16]{1,0,3,2:T(8,128)}, u32[]{:S(2)}) copy-start(f32[64,96,16,16]{1,0,3,2:T(8,128)} %reshape.208) | copy-start | bytes 18874372
  110.1 63.4 %copy-start.5 = (bf16[1024,1536]{1,0:T(8,128)(2,1)}, bf16[1024,1536]{1,0:T(8,128)(2,1)S(1)}, u32[]{:S(2)}) copy-start(bf16[1024,1536]{1,0:T(8,128)(2,1)S(1)} %convert_element_type.48) | copy-start | bytes 9437188
  178.0 83.8 %collective-permute-start.3 = (f32[512,128]{1,0:T(8,128)}, f32[512,128]{1,0:T(8,128)}, u32[]{:S(2)}, u32[]{:S(2)}) collective-permute-start(f32[512,128]{1,0:T(8,128)} %slice.157), channel_id=1, source_target_pairs={{13,0},{0,1},{1,4},{4,5},{5,8},{8,9},{9,12},{12,13},{15,2},{2,3},{... | collective-permute-start | bytes 786440 | tf_op jit(solution)/shard_map/ppermute | solution.py:13
  247.9 8.0 %copy-start.8 = (f32[64,16,128]{2,1,0:T(8,128)S(1)}, f32[64,16,128]{2,1,0:T(8,128)}, u32[]{:S(2)}) copy-start(f32[64,16,128]{2,1,0:T(8,128)} %param.15) | copy-start | bytes 1572868
  257.7 3.0 copy-start.6
  257.7 3.0 copy-start.11
  260.7 2.8 copy-start.9
  282.0 5.3 collective-permute-start
  286.9 7.9 %collective-permute-start.1 = (f32[512,128]{0,1:T(8,128)}, f32[512,128]{0,1:T(8,128)}, u32[]{:S(2)}, u32[]{:S(2)}) collective-permute-start(f32[512,128]{0,1:T(8,128)} %slice.173), channel_id=1, source_target_pairs={{13,0},{0,1},{1,4},{4,5},{5,8},{8,9},{9,12},{12,13},{15,2},{2,3},{... | collective-permute-start | bytes 786440 | tf_op jit(solution)/shard_map/while/body/eval_jaxpr/ppermute | solution.py:13
  319.4 5.3 collective-permute-start
  324.2 7.9 %collective-permute-start.1 = (f32[512,128]{0,1:T(8,128)}, f32[512,128]{0,1:T(8,128)}, u32[]{:S(2)}, u32[]{:S(2)}) collective-permute-start(f32[512,128]{0,1:T(8,128)} %slice.173), channel_id=1, source_target_pairs={{13,0},{0,1},{1,4},{4,5},{5,8},{8,9},{9,12},{12,13},{15,2},{2,3},{... | collective-permute-start | bytes 786440 | tf_op jit(solution)/shard_map/while/body/eval_jaxpr/ppermute | solution.py:13
  356.7 5.3 collective-permute-start
  361.5 7.9 %collective-permute-start.1 = (f32[512,128]{0,1:T(8,128)}, f32[512,128]{0,1:T(8,128)}, u32[]{:S(2)}, u32[]{:S(2)}) collective-permute-start(f32[512,128]{0,1:T(8,128)} %slice.173), channel_id=1, source_target_pairs={{13,0},{0,1},{1,4},{4,5},{5,8},{8,9},{9,12},{12,13},{15,2},{2,3},{... | collective-permute-start | bytes 786440 | tf_op jit(solution)/shard_map/while/body/eval_jaxpr/ppermute | solution.py:13
  394.0 5.3 collective-permute-start
  398.8 7.9 %collective-permute-start.1 = (f32[512,128]{0,1:T(8,128)}, f32[512,128]{0,1:T(8,128)}, u32[]{:S(2)}, u32[]{:S(2)}) collective-permute-start(f32[512,128]{0,1:T(8,128)} %slice.173), channel_id=1, source_target_pairs={{13,0},{0,1},{1,4},{4,5},{5,8},{8,9},{9,12},{12,13},{15,2},{2,3},{... | collective-permute-start | bytes 786440 | tf_op jit(solution)/shard_map/while/body/eval_jaxpr/ppermute | solution.py:13
  431.3 5.3 collective-permute-start
  436.2 7.9 %collective-permute-start.1 = (f32[512,128]{0,1:T(8,128)}, f32[512,128]{0,1:T(8,128)}, u32[]{:S(2)}, u32[]{:S(2)}) collective-permute-start(f32[512,128]{0,1:T(8,128)} %slice.173), channel_id=1, source_target_pairs={{13,0},{0,1},{1,4},{4,5},{5,8},{8,9},{9,12},{12,13},{15,2},{2,3},{... | collective-permute-start | bytes 786440 | tf_op jit(solution)/shard_map/while/body/eval_jaxpr/ppermute | solution.py:13
  468.7 5.3 collective-permute-start
  473.5 7.9 %collective-permute-start.1 = (f32[512,128]{0,1:T(8,128)}, f32[512,128]{0,1:T(8,128)}, u32[]{:S(2)}, u32[]{:S(2)}) collective-permute-start(f32[512,128]{0,1:T(8,128)} %slice.173), channel_id=1, source_target_pairs={{13,0},{0,1},{1,4},{4,5},{5,8},{8,9},{9,12},{12,13},{15,2},{2,3},{... | collective-permute-start | bytes 786440 | tf_op jit(solution)/shard_map/while/body/eval_jaxpr/ppermute | solution.py:13
  506.0 5.3 collective-permute-start
  510.8 7.9 %collective-permute-start.1 = (f32[512,128]{0,1:T(8,128)}, f32[512,128]{0,1:T(8,128)}, u32[]{:S(2)}, u32[]{:S(2)}) collective-permute-start(f32[512,128]{0,1:T(8,128)} %slice.173), channel_id=1, source_target_pairs={{13,0},{0,1},{1,4},{4,5},{5,8},{8,9},{9,12},{12,13},{15,2},{2,3},{... | collective-permute-start | bytes 786440 | tf_op jit(solution)/shard_map/while/body/eval_jaxpr/ppermute | solution.py:13
  (25 other events, 42.1 us)
where the time goes:
time: 548 us; the launch traced here: 543 us
  local copies, waits for them, and re-layouts  268 us (49%)
  blocking collectives  112 us (20%)
  other arithmetic  80 us (15%)
  matrix products  44.3 us (8%)
  waiting for transfers between devices  27.8 us (5%)
  starting transfers between devices  8.42 us (2%)
    psum x8, blocking collectives, moment(): return lax.psum(local_term, ('dom', 'orb'))  112 us
    convert_element_type x2, local copies, waits for them, and re-layouts, per_device(): low = (dense - high.astype(jnp.float32)).astype(jnp.bfloat16)  63.3 us
    convert_element_type x2, local copies, waits for them, and re-layouts, per_device(): high = dense.astype(jnp.bfloat16)  62.2 us
    reshape x1, local copies, waits for them, and re-layouts, per_device(): dense = dense.reshape(atoms * orbits, columns * orbits)  41.2 us
    while x56, local copies, waits for them, and re-layouts  32.3 us
    transpose x1, local copies, waits for them, and re-layouts, per_device(): dense = summed.reshape(atoms, columns, orbits, orbits).transpose(0, 2, 1, 3)  28.8 us
    ppermute x16, waiting for transfers between devices, from_behind(): return lax.ppermute(block, axis, route)  27.8 us
    dot_general x8, matrix products, two_part_t(): jnp.einsum('ac,ap->cp', high, right, preferred_element_type=jnp.float32)  18.6 us
  transfers between devices with their start and end apart: 16, of which 7 were waited for; matrix products, arithmetic and copies ran while one was open for 56% of the time, Pallas kernels for 0%

commit v1 on v0

v1 whole, which is shorter than its diff:
```python
import functools

import jax
import jax.numpy as jnp
from jax import lax
from jax.experimental import pallas as pl
from jax.experimental.pallas import tpu as pltpu
from jax.sharding import PartitionSpec as P

STEPS = 8
RING = ("dom", "orb")
F32, BF16 = jnp.float32, jnp.bfloat16
VMEM = pl.BlockSpec(memory_space=pltpu.VMEM)
SMEM = pl.BlockSpec(memory_space=pltpu.SMEM)


def call(body, outs, flops, *operands, scratch=(), smem=0, limit=16):
    size = sum(o.size * o.dtype.itemsize for o in operands)
    return pl.pallas_call(
        body,
        out_shape=tuple(jax.ShapeDtypeStruct(s, t) for s, t in outs),
        in_specs=[SMEM] * smem + [VMEM] * (len(operands) - smem),
        out_specs=(VMEM,) * len(outs),
        scratch_shapes=scratch,
        compiler_params=pltpu.CompilerParams(vmem_limit_bytes=limit << 20),
        cost_estimate=pl.CostEstimate(flops=flops, bytes_accessed=size, transcendentals=0),
    )(*operands)


def build_body(atoms, orbits, halo, counts, rows, cols, blocks, own_ref, cross_ref, crosst_ref, own_f32, cross_f32):
    chunk = 4 * atoms
    slots = blocks.shape[1]
    slot = lax.broadcasted_iota(jnp.int32, (1, slots), 1)
    pair = jnp.where(slot < counts[0], cols[...] * atoms + rows[...], -1)
    row_id = lax.broadcasted_iota(jnp.int32, (chunk, slots), 0)
    lane = lax.broadcasted_iota(jnp.int32, (orbits, 2 * atoms), 1)

    def place(first, total, target):
        def one(q, _):
            col = first + 4 * q
            onehot = jnp.where(row_id + col * atoms == pair, 1.0, 0.0).astype(BF16)
            tile = lax.dot_general(blocks[...], onehot, (((1,), (1,)), ((), ())), preferred_element_type=F32)
            for two in range(2):
                for i in range(0, orbits, 2):
                    lanes = slice(two * 2 * atoms, (two + 1) * 2 * atoms)
                    left = tile[i * orbits : (i + 1) * orbits, lanes]
                    right = tile[(i + 1) * orbits : (i + 2) * orbits, lanes]
                    low = jnp.where(lane < atoms, left, pltpu.roll(right, atoms, 1))
                    high = jnp.where(lane < atoms, pltpu.roll(left, atoms, 1), right)
                    target[i // 2, pl.ds(4 * q + 2 * two, orbits, stride=total), :] = low
                    target[i // 2, pl.ds(4 * q + 2 * two + 1, orbits, stride=total), :] = high
            return 0

        lax.fori_loop(0, total // 4, one, 0)

    place(0, atoms, own_f32)
    place(atoms, halo, cross_f32)

    size = atoms * orbits
    step = 256
    eye = (
        lax.broadcasted_iota(jnp.int32, (step, step), 0) == lax.broadcasted_iota(jnp.int32, (step, step), 1)
    ).astype(BF16)
    nt = (((1,), (1,)), ((), ()))
    lanes = 2 * atoms
    pieces = size // lanes
    for p in range(pieces):
        crosst_ref[:, p * lanes : (p + 1) * lanes] = cross_f32[p].astype(BF16)
    for t in range(0, size, step):
        part = jnp.concatenate([own_f32[t // lanes + n] for n in range(step // lanes)], axis=1)
        high = part.astype(BF16)
        low = (part - high.astype(F32)).astype(BF16)
        turned = lax.dot_general(eye, high, nt, preferred_element_type=F32)
        turned = turned + lax.dot_general(eye, low, nt, preferred_element_type=F32)
        for p in range(pieces):
            at = slice(p * lanes, (p + 1) * lanes)
            own_ref[t : t + step, at] = (own_f32[p, t : t + step, :] + turned[:, at]).astype(BF16)
        cross_ref[t : t + step, :] = lax.dot_general(
            eye, crosst_ref[:, t : t + step], nt, preferred_element_type=F32
        ).astype(BF16)


def load_body(atoms, orbits, turn, probes, v_ref, w_ref):
    for o in range(orbits):
        v = probes[pl.ds(o, atoms, stride=orbits), :] if turn else probes[o * atoms : (o + 1) * atoms, :]
        v_ref[o * atoms : (o + 1) * atoms, :] = v
        w_ref[o * atoms : (o + 1) * atoms, :] = v.astype(BF16)


def put_sends(atoms, orbits, halo, even, w, products, out_x, out_i):
    for o in range(orbits):
        edge = w[o * atoms : o * atoms + halo, :]
        product = products[o * halo : (o + 1) * halo, :]
        out_x[o * halo : (o + 1) * halo, :] = jnp.where(even, edge, product)
        out_i[o * halo : (o + 1) * halo, :] = jnp.where(even, product, edge)


def first_body(atoms, orbits, halo, parity, w_ref, crosst, out_x, out_i):
    products = jnp.dot(crosst[...], w_ref[...], preferred_element_type=F32).astype(BF16)
    put_sends(atoms, orbits, halo, parity[0] == 0, w_ref, products, out_x, out_i)


def own_body(own, w, v0, v, local_ref, moment_ref):
    local_ref[...] = jnp.dot(own[...], w[...], preferred_element_type=F32)
    moment_ref[...] = jnp.sum(v0[...] * v[...], axis=0, keepdims=True)


def next_vector(atoms, orbits, halo, first, even, got_x, got_i, local, previous, cross, write):
    edge = jnp.where(even, got_i[...], got_x[...])
    total = local[...] + jnp.dot(cross[...], edge, preferred_element_type=F32)
    for o in range(orbits):
        part = total[o * atoms : (o + 1) * atoms, :]
        back = jnp.where(even, got_x[o * halo : (o + 1) * halo, :], got_i[o * halo : (o + 1) * halo, :])
        for at, piece in ((0, part[:halo] + back.astype(F32)), (halo, part[halo:])):
            rows = slice(o * atoms + at, o * atoms + at + piece.shape[0])
            write(o, at, piece if first else 2.0 * piece - previous[rows, :])


def step_body(
    atoms, orbits, halo, first, parity, got_x, got_i, local, previous, cross, crosst, v_ref, w_ref, out_x, out_i
):
    even = parity[0] == 0

    def write(o, at, piece):
        rows = slice(o * atoms + at, o * atoms + at + piece.shape[0])
        v_ref[rows, :] = piece
        w_ref[rows, :] = piece.astype(BF16)

    next_vector(atoms, orbits, halo, first, even, got_x, got_i, local, previous, cross, write)
    products = jnp.dot(crosst[...], w_ref[...], preferred_element_type=F32).astype(BF16)
    put_sends(atoms, orbits, halo, even, w_ref, products, out_x, out_i)


def last_body(atoms, orbits, halo, turn, parity, got_x, got_i, local, previous, cross, v0, out_ref, moment_ref):
    sums = []

    def write(o, at, piece):
        rows = slice(o * atoms + at, o * atoms + at + piece.shape[0])
        out_ref[pl.ds(at * orbits + o, piece.shape[0], stride=orbits) if turn else rows, :] = piece
        sums.append(jnp.sum(v0[rows, :] * piece, axis=0, keepdims=True))

    next_vector(atoms, orbits, halo, False, parity[0] == 0, got_x, got_i, local, previous, cross, write)
    moment_ref[...] = functools.reduce(jnp.add, sums)


def per_device(probes, blocks, block_rows, block_cols, counts):
    atoms, orbits, width = probes.shape
    halo = atoms // 2
    size, edge_size = atoms * orbits, halo * orbits
    slots = blocks.shape[0]
    dims = (atoms, orbits, halo)
    turn = width == 128
    ring = lax.axis_size(RING)
    scale = jnp.float32(1.0 / (size * ring))
    parity = lax.axis_index("orb").astype(jnp.int32).reshape(1)
    between = [(i, (i + 1) % ring) for i in range(1, ring, 2)]
    between = between + [(b, a) for a, b in between]
    inside = [(0, 1), (1, 0)]

    def exchange(send_x, send_i):
        return lax.ppermute(send_x, RING, between), lax.ppermute(send_i, "orb", inside)

    flat = blocks.transpose(1, 2, 0).reshape(orbits * orbits, slots)
    own, cross, crosst = call(
        functools.partial(build_body, *dims),
        (((size, size), BF16), ((size, edge_size), BF16), ((edge_size, size), BF16)),
        2 * orbits * orbits * slots * atoms * (atoms + halo),
        counts,
        block_rows.reshape(1, slots),
        block_cols.reshape(1, slots),
        flat,
        scratch=[
            pltpu.VMEM((orbits // 2, size, 2 * atoms), F32),
            pltpu.VMEM((orbits // 2, edge_size, 2 * atoms), F32),
        ],
        smem=1,
        limit=32,
    )
    v0, w = call(
        functools.partial(load_body, atoms, orbits, turn),
        (((size, width), F32), ((size, width), BF16)),
        0,
        (probes if turn else probes.transpose(1, 0, 2)).reshape(size, width),
    )
    sends = (((edge_size, width), BF16),) * 2
    cross_flops = 2 * size * edge_size * width
    send_x, send_i = call(functools.partial(first_body, *dims), sends, cross_flops, parity, w, crosst, smem=1)
    previous, v = v0, v0
    moments = []
    for k in range(STEPS):
        got_x, got_i = exchange(send_x, send_i)
        local, moment = call(
            own_body, (((size, width), F32), ((1, width), F32)), 2 * size * size * width, own, w, v0, v
        )
        moments.append(moment)
        if k < STEPS - 1:
            following, w, send_x, send_i = call(
                functools.partial(step_body, *dims, k == 0),
                (((size, width), F32), ((size, width), BF16)) + sends,
                2 * cross_flops,
                parity, got_x, got_i, local, previous, cross, crosst,
                smem=1,
            )
            previous, v = v, following
        else:
            last, moment = call(
                functools.partial(last_body, *dims, turn),
                (((size, width), F32), ((1, width), F32)),
                cross_flops,
                parity, got_x, got_i, local, previous, cross, v0,
                smem=1,
            )
            moments.append(moment)
    table = lax.psum(jnp.concatenate(moments, axis=0) * scale, RING)
    last = last.reshape(atoms, orbits, width) if turn else last.reshape(orbits, atoms, width).transpose(1, 0, 2)
    return last, table


def solution(mesh):
    in_specs = (
        P(("groups", "dom", "orb"), None, "probe"),
        P(("groups", "dom", "orb"), None, None),
        P(("groups", "dom", "orb")),
        P(("groups", "dom", "orb")),
        P(("groups", "dom", "orb")),
    )
    out_specs = (P(("groups", "dom", "orb"), None, "probe"), P("groups", "probe"))
    return jax.shard_map(
        per_device, mesh=mesh, in_specs=in_specs, out_specs=out_specs, check_vma=False
    )
```

time: 548 us -> 102 us (0.19)
  local copies, waits for them, and re-layouts: 268 us -> 3.56 us
  blocking collectives: 112 us -> 17.1 us
  other arithmetic: 80 us -> 0.01 us
  matrix products: 44.3 us -> 0 us
  Pallas kernels: 0 us -> 33 us
  starting transfers between devices: 8.42 us -> 24 us
    convert_element_type x4 -> x0, local copies, waits for them, and re-layouts: 126 us -> none  [the longest x2 63.3 us: per_device(): low = (dense - high.astype(jnp.float32)).astype(jnp.bfloat16)]
    psum x8 -> x1, blocking collectives: 112 us -> 17.1 us  [per_device(): table = lax.psum(jnp.concatenate(moments, axis=0) * scale, RING)]
    reshape x3 -> x2, local copies, waits for them, and re-layouts: 50.6 us -> 1.4 us  [the longest x1 0.7 us: per_device(): block_rows.reshape(1, slots)]
    dot_general x32 -> x0, matrix products: 44.3 us -> none  [the longest x8 18.6 us: two_part_t(): jnp.einsum('ac,ap->cp', high, right, preferred_element_type=jnp.float32)]
    pallas_call x0 -> x19, Pallas kernels: none -> 33 us  [call(): pl.pallas_call(body, out_shape=tuple((jax.ShapeDtypeStruct(s, t) for s, t...]
    while x56 -> x0, local copies, waits for them, and re-layouts: 32.3 us -> none
    transpose x1 -> x0, local copies, waits for them, and re-layouts: 28.8 us -> none  [per_device(): dense = summed.reshape(atoms, columns, orbits, orbits).transpose(0, 2, 1, 3)]
    convert_element_type x11 -> x0, other arithmetic: 26.4 us -> none  [the longest x2 11.1 us: per_device(): low = (dense - high.astype(jnp.float32)).astype(jnp.bfloat16)]
  transfers between devices with their start and end apart: 16 -> 16, of which waited for: 7 -> 8; matrix products, arithmetic and copies ran while one was open for 56% -> 0% of each run, Pallas kernels for 0% -> 6%
where the time goes in v1:
time: 102 us
  Pallas kernels  33 us (32%)
  starting transfers between devices  24 us (24%)
  waiting for transfers between devices  22.7 us (22%)
  blocking collectives  17.1 us (17%)
  local copies, waits for them, and re-layouts  3.56 us (3%)
  between operations  1.42 us (1%)
    pallas_call x19, Pallas kernels, call(): pl.pallas_call(body, out_shape=tuple((jax.ShapeDtypeStruct(s, t) for s, t...  33 us
    ppermute x8, starting transfers between devices, exchange(): lax.ppermute(send_x, RING, between)  24 us
    ppermute x8, waiting for transfers between devices, exchange(): lax.ppermute(send_x, RING, between)  22.7 us
    psum x1, blocking collectives, per_device(): table = lax.psum(jnp.concatenate(moments, axis=0) * scale, RING)  17.1 us
    unnamed x4, local copies, waits for them, and re-layouts  2.12 us
  transfers between devices with their start and end apart: 16, of which 8 were waited for; matrix products, arithmetic and copies ran while one was open for 0% of the time, Pallas kernels for 6%

profile of v1, /device:TPU:0, one launch (start us, length us, event | category | flops | bytes accessed | tf_op | source)
XLA Modules:
  0.0 101.8 jit_solution(17375128192763078986)
XLA Ops:
  5.0 16.9 %shard_map.69 = (bf16[1024,1024]{1,0:T(8,128)(2,1)S(1)}, bf16[1024,512]{1,0:T(8,128)(2,1)S(1)}, bf16[512,1024]{1,0:T(8,128)(2,1)S(1)}) custom-call(s32[1]{0:T(128)S(6)} %copy.7.counts, s32[1,1280]{1,0:T(1,128)S(1)} %reshape.24.rows, s32[1,1280]{1,0:T(1,128)S(1)} %reshape.25.cols, bf16[256,1280]{1,0:T(8,128)(2,1)S(1)} %bitcast.7), custom_call_target="tpu_custom_call" | custom-call | flops 4026531840 | bytes 665604 | tf_op jit(solution)/shard_map/pallas_call | solution.py:19
  22.4 4.6 %collective-permute-start = (bf16[512,128]{1,0:T(8,128)(2,1)S(1)}, bf16[512,128]{1,0:T(8,128)(2,1)S(1)}, u32[]{:S(2)}, u32[]{:S(2)}) collective-permute-start(bf16[512,128]{1,0:T(8,128)(2,1)S(1)} %get-tuple-element.57), channel_id=1, source_target_pairs={{1,4},{5,8},{9,12},{13,0},{4,1},{8,5},{12,9},{0,13},{3,6},{7,10},{... | collective-permute-start | bytes 393224 | tf_op jit(solution)/shard_map/ppermute | solution.py:161
  27.7 2.5 %collective-permute-done.got_x = bf16[512,128]{1,0:T(8,128)(2,1)S(1)} collective-permute-done((bf16[512,128]{1,0:T(8,128)(2,1)S(1)}, bf16[512,128]{1,0:T(8,128)(2,1)S(1)}, u32[]{:S(2)}, u32[]{:S(2)}) %collective-permute-start) | collective-permute-done | bytes 131104 | tf_op jit(solution)/shard_map/ppermute | solution.py:161
  31.4 3.0 %collective-permute-start.2 = (bf16[512,128]{1,0:T(8,128)(2,1)S(1)}, bf16[512,128]{1,0:T(8,128)(2,1)S(1)}, u32[]{:S(2)}, u32[]{:S(2)}) collective-permute-start(bf16[512,128]{1,0:T(8,128)(2,1)S(1)} %get-tuple-element.63), channel_id=1, source_target_pairs={{1,4},{5,8},{9,12},{13,0},{4,1},{8,5},{12,9},{0,13},{3,6},{7,10},{... | collective-permute-start | bytes 393224 | tf_op jit(solution)/shard_map/ppermute | solution.py:161
  35.2 2.9 %collective-permute-done.2.got_x = bf16[512,128]{1,0:T(8,128)(2,1)S(1)} collective-permute-done((bf16[512,128]{1,0:T(8,128)(2,1)S(1)}, bf16[512,128]{1,0:T(8,128)(2,1)S(1)}, u32[]{:S(2)}, u32[]{:S(2)}) %collective-permute-start.2) | collective-permute-done | bytes 131104 | tf_op jit(solution)/shard_map/ppermute | solution.py:161
  38.1 1.2 %shard_map.74 = (f32[1024,128]{1,0:T(8,128)S(1)}, bf16[1024,128]{1,0:T(8,128)(2,1)S(1)}, bf16[512,128]{1,0:T(8,128)(2,1)S(1)}, bf16[512,128]{1,0:T(8,128)(2,1)S(1)}) custom-call(s32[1]{0:T(128)} %bitcast.parity, bf16[512,128]{1,0:T(8,128)(2,1)S(1)} %collective-permute-done.2.got_x, bf16[512,128]{1,0:T(8,128)(2,1)S(1)} %collective-permute-done.3.got_i, ...), custom_call_target="tpu_custom_call" | custom-call | flops 268435456 | bytes 3407876 | tf_op jit(solution)/shard_map/pallas_call | solution.py:19
  39.3 2.6 %collective-permute-start.4 = (bf16[512,128]{1,0:T(8,128)(2,1)S(1)}, bf16[512,128]{1,0:T(8,128)(2,1)S(1)}, u32[]{:S(2)}, u32[]{:S(2)}) collective-permute-start(bf16[512,128]{1,0:T(8,128)(2,1)S(1)} %get-tuple-element.68), channel_id=1, source_target_pairs={{1,4},{5,8},{9,12},{13,0},{4,1},{8,5},{12,9},{0,13},{3,6},{7,10},{... | collective-permute-start | bytes 393224 | tf_op jit(solution)/shard_map/ppermute | solution.py:161
  42.6 3.0 %collective-permute-done.4.got_x = bf16[512,128]{1,0:T(8,128)(2,1)S(1)} collective-permute-done((bf16[512,128]{1,0:T(8,128)(2,1)S(1)}, bf16[512,128]{1,0:T(8,128)(2,1)S(1)}, u32[]{:S(2)}, u32[]{:S(2)}) %collective-permute-start.4) | collective-permute-done | bytes 131104 | tf_op jit(solution)/shard_map/ppermute | solution.py:161
  45.6 1.2 %shard_map.76 = (f32[1024,128]{1,0:T(8,128)S(1)}, bf16[1024,128]{1,0:T(8,128)(2,1)S(1)}, bf16[512,128]{1,0:T(8,128)(2,1)S(1)}, bf16[512,128]{1,0:T(8,128)(2,1)S(1)}) custom-call(s32[1]{0:T(128)} %bitcast.parity, bf16[512,128]{1,0:T(8,128)(2,1)S(1)} %collective-permute-done.4.got_x, bf16[512,128]{1,0:T(8,128)(2,1)S(1)} %collective-permute-done.5.got_i, ...), custom_call_target="tpu_custom_call" | custom-call | flops 268435456 | bytes 3407876 | tf_op jit(solution)/shard_map/pallas_call | solution.py:19
  46.8 2.7 %collective-permute-start.6 = (bf16[512,128]{1,0:T(8,128)(2,1)S(1)}, bf16[512,128]{1,0:T(8,128)(2,1)S(1)}, u32[]{:S(2)}, u32[]{:S(2)}) collective-permute-start(bf16[512,128]{1,0:T(8,128)(2,1)S(1)} %get-tuple-element.73), channel_id=1, source_target_pairs={{1,4},{5,8},{9,12},{13,0},{4,1},{8,5},{12,9},{0,13},{3,6},{7,10},{... | collective-permute-start | bytes 393224 | tf_op jit(solution)/shard_map/ppermute | solution.py:161
  50.2 2.9 %collective-permute-done.6.got_x = bf16[512,128]{1,0:T(8,128)(2,1)S(1)} collective-permute-done((bf16[512,128]{1,0:T(8,128)(2,1)S(1)}, bf16[512,128]{1,0:T(8,128)(2,1)S(1)}, u32[]{:S(2)}, u32[]{:S(2)}) %collective-permute-start.6) | collective-permute-done | bytes 131104 | tf_op jit(solution)/shard_map/ppermute | solution.py:161
  53.1 1.2 %shard_map.78 = (f32[1024,128]{1,0:T(8,128)S(1)}, bf16[1024,128]{1,0:T(8,128)(2,1)S(1)}, bf16[512,128]{1,0:T(8,128)(2,1)S(1)}, bf16[512,128]{1,0:T(8,128)(2,1)S(1)}) custom-call(s32[1]{0:T(128)} %bitcast.parity, bf16[512,128]{1,0:T(8,128)(2,1)S(1)} %collective-permute-done.6.got_x, bf16[512,128]{1,0:T(8,128)(2,1)S(1)} %collective-permute-done.7.got_i, ...), custom_call_target="tpu_custom_call" | custom-call | flops 268435456 | bytes 3407876 | tf_op jit(solution)/shard_map/pallas_call | solution.py:19
  54.3 2.8 %collective-permute-start.8 = (bf16[512,128]{1,0:T(8,128)(2,1)S(1)}, bf16[512,128]{1,0:T(8,128)(2,1)S(1)}, u32[]{:S(2)}, u32[]{:S(2)}) collective-permute-start(bf16[512,128]{1,0:T(8,128)(2,1)S(1)} %get-tuple-element.78), channel_id=1, source_target_pairs={{1,4},{5,8},{9,12},{13,0},{4,1},{8,5},{12,9},{0,13},{3,6},{7,10},{... | collective-permute-start | bytes 393224 | tf_op jit(solution)/shard_map/ppermute | solution.py:161
  57.8 2.8 %collective-permute-done.8.got_x = bf16[512,128]{1,0:T(8,128)(2,1)S(1)} collective-permute-done((bf16[512,128]{1,0:T(8,128)(2,1)S(1)}, bf16[512,128]{1,0:T(8,128)(2,1)S(1)}, u32[]{:S(2)}, u32[]{:S(2)}) %collective-permute-start.8) | collective-permute-done | bytes 131104 | tf_op jit(solution)/shard_map/ppermute | solution.py:161
  60.7 1.2 %shard_map.80 = (f32[1024,128]{1,0:T(8,128)S(1)}, bf16[1024,128]{1,0:T(8,128)(2,1)S(1)}, bf16[512,128]{1,0:T(8,128)(2,1)S(1)}, bf16[512,128]{1,0:T(8,128)(2,1)S(1)}) custom-call(s32[1]{0:T(128)} %bitcast.parity, bf16[512,128]{1,0:T(8,128)(2,1)S(1)} %collective-permute-done.8.got_x, bf16[512,128]{1,0:T(8,128)(2,1)S(1)} %collective-permute-done.9.got_i, ...), custom_call_target="tpu_custom_call" | custom-call | flops 268435456 | bytes 3407876 | tf_op jit(solution)/shard_map/pallas_call | solution.py:19
  61.9 2.8 %collective-permute-start.10 = (bf16[512,128]{1,0:T(8,128)(2,1)S(1)}, bf16[512,128]{1,0:T(8,128)(2,1)S(1)}, u32[]{:S(2)}, u32[]{:S(2)}) collective-permute-start(bf16[512,128]{1,0:T(8,128)(2,1)S(1)} %get-tuple-element.83), channel_id=1, source_target_pairs={{1,4},{5,8},{9,12},{13,0},{4,1},{8,5},{12,9},{0,13},{3,6},{7,10},{... | collective-permute-start | bytes 393224 | tf_op jit(solution)/shard_map/ppermute | solution.py:161
  65.5 2.8 %collective-permute-done.10.got_x = bf16[512,128]{1,0:T(8,128)(2,1)S(1)} collective-permute-done((bf16[512,128]{1,0:T(8,128)(2,1)S(1)}, bf16[512,128]{1,0:T(8,128)(2,1)S(1)}, u32[]{:S(2)}, u32[]{:S(2)}) %collective-permute-start.10) | collective-permute-done | bytes 131104 | tf_op jit(solution)/shard_map/ppermute | solution.py:161
  68.3 1.2 %shard_map.82 = (f32[1024,128]{1,0:T(8,128)S(1)}, bf16[1024,128]{1,0:T(8,128)(2,1)S(1)}, bf16[512,128]{1,0:T(8,128)(2,1)S(1)}, bf16[512,128]{1,0:T(8,128)(2,1)S(1)}) custom-call(s32[1]{0:T(128)} %bitcast.parity, bf16[512,128]{1,0:T(8,128)(2,1)S(1)} %collective-permute-done.10.got_x, bf16[512,128]{1,0:T(8,128)(2,1)S(1)} %collective-permute-done.11.got_i, ...), custom_call_target="tpu_custom_call" | custom-call | flops 268435456 | bytes 3407876 | tf_op jit(solution)/shard_map/pallas_call | solution.py:19
  69.5 2.8 %collective-permute-start.12 = (bf16[512,128]{1,0:T(8,128)(2,1)S(1)}, bf16[512,128]{1,0:T(8,128)(2,1)S(1)}, u32[]{:S(2)}, u32[]{:S(2)}) collective-permute-start(bf16[512,128]{1,0:T(8,128)(2,1)S(1)} %get-tuple-element.88), channel_id=1, source_target_pairs={{1,4},{5,8},{9,12},{13,0},{4,1},{8,5},{12,9},{0,13},{3,6},{7,10},{... | collective-permute-start | bytes 393224 | tf_op jit(solution)/shard_map/ppermute | solution.py:161
  73.0 2.9 %collective-permute-done.12.got_x = bf16[512,128]{1,0:T(8,128)(2,1)S(1)} collective-permute-done((bf16[512,128]{1,0:T(8,128)(2,1)S(1)}, bf16[512,128]{1,0:T(8,128)(2,1)S(1)}, u32[]{:S(2)}, u32[]{:S(2)}) %collective-permute-start.12) | collective-permute-done | bytes 131104 | tf_op jit(solution)/shard_map/ppermute | solution.py:161
  77.1 2.7 %collective-permute-start.14 = (bf16[512,128]{1,0:T(8,128)(2,1)S(1)}, bf16[512,128]{1,0:T(8,128)(2,1)S(1)}, u32[]{:S(2)}, u32[]{:S(2)}) collective-permute-start(bf16[512,128]{1,0:T(8,128)(2,1)S(1)} %get-tuple-element.93), channel_id=1, source_target_pairs={{1,4},{5,8},{9,12},{13,0},{4,1},{8,5},{12,9},{0,13},{3,6},{7,10},{... | collective-permute-start | bytes 393224 | tf_op jit(solution)/shard_map/ppermute | solution.py:161
  80.5 2.8 %collective-permute-done.14.got_x = bf16[512,128]{1,0:T(8,128)(2,1)S(1)} collective-permute-done((bf16[512,128]{1,0:T(8,128)(2,1)S(1)}, bf16[512,128]{1,0:T(8,128)(2,1)S(1)}, u32[]{:S(2)}, u32[]{:S(2)}) %collective-permute-start.14) | collective-permute-done | bytes 131104 | tf_op jit(solution)/shard_map/ppermute | solution.py:161
  83.3 1.3 %shard_map.86 = (f32[1024,128]{1,0:T(8,128)}, f32[1,128]{1,0:T(1,128)S(1)}) custom-call(s32[1]{0:T(128)} %bitcast.parity, bf16[512,128]{1,0:T(8,128)(2,1)S(1)} %collective-permute-done.14.got_x, bf16[512,128]{1,0:T(8,128)(2,1)S(1)} %collective-permute-done.15.got_i, f32[1024,128]{1,0:T(8,128)S(1)} %get-tuple-element.97.local, ...), custom_call_target="tpu_custom_call" | custom-call | flops 134217728 | bytes 2883588 | tf_op jit(solution)/shard_map/pallas_call | solution.py:19
  84.7 17.1 %psum.7 = f32[9,128]{1,0:T(8,128)} all-reduce(f32[9,128]{1,0:T(8,128)S(1)} %broadcast_multiply_fusion), channel_id=1, replica_groups=mesh['groups'=2,'dom'=4,'probe'=2,'orb'=2] {'dom','orb'}, use_global_device_ids=true, to_apply=%region_0.0 | all-reduce | flops 1152 | bytes 9216 | tf_op jit(solution)/shard_map/psum | solution.py:214
  (36 shorter events, 12.3 us)
Async XLA Ops:
  2.7 1.0 %copy-start = (f32[64,16,128]{2,1,0:T(8,128)S(1)}, f32[64,16,128]{2,1,0:T(8,128)}, u32[]{:S(2)}) copy-start(f32[64,16,128]{2,1,0:T(8,128)} %param.5) | copy-start | bytes 1572868
  3.9 1.1 %copy-start.1 = (bf16[1280,16,16]{0,2,1:T(8,128)(2,1)S(1)}, bf16[1280,16,16]{0,2,1:T(8,128)(2,1)}, u32[]{:S(2)}) copy-start(bf16[1280,16,16]{0,2,1:T(8,128)(2,1)} %param.6) | copy-start | bytes 1966084
  22.4 7.8 %collective-permute-start = (bf16[512,128]{1,0:T(8,128)(2,1)S(1)}, bf16[512,128]{1,0:T(8,128)(2,1)S(1)}, u32[]{:S(2)}, u32[]{:S(2)}) collective-permute-start(bf16[512,128]{1,0:T(8,128)(2,1)S(1)} %get-tuple-element.57), channel_id=1, source_target_pairs={{1,4},{5,8},{9,12},{13,0},{4,1},{8,5},{12,9},{0,13},{3,6},{7,10},{... | collective-permute-start | bytes 393224 | tf_op jit(solution)/shard_map/ppermute | solution.py:161
  27.0 3.3 %collective-permute-start.1 = (bf16[512,128]{1,0:T(8,128)(2,1)S(1)}, bf16[512,128]{1,0:T(8,128)(2,1)S(1)}, u32[]{:S(2)}, u32[]{:S(2)}) collective-permute-start(bf16[512,128]{1,0:T(8,128)(2,1)S(1)} %get-tuple-element.58), channel_id=1, source_target_pairs={{0,1},{1,0},{2,3},{3,2},{4,5},{5,4},{6,7},{7,6},{8,9},{9,8},{10,11... | collective-permute-start | bytes 393224 | tf_op jit(solution)/shard_map/ppermute | solution.py:161
  31.4 6.7 %collective-permute-start.2 = (bf16[512,128]{1,0:T(8,128)(2,1)S(1)}, bf16[512,128]{1,0:T(8,128)(2,1)S(1)}, u32[]{:S(2)}, u32[]{:S(2)}) collective-permute-start(bf16[512,128]{1,0:T(8,128)(2,1)S(1)} %get-tuple-element.63), channel_id=1, source_target_pairs={{1,4},{5,8},{9,12},{13,0},{4,1},{8,5},{12,9},{0,13},{3,6},{7,10},{... | collective-permute-start | bytes 393224 | tf_op jit(solution)/shard_map/ppermute | solution.py:161
  34.4 3.7 %collective-permute-start.3 = (bf16[512,128]{1,0:T(8,128)(2,1)S(1)}, bf16[512,128]{1,0:T(8,128)(2,1)S(1)}, u32[]{:S(2)}, u32[]{:S(2)}) collective-permute-start(bf16[512,128]{1,0:T(8,128)(2,1)S(1)} %get-tuple-element.64), channel_id=1, source_target_pairs={{0,1},{1,0},{2,3},{3,2},{4,5},{5,4},{6,7},{7,6},{8,9},{9,8},{10,11... | collective-permute-start | bytes 393224 | tf_op jit(solution)/shard_map/ppermute | solution.py:161
  39.3 6.3 %collective-permute-start.4 = (bf16[512,128]{1,0:T(8,128)(2,1)S(1)}, bf16[512,128]{1,0:T(8,128)(2,1)S(1)}, u32[]{:S(2)}, u32[]{:S(2)}) collective-permute-start(bf16[512,128]{1,0:T(8,128)(2,1)S(1)} %get-tuple-element.68), channel_id=1, source_target_pairs={{1,4},{5,8},{9,12},{13,0},{4,1},{8,5},{12,9},{0,13},{3,6},{7,10},{... | collective-permute-start | bytes 393224 | tf_op jit(solution)/shard_map/ppermute | solution.py:161
  41.9 3.7 %collective-permute-start.5 = (bf16[512,128]{1,0:T(8,128)(2,1)S(1)}, bf16[512,128]{1,0:T(8,128)(2,1)S(1)}, u32[]{:S(2)}, u32[]{:S(2)}) collective-permute-start(bf16[512,128]{1,0:T(8,128)(2,1)S(1)} %get-tuple-element.69), channel_id=1, source_target_pairs={{0,1},{1,0},{2,3},{3,2},{4,5},{5,4},{6,7},{7,6},{8,9},{9,8},{10,11... | collective-permute-start | bytes 393224 | tf_op jit(solution)/shard_map/ppermute | solution.py:161
  46.8 6.3 %collective-permute-start.6 = (bf16[512,128]{1,0:T(8,128)(2,1)S(1)}, bf16[512,128]{1,0:T(8,128)(2,1)S(1)}, u32[]{:S(2)}, u32[]{:S(2)}) collective-permute-start(bf16[512,128]{1,0:T(8,128)(2,1)S(1)} %get-tuple-element.73), channel_id=1, source_target_pairs={{1,4},{5,8},{9,12},{13,0},{4,1},{8,5},{12,9},{0,13},{3,6},{7,10},{... | collective-permute-start | bytes 393224 | tf_op jit(solution)/shard_map/ppermute | solution.py:161
  49.5 3.6 %collective-permute-start.7 = (bf16[512,128]{1,0:T(8,128)(2,1)S(1)}, bf16[512,128]{1,0:T(8,128)(2,1)S(1)}, u32[]{:S(2)}, u32[]{:S(2)}) collective-permute-start(bf16[512,128]{1,0:T(8,128)(2,1)S(1)} %get-tuple-element.74), channel_id=1, source_target_pairs={{0,1},{1,0},{2,3},{3,2},{4,5},{5,4},{6,7},{7,6},{8,9},{9,8},{10,11... | collective-permute-start | bytes 393224 | tf_op jit(solution)/shard_map/ppermute | solution.py:161
  54.3 6.4 %collective-permute-start.8 = (bf16[512,128]{1,0:T(8,128)(2,1)S(1)}, bf16[512,128]{1,0:T(8,128)(2,1)S(1)}, u32[]{:S(2)}, u32[]{:S(2)}) collective-permute-start(bf16[512,128]{1,0:T(8,128)(2,1)S(1)} %get-tuple-element.78), channel_id=1, source_target_pairs={{1,4},{5,8},{9,12},{13,0},{4,1},{8,5},{12,9},{0,13},{3,6},{7,10},{... | collective-permute-start | bytes 393224 | tf_op jit(solution)/shard_map/ppermute | solution.py:161
  57.1 3.6 %collective-permute-start.9 = (bf16[512,128]{1,0:T(8,128)(2,1)S(1)}, bf16[512,128]{1,0:T(8,128)(2,1)S(1)}, u32[]{:S(2)}, u32[]{:S(2)}) collective-permute-start(bf16[512,128]{1,0:T(8,128)(2,1)S(1)} %get-tuple-element.79), channel_id=1, source_target_pairs={{0,1},{1,0},{2,3},{3,2},{4,5},{5,4},{6,7},{7,6},{8,9},{9,8},{10,11... | collective-permute-start | bytes 393224 | tf_op jit(solution)/shard_map/ppermute | solution.py:161
  61.9 6.4 %collective-permute-start.10 = (bf16[512,128]{1,0:T(8,128)(2,1)S(1)}, bf16[512,128]{1,0:T(8,128)(2,1)S(1)}, u32[]{:S(2)}, u32[]{:S(2)}) collective-permute-start(bf16[512,128]{1,0:T(8,128)(2,1)S(1)} %get-tuple-element.83), channel_id=1, source_target_pairs={{1,4},{5,8},{9,12},{13,0},{4,1},{8,5},{12,9},{0,13},{3,6},{7,10},{... | collective-permute-start | bytes 393224 | tf_op jit(solution)/shard_map/ppermute | solution.py:161
  64.7 3.5 %collective-permute-start.11 = (bf16[512,128]{1,0:T(8,128)(2,1)S(1)}, bf16[512,128]{1,0:T(8,128)(2,1)S(1)}, u32[]{:S(2)}, u32[]{:S(2)}) collective-permute-start(bf16[512,128]{1,0:T(8,128)(2,1)S(1)} %get-tuple-element.84), channel_id=1, source_target_pairs={{0,1},{1,0},{2,3},{3,2},{4,5},{5,4},{6,7},{7,6},{8,9},{9,8},{10,11... | collective-permute-start | bytes 393224 | tf_op jit(solution)/shard_map/ppermute | solution.py:161
  69.5 6.4 %collective-permute-start.12 = (bf16[512,128]{1,0:T(8,128)(2,1)S(1)}, bf16[512,128]{1,0:T(8,128)(2,1)S(1)}, u32[]{:S(2)}, u32[]{:S(2)}) collective-permute-start(bf16[512,128]{1,0:T(8,128)(2,1)S(1)} %get-tuple-element.88), channel_id=1, source_target_pairs={{1,4},{5,8},{9,12},{13,0},{4,1},{8,5},{12,9},{0,13},{3,6},{7,10},{... | collective-permute-start | bytes 393224 | tf_op jit(solution)/shard_map/ppermute | solution.py:161
  72.3 3.6 %collective-permute-start.13 = (bf16[512,128]{1,0:T(8,128)(2,1)S(1)}, bf16[512,128]{1,0:T(8,128)(2,1)S(1)}, u32[]{:S(2)}, u32[]{:S(2)}) collective-permute-start(bf16[512,128]{1,0:T(8,128)(2,1)S(1)} %get-tuple-element.89), channel_id=1, source_target_pairs={{0,1},{1,0},{2,3},{3,2},{4,5},{5,4},{6,7},{7,6},{8,9},{9,8},{10,11... | collective-permute-start | bytes 393224 | tf_op jit(solution)/shard_map/ppermute | solution.py:161
  77.1 6.3 %collective-permute-start.14 = (bf16[512,128]{1,0:T(8,128)(2,1)S(1)}, bf16[512,128]{1,0:T(8,128)(2,1)S(1)}, u32[]{:S(2)}, u32[]{:S(2)}) collective-permute-start(bf16[512,128]{1,0:T(8,128)(2,1)S(1)} %get-tuple-element.93), channel_id=1, source_target_pairs={{1,4},{5,8},{9,12},{13,0},{4,1},{8,5},{12,9},{0,13},{3,6},{7,10},{... | collective-permute-start | bytes 393224 | tf_op jit(solution)/shard_map/ppermute | solution.py:161
  79.8 3.6 %collective-permute-start.15 = (bf16[512,128]{1,0:T(8,128)(2,1)S(1)}, bf16[512,128]{1,0:T(8,128)(2,1)S(1)}, u32[]{:S(2)}, u32[]{:S(2)}) collective-permute-start(bf16[512,128]{1,0:T(8,128)(2,1)S(1)} %get-tuple-element.94), channel_id=1, source_target_pairs={{0,1},{1,0},{2,3},{3,2},{4,5},{5,4},{6,7},{7,6},{8,9},{9,8},{10,11... | collective-permute-start | bytes 393224 | tf_op jit(solution)/shard_map/ppermute | solution.py:161

commit v2 on v1

v2 whole, which is shorter than its diff:
```python
import functools

import jax
import jax.numpy as jnp
from jax import lax
from jax.experimental import pallas as pl
from jax.experimental.pallas import tpu as pltpu
from jax.sharding import PartitionSpec as P

STEPS = 8
RING = ("dom", "orb")
F32, BF16 = jnp.float32, jnp.bfloat16
VMEM = pl.BlockSpec(memory_space=pltpu.VMEM)
SMEM = pl.BlockSpec(memory_space=pltpu.SMEM)
NT = (((1,), (1,)), ((), ()))
UNROLL = 8
PAD = 8
HALF = STEPS // 2
DOTS = [
    [(0, n)] + [(m, n) for m in (n - 1, n) if m > 0 and HALF < m + n] for n in range(HALF + 1)
]


def operands_of(k):
    return sorted({m for pair in DOTS[k] for m in pair})


def call(body, outs, flops, *operands, scratch=(), smem=0, limit=16):
    size = sum(o.size * o.dtype.itemsize for o in operands)
    return pl.pallas_call(
        body,
        out_shape=tuple(jax.ShapeDtypeStruct(s, t) for s, t in outs),
        in_specs=[SMEM] * smem + [VMEM] * (len(operands) - smem),
        out_specs=(VMEM,) * len(outs),
        scratch_shapes=scratch,
        compiler_params=pltpu.CompilerParams(vmem_limit_bytes=limit << 20),
        cost_estimate=pl.CostEstimate(flops=flops, bytes_accessed=size, transcendentals=0),
    )(*operands)


def build_body(atoms, orbits, halo, pair, blocks, own_ref, cross_ref, crosst_ref, own_f32, cross_f32, row_hot):
    slots = blocks.shape[1]
    pair_id = pair[...].reshape(1, slots)
    col_id = lax.div(pair_id, atoms)
    row_id = pair_id - col_id * atoms
    row_hot[...] = jnp.where(lax.broadcasted_iota(jnp.int32, (atoms, slots), 0) == row_id, 1.0, 0.0).astype(BF16)
    lanes = 2 * atoms
    lane = lax.broadcasted_iota(jnp.int32, (orbits, lanes), 1)

    def place(first, total, target):
        def one(q, _):
            hot = []
            for n in range(4):
                here = jnp.where(col_id == first + 4 * q + n, 1.0, 0.0).astype(BF16)
                hot.append(row_hot[...] * here)
            hot = jnp.concatenate(hot, axis=0)
            tile = lax.dot_general(blocks[...], hot, NT, preferred_element_type=F32)
            for two in range(2):
                for i in range(0, orbits, 2):
                    at = slice(two * lanes, (two + 1) * lanes)
                    left = tile[i * orbits : (i + 1) * orbits, at]
                    right = tile[(i + 1) * orbits : (i + 2) * orbits, at]
                    low = jnp.where(lane < atoms, left, pltpu.roll(right, atoms, 1))
                    high = jnp.where(lane < atoms, pltpu.roll(left, atoms, 1), right)
                    col = 4 * q + 2 * two
                    target[i // 2, pl.ds(col, orbits, stride=total + PAD), :] = low
                    target[i // 2, pl.ds(col + 1, orbits, stride=total + PAD), :] = high
            return 0

        lax.fori_loop(0, total // 4, one, 0, unroll=UNROLL)

    place(0, atoms, own_f32)
    place(atoms, halo, cross_f32)

    def rows(source, piece, total):
        apart = [source[piece, j * (total + PAD) : j * (total + PAD) + total, :] for j in range(orbits)]
        return jnp.concatenate(apart, axis=0)

    for p in range(orbits // 2):
        at = slice(p * lanes, (p + 1) * lanes)
        mine = rows(cross_f32, p, halo)
        crosst_ref[:, at] = mine.astype(BF16)
        cross_ref[at, :] = mine.T.astype(BF16)
        turned = rows(own_f32, p, atoms).T
        for n in range(orbits // 2):
            here = slice(n * lanes, (n + 1) * lanes)
            starts = [(2 * p + m) * (atoms + PAD) for m in range(2)]
            other = jnp.concatenate([own_f32[n, start : start + atoms, :] for start in starts], axis=0)
            own_ref[at, here] = (other + turned[:, here]).astype(BF16)


def put_sends(atoms, orbits, halo, even, w, products, out_x, out_i):
    for o in range(orbits):
        edge = w[o * atoms : o * atoms + halo, :]
        product = products[o * halo : (o + 1) * halo, :]
        out_x[o * halo : (o + 1) * halo, :] = jnp.where(even, edge, product)
        out_i[o * halo : (o + 1) * halo, :] = jnp.where(even, product, edge)


def first_body(atoms, orbits, halo, turn, parity, probes, crosst, v_ref, w_ref, out_x, out_i):
    for o in range(orbits):
        rows = slice(o * atoms, (o + 1) * atoms)
        v = probes[pl.ds(o, atoms, stride=orbits), :] if turn else probes[rows, :]
        v_ref[rows, :] = v
        w_ref[rows, :] = v.astype(BF16)
    products = jnp.dot(crosst[...], w_ref[...], preferred_element_type=F32).astype(BF16)
    put_sends(atoms, orbits, halo, parity[0] == 0, w_ref, products, out_x, out_i)


def own_body(k, scale, own, w, *refs):
    local_ref, table_ref = refs[-2:]
    local_ref[...] = jnp.dot(own[...], w[...], preferred_element_type=F32)
    if k > HALF:
        table_ref[...] = refs[0][...] + refs[1][...]
        return
    vectors = dict(zip(operands_of(k), refs))
    made = [jnp.sum(vectors[m][...] * vectors[n][...], axis=0, keepdims=True) for m, n in DOTS[k]]
    if k < HALF:
        table_ref[...] = jnp.concatenate(made, axis=0)
        return
    dots = dict(zip(DOTS[k], made))
    for table, pairs in zip(refs[len(vectors) : -2], DOTS):
        dots.update({pair: table[n : n + 1, :] for n, pair in enumerate(pairs)})
    rows = []
    for n in range(STEPS + 1):
        if n <= HALF:
            rows.append(dots[0, n])
        else:
            rows.append(2.0 * dots[n // 2, n - n // 2] - dots[0, n % 2])
    table_ref[...] = jnp.concatenate(rows, axis=0) * scale


def next_vector(atoms, orbits, halo, first, even, got_x, got_i, local, previous, cross, write):
    edge = jnp.where(even, got_i[...], got_x[...])
    total = local[...] + jnp.dot(cross[...], edge, preferred_element_type=F32)
    for o in range(orbits):
        part = total[o * atoms : (o + 1) * atoms, :]
        back = jnp.where(even, got_x[o * halo : (o + 1) * halo, :], got_i[o * halo : (o + 1) * halo, :])
        for at, piece in ((0, part[:halo] + back.astype(F32)), (halo, part[halo:])):
            rows = slice(o * atoms + at, o * atoms + at + piece.shape[0])
            write(o, at, piece if first else 2.0 * piece - previous[rows, :])


def step_body(
    atoms, orbits, halo, first, parity, got_x, got_i, local, previous, cross, crosst, v_ref, w_ref, out_x, out_i
):
    even = parity[0] == 0

    def write(o, at, piece):
        rows = slice(o * atoms + at, o * atoms + at + piece.shape[0])
        v_ref[rows, :] = piece
        w_ref[rows, :] = piece.astype(BF16)

    next_vector(atoms, orbits, halo, first, even, got_x, got_i, local, previous, cross, write)
    products = jnp.dot(crosst[...], w_ref[...], preferred_element_type=F32).astype(BF16)
    put_sends(atoms, orbits, halo, even, w_ref, products, out_x, out_i)


def last_body(atoms, orbits, halo, turn, parity, got_x, got_i, local, previous, cross, out_ref):
    def write(o, at, piece):
        rows = slice(o * atoms + at, o * atoms + at + piece.shape[0])
        out_ref[pl.ds(at * orbits + o, piece.shape[0], stride=orbits) if turn else rows, :] = piece

    next_vector(atoms, orbits, halo, False, parity[0] == 0, got_x, got_i, local, previous, cross, write)


def sum_rounds():
    doms = lax.axis_size("dom")
    swap = lambda axis, bit: lambda x: lax.ppermute(x, axis, [(i, i ^ bit) for i in range(lax.axis_size(axis))])
    if doms & (doms - 1):
        return [lambda x: lax.psum(x, RING) - x]
    return [swap("orb", 1)] + [swap("dom", 1 << n) for n in range(doms.bit_length() - 1)]


def per_device(probes, blocks, block_rows, block_cols, counts):
    atoms, orbits, width = probes.shape
    halo = atoms // 2
    size, edge_size = atoms * orbits, halo * orbits
    slots = blocks.shape[0]
    dims = (atoms, orbits, halo)
    turn = width == 128
    ring = lax.axis_size(RING)
    scale = 1.0 / (size * ring)
    parity = lax.axis_index("orb").astype(jnp.int32).reshape(1)
    between = [(i, (i + 1) % ring) for i in range(1, ring, 2)]
    between = between + [(b, a) for a, b in between]
    inside = [(0, 1), (1, 0)]

    def exchange(send_x, send_i):
        return lax.ppermute(send_x, RING, between), lax.ppermute(send_i, "orb", inside)

    slot = jnp.arange(slots, dtype=jnp.int32)
    pair = jnp.where(slot < counts[0], block_cols * atoms + block_rows, -atoms)
    own, cross, crosst = call(
        functools.partial(build_body, *dims),
        (((size, size), BF16), ((size, edge_size), BF16), ((edge_size, size), BF16)),
        2 * orbits * orbits * slots * atoms * (atoms + halo),
        pair,
        blocks.transpose(1, 2, 0).reshape(orbits * orbits, slots),
        scratch=[
            pltpu.VMEM((orbits // 2, orbits * (atoms + PAD), 2 * atoms), F32),
            pltpu.VMEM((orbits // 2, orbits * (halo + PAD), 2 * atoms), F32),
            pltpu.VMEM((atoms, slots), BF16),
        ],
        limit=32,
    )
    vector = (((size, width), F32), ((size, width), BF16))
    sends = (((edge_size, width), BF16),) * 2
    cross_flops = 2 * size * edge_size * width
    v, w, send_x, send_i = call(
        functools.partial(first_body, *dims, turn),
        vector + sends,
        cross_flops,
        parity,
        (probes if turn else probes.transpose(1, 0, 2)).reshape(size, width),
        crosst,
        smem=1,
    )
    vectors, tables, rounds = [v], [], sum_rounds()
    table = None
    for k in range(STEPS):
        got_x, got_i = exchange(send_x, send_i)
        if k <= HALF:
            extra = [vectors[m] for m in operands_of(k)] + (tables if k == HALF else [])
        else:
            extra = [table, rounds.pop(0)(table) if rounds else jnp.zeros_like(table)]
        height = len(DOTS[k]) if k < HALF else STEPS + 1
        local, table = call(
            functools.partial(own_body, k, scale),
            (((size, width), F32), ((height, width), F32)),
            2 * size * size * width,
            own, w, *extra,
        )
        tables.append(table)
        operands = (parity, got_x, got_i, local, vectors[max(k - 1, 0)], cross)
        if k < STEPS - 1:
            v, w, send_x, send_i = call(
                functools.partial(step_body, *dims, k == 0), vector + sends, 2 * cross_flops, *operands, crosst, smem=1
            )
            vectors.append(v)
        else:
            (last,) = call(functools.partial(last_body, *dims, turn), vector[:1], cross_flops, *operands, smem=1)
    for one in rounds:
        table = table + one(table)
    last = last.reshape(atoms, orbits, width) if turn else last.reshape(orbits, atoms, width).transpose(1, 0, 2)
    return last, table


def solution(mesh):
    in_specs = (
        P(("groups", "dom", "orb"), None, "probe"),
        P(("groups", "dom", "orb"), None, None),
        P(("groups", "dom", "orb")),
        P(("groups", "dom", "orb")),
        P(("groups", "dom", "orb")),
    )
    out_specs = (P(("groups", "dom", "orb"), None, "probe"), P("groups", "probe"))
    return jax.shard_map(
        per_device, mesh=mesh, in_specs=in_specs, out_specs=out_specs, check_vma=False
    )
```

time: 102 us -> 75.2 us (0.74)
  blocking collectives: 17.1 us -> 0 us
  Pallas kernels: 33 us -> 23.2 us
  local copies, waits for them, and re-layouts: 3.56 us -> 1.09 us
  waiting for transfers between devices: 22.7 us -> 24.7 us
    psum x1 -> x0, blocking collectives: 17.1 us -> none  [per_device(): table = lax.psum(jnp.concatenate(moments, axis=0) * scale, RING)]
    pallas_call x19 -> x18, Pallas kernels: 33 us -> 23.2 us  [call(): pl.pallas_call(body, out_shape=tuple((jax.ShapeDtypeStruct(s, t) for s, t...]
    ppermute x0 -> x3, waiting for transfers between devices: none -> 9.27 us  [sum_rounds(): lax.ppermute(x, axis, [(i, i ^ bit) for i in range(lax.axis_size(axis))])]
    ppermute x8, waiting for transfers between devices: 22.7 us -> 15.4 us  [exchange(): lax.ppermute(send_x, RING, between)]
    reshape x2 -> x0, local copies, waits for them, and re-layouts: 1.4 us -> none  [the longest x1 0.7 us: per_device(): block_rows.reshape(1, slots)]
    unnamed x4, local copies, waits for them, and re-layouts: 2.12 us -> 1.09 us
  transfers between devices with their start and end apart: 16 -> 19, of which waited for: 8 -> 9; matrix products, arithmetic and copies ran while one was open for 0% -> 0% of each run, Pallas kernels for 6% -> 8%
where the time goes in v2:
time: 75.2 us; the launch traced here: 74.9 us
  waiting for transfers between devices  24.7 us (33%)
  starting transfers between devices  23.7 us (32%)
  Pallas kernels  23.2 us (31%)
  between operations  1.43 us (2%)
  local copies, waits for them, and re-layouts  1.09 us (1%)
    pallas_call x18, Pallas kernels, call(): pl.pallas_call(body, out_shape=tuple((jax.ShapeDtypeStruct(s, t) for s, t...  23.2 us
    ppermute x8, starting transfers between devices, exchange(): lax.ppermute(send_x, RING, between)  23.1 us
    ppermute x8, waiting for transfers between devices, exchange(): lax.ppermute(send_x, RING, between)  15.4 us
    ppermute x3, waiting for transfers between devices, sum_rounds(): lax.ppermute(x, axis, [(i, i ^ bit) for i in range(lax.axis_size(axis))])  9.27 us
  transfers between devices with their start and end apart: 19, of which 9 were waited for; matrix products, arithmetic and copies ran while one was open for 0% of the time, Pallas kernels for 8%

profile of v2, /device:TPU:0, one launch (start us, length us, event | category | flops | bytes accessed | tf_op | source)
XLA Modules:
  0.0 74.9 jit_solution(4091357726082101888)
XLA Ops:
  3.1 6.2 %shard_map.68 = (bf16[1024,1024]{1,0:T(8,128)(2,1)S(1)}, bf16[1024,512]{1,0:T(8,128)(2,1)S(1)}, bf16[512,1024]{1,0:T(8,128)(2,1)S(1)}) custom-call(s32[1280]{0:T(1024)S(1)} %add_select_fusion.pair, bf16[256,1280]{1,0:T(8,128)(2,1)S(1)} %bitcast.9), custom_call_target="tpu_custom_call" | custom-call | flops 4026531840 | bytes 660480 | tf_op jit(solution)/shard_map/pallas_call | solution.py:30
  9.9 4.6 %collective-permute-start = (bf16[512,128]{1,0:T(8,128)(2,1)S(1)}, bf16[512,128]{1,0:T(8,128)(2,1)S(1)}, u32[]{:S(2)}, u32[]{:S(2)}) collective-permute-start(bf16[512,128]{1,0:T(8,128)(2,1)S(1)} %get-tuple-element.53), channel_id=1, source_target_pairs={{1,4},{5,8},{9,12},{13,0},{4,1},{8,5},{12,9},{0,13},{3,6},{7,10},{... | collective-permute-start | bytes 393224 | tf_op jit(solution)/shard_map/ppermute | solution.py:190
  15.2 2.5 %collective-permute-done.got_x = bf16[512,128]{1,0:T(8,128)(2,1)S(1)} collective-permute-done((bf16[512,128]{1,0:T(8,128)(2,1)S(1)}, bf16[512,128]{1,0:T(8,128)(2,1)S(1)}, u32[]{:S(2)}, u32[]{:S(2)}) %collective-permute-start) | collective-permute-done | bytes 131104 | tf_op jit(solution)/shard_map/ppermute | solution.py:190
  18.9 3.0 %collective-permute-start.2 = (bf16[512,128]{1,0:T(8,128)(2,1)S(1)}, bf16[512,128]{1,0:T(8,128)(2,1)S(1)}, u32[]{:S(2)}, u32[]{:S(2)}) collective-permute-start(bf16[512,128]{1,0:T(8,128)(2,1)S(1)} %get-tuple-element.60), channel_id=1, source_target_pairs={{1,4},{5,8},{9,12},{13,0},{4,1},{8,5},{12,9},{0,13},{3,6},{7,10},{... | collective-permute-start | bytes 393224 | tf_op jit(solution)/shard_map/ppermute | solution.py:190
  22.7 2.9 %collective-permute-done.2.got_x = bf16[512,128]{1,0:T(8,128)(2,1)S(1)} collective-permute-done((bf16[512,128]{1,0:T(8,128)(2,1)S(1)}, bf16[512,128]{1,0:T(8,128)(2,1)S(1)}, u32[]{:S(2)}, u32[]{:S(2)}) %collective-permute-start.2) | collective-permute-done | bytes 131104 | tf_op jit(solution)/shard_map/ppermute | solution.py:190
  25.6 1.2 %shard_map.73 = (f32[1024,128]{1,0:T(8,128)S(1)}, bf16[1024,128]{1,0:T(8,128)(2,1)S(1)}, bf16[512,128]{1,0:T(8,128)(2,1)S(1)}, bf16[512,128]{1,0:T(8,128)(2,1)S(1)}) custom-call(s32[1]{0:T(128)} %bitcast.parity, bf16[512,128]{1,0:T(8,128)(2,1)S(1)} %collective-permute-done.2.got_x, bf16[512,128]{1,0:T(8,128)(2,1)S(1)} %collective-permute-done.3.got_i, ...), custom_call_target="tpu_custom_call" | custom-call | flops 268435456 | bytes 3407876 | tf_op jit(solution)/shard_map/pallas_call | solution.py:30
  26.8 2.6 %collective-permute-start.4 = (bf16[512,128]{1,0:T(8,128)(2,1)S(1)}, bf16[512,128]{1,0:T(8,128)(2,1)S(1)}, u32[]{:S(2)}, u32[]{:S(2)}) collective-permute-start(bf16[512,128]{1,0:T(8,128)(2,1)S(1)} %get-tuple-element.65), channel_id=1, source_target_pairs={{1,4},{5,8},{9,12},{13,0},{4,1},{8,5},{12,9},{0,13},{3,6},{7,10},{... | collective-permute-start | bytes 393224 | tf_op jit(solution)/shard_map/ppermute | solution.py:190
  30.2 2.9 %collective-permute-done.4.got_x = bf16[512,128]{1,0:T(8,128)(2,1)S(1)} collective-permute-done((bf16[512,128]{1,0:T(8,128)(2,1)S(1)}, bf16[512,128]{1,0:T(8,128)(2,1)S(1)}, u32[]{:S(2)}, u32[]{:S(2)}) %collective-permute-start.4) | collective-permute-done | bytes 131104 | tf_op jit(solution)/shard_map/ppermute | solution.py:190
  33.1 1.2 %shard_map.75 = (f32[1024,128]{1,0:T(8,128)S(1)}, bf16[1024,128]{1,0:T(8,128)(2,1)S(1)}, bf16[512,128]{1,0:T(8,128)(2,1)S(1)}, bf16[512,128]{1,0:T(8,128)(2,1)S(1)}) custom-call(s32[1]{0:T(128)} %bitcast.parity, bf16[512,128]{1,0:T(8,128)(2,1)S(1)} %collective-permute-done.4.got_x, bf16[512,128]{1,0:T(8,128)(2,1)S(1)} %collective-permute-done.5.got_i, ...), custom_call_target="tpu_custom_call" | custom-call | flops 268435456 | bytes 3407876 | tf_op jit(solution)/shard_map/pallas_call | solution.py:30
  34.3 2.7 %collective-permute-start.6 = (bf16[512,128]{1,0:T(8,128)(2,1)S(1)}, bf16[512,128]{1,0:T(8,128)(2,1)S(1)}, u32[]{:S(2)}, u32[]{:S(2)}) collective-permute-start(bf16[512,128]{1,0:T(8,128)(2,1)S(1)} %get-tuple-element.70), channel_id=1, source_target_pairs={{1,4},{5,8},{9,12},{13,0},{4,1},{8,5},{12,9},{0,13},{3,6},{7,10},{... | collective-permute-start | bytes 393224 | tf_op jit(solution)/shard_map/ppermute | solution.py:190
  37.8 2.8 %collective-permute-done.6.got_x = bf16[512,128]{1,0:T(8,128)(2,1)S(1)} collective-permute-done((bf16[512,128]{1,0:T(8,128)(2,1)S(1)}, bf16[512,128]{1,0:T(8,128)(2,1)S(1)}, u32[]{:S(2)}, u32[]{:S(2)}) %collective-permute-start.6) | collective-permute-done | bytes 131104 | tf_op jit(solution)/shard_map/ppermute | solution.py:190
  40.6 1.2 %shard_map.77 = (f32[1024,128]{1,0:T(8,128)S(1)}, bf16[1024,128]{1,0:T(8,128)(2,1)S(1)}, bf16[512,128]{1,0:T(8,128)(2,1)S(1)}, bf16[512,128]{1,0:T(8,128)(2,1)S(1)}) custom-call(s32[1]{0:T(128)} %bitcast.parity, bf16[512,128]{1,0:T(8,128)(2,1)S(1)} %collective-permute-done.6.got_x, bf16[512,128]{1,0:T(8,128)(2,1)S(1)} %collective-permute-done.7.got_i, ...), custom_call_target="tpu_custom_call" | custom-call | flops 268435456 | bytes 3407876 | tf_op jit(solution)/shard_map/pallas_call | solution.py:30
  41.9 2.8 %collective-permute-start.8 = (bf16[512,128]{1,0:T(8,128)(2,1)S(1)}, bf16[512,128]{1,0:T(8,128)(2,1)S(1)}, u32[]{:S(2)}, u32[]{:S(2)}) collective-permute-start(bf16[512,128]{1,0:T(8,128)(2,1)S(1)} %get-tuple-element.75), channel_id=1, source_target_pairs={{1,4},{5,8},{9,12},{13,0},{4,1},{8,5},{12,9},{0,13},{3,6},{7,10},{... | collective-permute-start | bytes 393224 | tf_op jit(solution)/shard_map/ppermute | solution.py:190
  45.4 2.8 %collective-permute-done.8.got_x = bf16[512,128]{1,0:T(8,128)(2,1)S(1)} collective-permute-done((bf16[512,128]{1,0:T(8,128)(2,1)S(1)}, bf16[512,128]{1,0:T(8,128)(2,1)S(1)}, u32[]{:S(2)}, u32[]{:S(2)}) %collective-permute-start.8) | collective-permute-done | bytes 131104 | tf_op jit(solution)/shard_map/ppermute | solution.py:190
  48.2 1.2 %shard_map.79 = (f32[1024,128]{1,0:T(8,128)S(1)}, bf16[1024,128]{1,0:T(8,128)(2,1)S(1)}, bf16[512,128]{1,0:T(8,128)(2,1)S(1)}, bf16[512,128]{1,0:T(8,128)(2,1)S(1)}) custom-call(s32[1]{0:T(128)} %bitcast.parity, bf16[512,128]{1,0:T(8,128)(2,1)S(1)} %collective-permute-done.8.got_x, bf16[512,128]{1,0:T(8,128)(2,1)S(1)} %collective-permute-done.9.got_i, ...), custom_call_target="tpu_custom_call" | custom-call | flops 268435456 | bytes 3407876 | tf_op jit(solution)/shard_map/pallas_call | solution.py:30
  49.5 2.8 %collective-permute-start.10 = (bf16[512,128]{1,0:T(8,128)(2,1)S(1)}, bf16[512,128]{1,0:T(8,128)(2,1)S(1)}, u32[]{:S(2)}, u32[]{:S(2)}) collective-permute-start(bf16[512,128]{1,0:T(8,128)(2,1)S(1)} %get-tuple-element.84), channel_id=1, source_target_pairs={{1,4},{5,8},{9,12},{13,0},{4,1},{8,5},{12,9},{0,13},{3,6},{7,10},{... | collective-permute-start | bytes 393224 | tf_op jit(solution)/shard_map/ppermute | solution.py:190
  54.4 1.4 %collective-permute-done.10.got_x = bf16[512,128]{1,0:T(8,128)(2,1)S(1)} collective-permute-done((bf16[512,128]{1,0:T(8,128)(2,1)S(1)}, bf16[512,128]{1,0:T(8,128)(2,1)S(1)}, u32[]{:S(2)}, u32[]{:S(2)}) %collective-permute-start.10) | collective-permute-done | bytes 131104 | tf_op jit(solution)/shard_map/ppermute | solution.py:190
  57.0 2.8 %collective-permute-start.13 = (bf16[512,128]{1,0:T(8,128)(2,1)S(1)}, bf16[512,128]{1,0:T(8,128)(2,1)S(1)}, u32[]{:S(2)}, u32[]{:S(2)}) collective-permute-start(bf16[512,128]{1,0:T(8,128)(2,1)S(1)} %get-tuple-element.89), channel_id=1, source_target_pairs={{1,4},{5,8},{9,12},{13,0},{4,1},{8,5},{12,9},{0,13},{3,6},{7,10},{... | collective-permute-start | bytes 393224 | tf_op jit(solution)/shard_map/ppermute | solution.py:190
  59.8 3.7 %collective-permute-done.15.refs_1_ = f32[9,128]{1,0:T(8,128)S(1)} collective-permute-done((f32[9,128]{1,0:T(8,128)S(1)}, f32[9,128]{1,0:T(8,128)S(1)}, u32[]{:S(2)}, u32[]{:S(2)}) %collective-permute-start.15) | collective-permute-done | bytes 4640 | tf_op jit(solution)/shard_map/ppermute | solution.py:169
  64.2 1.6 %shard_map.83 = (f32[1024,128]{1,0:T(8,128)}, bf16[1024,128]{1,0:T(8,128)(2,1)S(1)}, bf16[512,128]{1,0:T(8,128)(2,1)S(1)}, bf16[512,128]{1,0:T(8,128)(2,1)S(1)}) custom-call(s32[1]{0:T(128)} %bitcast.parity, bf16[512,128]{1,0:T(8,128)(2,1)S(1)} %collective-permute-done.13.got_x, bf16[512,128]{1,0:T(8,128)(2,1)S(1)} %collective-permute-done.14.got_i, ...), custom_call_target="tpu_custom_call" | custom-call | flops 268435456 | bytes 3407876 | tf_op jit(solution)/shard_map/pallas_call | solution.py:30
  65.8 1.8 %collective-permute-start.16 = (bf16[512,128]{1,0:T(8,128)(2,1)S(1)}, bf16[512,128]{1,0:T(8,128)(2,1)S(1)}, u32[]{:S(2)}, u32[]{:S(2)}) collective-permute-start(bf16[512,128]{1,0:T(8,128)(2,1)S(1)} %get-tuple-element.95), channel_id=1, source_target_pairs={{1,4},{5,8},{9,12},{13,0},{4,1},{8,5},{12,9},{0,13},{3,6},{7,10},{... | collective-permute-start | bytes 393224 | tf_op jit(solution)/shard_map/ppermute | solution.py:190
  67.6 4.7 %collective-permute-done.18.refs_1_ = f32[9,128]{1,0:T(8,128)S(1)} collective-permute-done((f32[9,128]{1,0:T(8,128)S(1)}, f32[9,128]{1,0:T(8,128)S(1)}, u32[]{:S(2)}, u32[]{:S(2)}) %collective-permute-start.18) | collective-permute-done | bytes 4640 | tf_op jit(solution)/shard_map/ppermute | solution.py:169
  72.3 1.2 %shard_map.84 = (f32[1024,128]{1,0:T(8,128)S(1)}, f32[9,128]{1,0:T(8,128)}) custom-call(bf16[1024,1024]{1,0:T(8,128)(2,1)S(1)} %get-tuple-element.55.own, bf16[1024,128]{1,0:T(8,128)(2,1)S(1)} %get-tuple-element.97.w, f32[9,128]{1,0:T(8,128)S(1)} %get-tuple-element.98.refs_0_, f32[9,128]{1,0:T(8,128)S(1)} %collective-permute-done.18.refs_1_), custom_call_target="tpu_custom_call" | custom-call | flops 268435456 | bytes 2368512 | tf_op jit(solution)/shard_map/pallas_call | solution.py:30
  73.5 1.3 %shard_map.85 = f32[1024,128]{1,0:T(8,128)} custom-call(s32[1]{0:T(128)} %bitcast.parity, bf16[512,128]{1,0:T(8,128)(2,1)S(1)} %collective-permute-done.16.got_x, bf16[512,128]{1,0:T(8,128)(2,1)S(1)} %collective-permute-done.17.got_i, f32[1024,128]{1,0:T(8,128)S(1)} %get-tuple-element.99.local, f32[1024,128]{1,0:T(8,128)S(1)} %get-tuple-element.100.previous, ...), custom_call_target="tpu_custom_call" | custom-call | flops 134217728 | bytes 2359300 | tf_op jit(solution)/shard_map/pallas_call | solution.py:30
  (37 shorter events, 11.2 us)
Async XLA Ops:
  2.0 1.1 %copy-start.1 = (bf16[1280,16,16]{0,2,1:T(8,128)(2,1)S(1)}, bf16[1280,16,16]{0,2,1:T(8,128)(2,1)}, u32[]{:S(2)}) copy-start(bf16[1280,16,16]{0,2,1:T(8,128)(2,1)} %param.6) | copy-start | bytes 1966084
  3.1 6.3 %copy-start = (f32[64,16,128]{2,1,0:T(8,128)S(1)}, f32[64,16,128]{2,1,0:T(8,128)}, u32[]{:S(2)}) copy-start(f32[64,16,128]{2,1,0:T(8,128)} %param.5) | copy-start | bytes 1572868
  9.9 7.8 %collective-permute-start = (bf16[512,128]{1,0:T(8,128)(2,1)S(1)}, bf16[512,128]{1,0:T(8,128)(2,1)S(1)}, u32[]{:S(2)}, u32[]{:S(2)}) collective-permute-start(bf16[512,128]{1,0:T(8,128)(2,1)S(1)} %get-tuple-element.53), channel_id=1, source_target_pairs={{1,4},{5,8},{9,12},{13,0},{4,1},{8,5},{12,9},{0,13},{3,6},{7,10},{... | collective-permute-start | bytes 393224 | tf_op jit(solution)/shard_map/ppermute | solution.py:190
  14.5 3.2 %collective-permute-start.1 = (bf16[512,128]{1,0:T(8,128)(2,1)S(1)}, bf16[512,128]{1,0:T(8,128)(2,1)S(1)}, u32[]{:S(2)}, u32[]{:S(2)}) collective-permute-start(bf16[512,128]{1,0:T(8,128)(2,1)S(1)} %get-tuple-element.54), channel_id=1, source_target_pairs={{0,1},{1,0},{2,3},{3,2},{4,5},{5,4},{6,7},{7,6},{8,9},{9,8},{10,11... | collective-permute-start | bytes 393224 | tf_op jit(solution)/shard_map/ppermute | solution.py:190
  18.9 6.7 %collective-permute-start.2 = (bf16[512,128]{1,0:T(8,128)(2,1)S(1)}, bf16[512,128]{1,0:T(8,128)(2,1)S(1)}, u32[]{:S(2)}, u32[]{:S(2)}) collective-permute-start(bf16[512,128]{1,0:T(8,128)(2,1)S(1)} %get-tuple-element.60), channel_id=1, source_target_pairs={{1,4},{5,8},{9,12},{13,0},{4,1},{8,5},{12,9},{0,13},{3,6},{7,10},{... | collective-permute-start | bytes 393224 | tf_op jit(solution)/shard_map/ppermute | solution.py:190
  21.9 3.7 %collective-permute-start.3 = (bf16[512,128]{1,0:T(8,128)(2,1)S(1)}, bf16[512,128]{1,0:T(8,128)(2,1)S(1)}, u32[]{:S(2)}, u32[]{:S(2)}) collective-permute-start(bf16[512,128]{1,0:T(8,128)(2,1)S(1)} %get-tuple-element.61), channel_id=1, source_target_pairs={{0,1},{1,0},{2,3},{3,2},{4,5},{5,4},{6,7},{7,6},{8,9},{9,8},{10,11... | collective-permute-start | bytes 393224 | tf_op jit(solution)/shard_map/ppermute | solution.py:190
  26.8 6.3 %collective-permute-start.4 = (bf16[512,128]{1,0:T(8,128)(2,1)S(1)}, bf16[512,128]{1,0:T(8,128)(2,1)S(1)}, u32[]{:S(2)}, u32[]{:S(2)}) collective-permute-start(bf16[512,128]{1,0:T(8,128)(2,1)S(1)} %get-tuple-element.65), channel_id=1, source_target_pairs={{1,4},{5,8},{9,12},{13,0},{4,1},{8,5},{12,9},{0,13},{3,6},{7,10},{... | collective-permute-start | bytes 393224 | tf_op jit(solution)/shard_map/ppermute | solution.py:190
  29.4 3.7 %collective-permute-start.5 = (bf16[512,128]{1,0:T(8,128)(2,1)S(1)}, bf16[512,128]{1,0:T(8,128)(2,1)S(1)}, u32[]{:S(2)}, u32[]{:S(2)}) collective-permute-start(bf16[512,128]{1,0:T(8,128)(2,1)S(1)} %get-tuple-element.66), channel_id=1, source_target_pairs={{0,1},{1,0},{2,3},{3,2},{4,5},{5,4},{6,7},{7,6},{8,9},{9,8},{10,11... | collective-permute-start | bytes 393224 | tf_op jit(solution)/shard_map/ppermute | solution.py:190
  34.3 6.3 %collective-permute-start.6 = (bf16[512,128]{1,0:T(8,128)(2,1)S(1)}, bf16[512,128]{1,0:T(8,128)(2,1)S(1)}, u32[]{:S(2)}, u32[]{:S(2)}) collective-permute-start(bf16[512,128]{1,0:T(8,128)(2,1)S(1)} %get-tuple-element.70), channel_id=1, source_target_pairs={{1,4},{5,8},{9,12},{13,0},{4,1},{8,5},{12,9},{0,13},{3,6},{7,10},{... | collective-permute-start | bytes 393224 | tf_op jit(solution)/shard_map/ppermute | solution.py:190
  37.0 3.6 %collective-permute-start.7 = (bf16[512,128]{1,0:T(8,128)(2,1)S(1)}, bf16[512,128]{1,0:T(8,128)(2,1)S(1)}, u32[]{:S(2)}, u32[]{:S(2)}) collective-permute-start(bf16[512,128]{1,0:T(8,128)(2,1)S(1)} %get-tuple-element.71), channel_id=1, source_target_pairs={{0,1},{1,0},{2,3},{3,2},{4,5},{5,4},{6,7},{7,6},{8,9},{9,8},{10,11... | collective-permute-start | bytes 393224 | tf_op jit(solution)/shard_map/ppermute | solution.py:190
  41.9 6.4 %collective-permute-start.8 = (bf16[512,128]{1,0:T(8,128)(2,1)S(1)}, bf16[512,128]{1,0:T(8,128)(2,1)S(1)}, u32[]{:S(2)}, u32[]{:S(2)}) collective-permute-start(bf16[512,128]{1,0:T(8,128)(2,1)S(1)} %get-tuple-element.75), channel_id=1, source_target_pairs={{1,4},{5,8},{9,12},{13,0},{4,1},{8,5},{12,9},{0,13},{3,6},{7,10},{... | collective-permute-start | bytes 393224 | tf_op jit(solution)/shard_map/ppermute | solution.py:190
  44.7 3.6 %collective-permute-start.9 = (bf16[512,128]{1,0:T(8,128)(2,1)S(1)}, bf16[512,128]{1,0:T(8,128)(2,1)S(1)}, u32[]{:S(2)}, u32[]{:S(2)}) collective-permute-start(bf16[512,128]{1,0:T(8,128)(2,1)S(1)} %get-tuple-element.76), channel_id=1, source_target_pairs={{0,1},{1,0},{2,3},{3,2},{4,5},{5,4},{6,7},{7,6},{8,9},{9,8},{10,11... | collective-permute-start | bytes 393224 | tf_op jit(solution)/shard_map/ppermute | solution.py:190
  49.5 6.3 %collective-permute-start.10 = (bf16[512,128]{1,0:T(8,128)(2,1)S(1)}, bf16[512,128]{1,0:T(8,128)(2,1)S(1)}, u32[]{:S(2)}, u32[]{:S(2)}) collective-permute-start(bf16[512,128]{1,0:T(8,128)(2,1)S(1)} %get-tuple-element.84), channel_id=1, source_target_pairs={{1,4},{5,8},{9,12},{13,0},{4,1},{8,5},{12,9},{0,13},{3,6},{7,10},{... | collective-permute-start | bytes 393224 | tf_op jit(solution)/shard_map/ppermute | solution.py:190
  52.3 3.4 %collective-permute-start.11 = (bf16[512,128]{1,0:T(8,128)(2,1)S(1)}, bf16[512,128]{1,0:T(8,128)(2,1)S(1)}, u32[]{:S(2)}, u32[]{:S(2)}) collective-permute-start(bf16[512,128]{1,0:T(8,128)(2,1)S(1)} %get-tuple-element.85), channel_id=1, source_target_pairs={{0,1},{1,0},{2,3},{3,2},{4,5},{5,4},{6,7},{7,6},{8,9},{9,8},{10,11... | collective-permute-start | bytes 393224 | tf_op jit(solution)/shard_map/ppermute | solution.py:190
  52.3 1.4 %collective-permute-start.12 = (f32[9,128]{1,0:T(8,128)S(1)}, f32[9,128]{1,0:T(8,128)S(1)}, u32[]{:S(2)}, u32[]{:S(2)}) collective-permute-start(f32[9,128]{1,0:T(8,128)S(1)} %get-tuple-element.87.refs_0_), channel_id=1, source_target_pairs={{0,1},{1,0},{2,3},{3,2},{4,5},{5,4},{6,7},{7,6},{8,9},{9,8},{10,11... | collective-permute-start | bytes 13832 | tf_op jit(solution)/shard_map/ppermute | solution.py:169
  57.0 7.2 %collective-permute-start.13 = (bf16[512,128]{1,0:T(8,128)(2,1)S(1)}, bf16[512,128]{1,0:T(8,128)(2,1)S(1)}, u32[]{:S(2)}, u32[]{:S(2)}) collective-permute-start(bf16[512,128]{1,0:T(8,128)(2,1)S(1)} %get-tuple-element.89), channel_id=1, source_target_pairs={{1,4},{5,8},{9,12},{13,0},{4,1},{8,5},{12,9},{0,13},{3,6},{7,10},{... | collective-permute-start | bytes 393224 | tf_op jit(solution)/shard_map/ppermute | solution.py:190
  59.8 4.4 %collective-permute-start.14 = (bf16[512,128]{1,0:T(8,128)(2,1)S(1)}, bf16[512,128]{1,0:T(8,128)(2,1)S(1)}, u32[]{:S(2)}, u32[]{:S(2)}) collective-permute-start(bf16[512,128]{1,0:T(8,128)(2,1)S(1)} %get-tuple-element.90), channel_id=1, source_target_pairs={{0,1},{1,0},{2,3},{3,2},{4,5},{5,4},{6,7},{7,6},{8,9},{9,8},{10,11... | collective-permute-start | bytes 393224 | tf_op jit(solution)/shard_map/ppermute | solution.py:190
  59.8 3.7 %collective-permute-start.15 = (f32[9,128]{1,0:T(8,128)S(1)}, f32[9,128]{1,0:T(8,128)S(1)}, u32[]{:S(2)}, u32[]{:S(2)}) collective-permute-start(f32[9,128]{1,0:T(8,128)S(1)} %get-tuple-element.92.refs_0_), channel_id=1, source_target_pairs={{0,4},{4,0},{8,12},{12,8},{1,5},{5,1},{9,13},{13,9},{2,6},{6,2},{1... | collective-permute-start | bytes 13832 | tf_op jit(solution)/shard_map/ppermute | solution.py:169
  65.8 7.8 %collective-permute-start.16 = (bf16[512,128]{1,0:T(8,128)(2,1)S(1)}, bf16[512,128]{1,0:T(8,128)(2,1)S(1)}, u32[]{:S(2)}, u32[]{:S(2)}) collective-permute-start(bf16[512,128]{1,0:T(8,128)(2,1)S(1)} %get-tuple-element.95), channel_id=1, source_target_pairs={{1,4},{5,8},{9,12},{13,0},{4,1},{8,5},{12,9},{0,13},{3,6},{7,10},{... | collective-permute-start | bytes 393224 | tf_op jit(solution)/shard_map/ppermute | solution.py:190
  67.5 6.0 %collective-permute-start.17 = (bf16[512,128]{1,0:T(8,128)(2,1)S(1)}, bf16[512,128]{1,0:T(8,128)(2,1)S(1)}, u32[]{:S(2)}, u32[]{:S(2)}) collective-permute-start(bf16[512,128]{1,0:T(8,128)(2,1)S(1)} %get-tuple-element.96), channel_id=1, source_target_pairs={{0,1},{1,0},{2,3},{3,2},{4,5},{5,4},{6,7},{7,6},{8,9},{9,8},{10,11... | collective-permute-start | bytes 393224 | tf_op jit(solution)/shard_map/ppermute | solution.py:190
  67.5 4.8 %collective-permute-start.18 = (f32[9,128]{1,0:T(8,128)S(1)}, f32[9,128]{1,0:T(8,128)S(1)}, u32[]{:S(2)}, u32[]{:S(2)}) collective-permute-start(f32[9,128]{1,0:T(8,128)S(1)} %get-tuple-element.98.refs_0_), channel_id=1, source_target_pairs={{0,8},{4,12},{8,0},{12,4},{1,9},{5,13},{9,1},{13,5},{2,10},{6,14},... | collective-permute-start | bytes 13832 | tf_op jit(solution)/shard_map/ppermute | solution.py:169

commit v3 on v0

v3 whole, which is shorter than its diff:
```python
import functools

import jax
import jax.numpy as jnp
from jax import lax
from jax.experimental import pallas as pl
from jax.experimental.pallas import tpu as pltpu
from jax.sharding import PartitionSpec as P

STEPS = 8
HALF = STEPS // 2
RING = ("dom", "orb")
F32, BF16 = jnp.float32, jnp.bfloat16
VMEM = pl.BlockSpec(memory_space=pltpu.VMEM)
SMEM = pl.BlockSpec(memory_space=pltpu.SMEM)
NT = (((1,), (1,)), ((), ()))
UNROLL = 8
PAD = 8
ROWS = 16
TAIL = 3 * ROWS
LONGER = ROWS
DOTS = [[(0, n)] + [(m, n) for m in (n - 1, n) if m > 0 and HALF < m + n] for n in range(HALF + 1)]


def operands_of(n):
    return sorted({m for pair in DOTS[n] for m in pair})


def call(body, outs, *operands, flops=0, scratch=(), smem=0, limit=16):
    size = sum(o.size * o.dtype.itemsize for o in operands)
    return pl.pallas_call(
        body,
        out_shape=tuple(jax.ShapeDtypeStruct(s, t) for s, t in outs),
        in_specs=[SMEM] * smem + [VMEM] * (len(operands) - smem),
        out_specs=(VMEM,) * len(outs),
        scratch_shapes=scratch,
        compiler_params=pltpu.CompilerParams(vmem_limit_bytes=limit << 20),
        cost_estimate=pl.CostEstimate(flops=flops, bytes_accessed=size, transcendentals=0) if flops else None,
    )(*operands)


def place(atoms, orbits, first, total, pair, blocks, target, row_hot):
    slots = blocks.shape[1]
    pair_id = pair[...].reshape(1, slots)
    col_id = lax.div(pair_id, atoms)
    row_id = pair_id - col_id * atoms
    row_hot[...] = jnp.where(lax.broadcasted_iota(jnp.int32, (atoms, slots), 0) == row_id, 1.0, 0.0).astype(BF16)
    lanes = 2 * atoms
    lane = lax.broadcasted_iota(jnp.int32, (orbits, lanes), 1)

    def one(q, _):
        hot = []
        for n in range(4):
            here = jnp.where(col_id == first + 4 * q + n, 1.0, 0.0).astype(BF16)
            hot.append(row_hot[...] * here)
        hot = jnp.concatenate(hot, axis=0)
        tile = lax.dot_general(blocks[...], hot, NT, preferred_element_type=F32)
        for two in range(2):
            for i in range(0, orbits, 2):
                at = slice(two * lanes, (two + 1) * lanes)
                left = tile[i * orbits : (i + 1) * orbits, at]
                right = tile[(i + 1) * orbits : (i + 2) * orbits, at]
                low = jnp.where(lane < atoms, left, pltpu.roll(right, atoms, 1))
                high = jnp.where(lane < atoms, pltpu.roll(left, atoms, 1), right)
                col = 4 * q + 2 * two
                target[i // 2, pl.ds(col, orbits, stride=total + PAD), :] = low
                target[i // 2, pl.ds(col + 1, orbits, stride=total + PAD), :] = high
        return 0

    lax.fori_loop(0, total // 4, one, 0, unroll=UNROLL)


def gather_rows(source, piece, total, orbitals):
    starts = [j * (total + PAD) for j in orbitals]
    return jnp.concatenate([source[piece, start : start + total, :] for start in starts], axis=0)


def cross_body(atoms, orbits, halo, pair, blocks, crosst_ref, cross_f32, row_hot):
    place(atoms, orbits, atoms, halo, pair, blocks, cross_f32, row_hot)
    lanes = 2 * atoms
    for p in range(orbits // 2):
        at = slice(p * lanes, (p + 1) * lanes)
        crosst_ref[:, at] = gather_rows(cross_f32, p, halo, range(orbits)).astype(BF16)


def own_body(atoms, orbits, halo, pair, blocks, crosst, _, own_ref, cross_ref, gram_ref, own_f32, row_hot):
    place(atoms, orbits, 0, atoms, pair, blocks, own_f32, row_hot)
    lanes = 2 * atoms
    for p in range(orbits // 2):
        at = slice(p * lanes, (p + 1) * lanes)
        cross_ref[at, :] = crosst[:, at].astype(F32).T.astype(BF16)
        turned = gather_rows(own_f32, p, atoms, range(orbits)).T
        for n in range(orbits // 2):
            here = slice(n * lanes, (n + 1) * lanes)
            other = gather_rows(own_f32, n, atoms, (2 * p, 2 * p + 1))
            own_ref[at, here] = (other + turned[:, here]).astype(BF16)
    gram_ref[...] = jnp.dot(crosst[...], cross_ref[...], preferred_element_type=F32).astype(BF16)


def put_edge(atoms, halo, w, out):
    for o in range(w.shape[0] // atoms):
        out[o * halo : (o + 1) * halo, :] = w[o * atoms : o * atoms + halo, :]


def blank(out, start):
    out[start:, :] = jnp.zeros((out.shape[0] - start, out.shape[1]), out.dtype)


def times(left, right):
    return jnp.dot(left[...], right[...], preferred_element_type=F32)


def first_body(atoms, orbits, halo, turn, parity, probes, crosst, v_ref, w_ref, out_x, out_i):
    for o in range(orbits):
        rows = slice(o * atoms, (o + 1) * atoms)
        v = probes[pl.ds(o, atoms, stride=orbits), :] if turn else probes[rows, :]
        v_ref[rows, :] = v
        w_ref[rows, :] = v.astype(BF16)

    @pl.when(parity[0] == 0)
    def _():
        put_edge(atoms, halo, w_ref, out_x)
        out_i[...] = times(crosst, w_ref).astype(BF16)

    blank(out_x, orbits * halo)

    @pl.when(parity[0] != 0)
    def _():
        put_edge(atoms, halo, w_ref, out_i)
        out_x[: orbits * halo, :] = times(crosst, w_ref).astype(BF16)


def dots_of(n, refs):
    vectors = dict(zip(operands_of(n), refs))
    return [jnp.sum(vectors[a][...] * vectors[b][...], axis=0, keepdims=True) for a, b in DOTS[n]]


def local_body(k, own, w, *refs):
    refs[-1 if k >= HALF else -2][...] = times(own, w)
    if k < HALF:
        refs[-1][...] = jnp.concatenate(dots_of(k, refs), axis=0)


def table_of(scale, made, tables):
    dots = dict(zip(DOTS[HALF], made))
    for table, pairs in zip(tables, DOTS):
        dots.update({pair: table[n : n + 1, :] for n, pair in enumerate(pairs)})
    rows = [dots[0, n] for n in range(HALF + 1)]
    for n in range(HALF + 1, STEPS + 1):
        rows.append(2.0 * dots[n // 2, n - n // 2] - dots[0, n % 2])
    rows.append(jnp.zeros((ROWS - STEPS - 1, rows[0].shape[1]), F32))
    return jnp.concatenate(rows, axis=0) * scale


def put_table(table, out, start):
    for n in range(3):
        piece = table.astype(BF16)
        out[start + n * ROWS : start + (n + 1) * ROWS, :] = piece
        table = table - piece.astype(F32)


def get_table(got, start):
    pieces = [got[start + n * ROWS : start + (n + 1) * ROWS, :].astype(F32) for n in range(3)]
    return pieces[0] + (pieces[1] + pieces[2])


def before_body(atoms, orbits, halo, k, parity, got_i, local, previous, cross, crosst, base_ref, pre_ref=None):
    edge_size = orbits * halo
    grown = lambda total, rows: total if k == 0 else 2.0 * total - previous[rows, :]

    @pl.when(parity[0] == 0)
    def _():
        total = local[...] + times(cross, got_i[:edge_size, :])
        base_ref[...] = grown(total, slice(None))
        if pre_ref is not None:
            put_edge(atoms, halo, base_ref, pre_ref)

    @pl.when(parity[0] != 0)
    def _():
        for o in range(orbits):
            near = slice(o * atoms, o * atoms + halo)
            far = slice(o * atoms + halo, (o + 1) * atoms)
            back = got_i[o * halo : (o + 1) * halo, :].astype(F32)
            base_ref[near, :] = grown(local[near, :] + back, near)
            base_ref[far, :] = grown(local[far, :], far)
        if pre_ref is not None:
            pre_ref[...] = times(crosst, base_ref[...].astype(BF16))


def send_body(k, tail, parity, got_x, pre, gram, *refs):
    out = refs[-1]
    edge_size = pre.shape[0]
    factor = 1.0 if k == 0 else 2.0

    @pl.when(parity[0] == 0)
    def _():
        out[:edge_size, :] = (pre[...] + factor * got_x[:edge_size, :].astype(F32)).astype(BF16)

    @pl.when(parity[0] != 0)
    def _():
        out[:edge_size, :] = (pre[...] + factor * times(gram, got_x[:edge_size, :])).astype(BF16)

    if tail == "sum":
        table, got = refs[:-1]
        put_table(table[...] + get_table(got, edge_size), out, edge_size)
        blank(out, edge_size + TAIL)
    elif tail == "pass":
        out[edge_size : edge_size + TAIL, :] = refs[0][edge_size : edge_size + TAIL, :]
        blank(out, edge_size + TAIL)
    else:
        blank(out, edge_size)


def finish(atoms, orbits, halo, k, parity, got_x, base, cross, write):
    factor = 1.0 if k == 0 else 2.0

    @pl.when(parity[0] == 0)
    def _():
        for o in range(orbits):
            near = slice(o * atoms, o * atoms + halo)
            back = got_x[o * halo : (o + 1) * halo, :].astype(F32)
            write(o, 0, base[near, :] + factor * back)
            write(o, halo, base[o * atoms + halo : (o + 1) * atoms, :])

    @pl.when(parity[0] != 0)
    def _():
        total = base[...] + factor * times(cross, got_x[: orbits * halo, :])
        for o in range(orbits):
            write(o, 0, total[o * atoms : (o + 1) * atoms, :])


def next_body(atoms, orbits, halo, k, tail, scale, ride, parity, got_x, base, cross, crosst, _, *refs):
    keep = k < STEPS - 2
    outs = refs[len(refs) - 2 - keep - (tail == "start") :]
    (v_ref, w_ref, out) = outs[:3] if keep else (None, *outs)
    edge_size = orbits * halo

    def write(o, at, piece):
        rows = slice(o * atoms + at, o * atoms + at + piece.shape[0])
        if keep:
            v_ref[rows, :] = piece
        w_ref[rows, :] = piece.astype(BF16)

    finish(atoms, orbits, halo, k, parity, got_x, base, cross, write)

    @pl.when(parity[0] == 0)
    def _():
        out[:edge_size, :] = times(crosst, w_ref).astype(BF16)

    @pl.when(parity[0] != 0)
    def _():
        put_edge(atoms, halo, w_ref, out)

    if tail == "start":
        others = operands_of(HALF)[:-1]
        made = dots_of(HALF, refs[: len(others)] + (v_ref,))
        table = table_of(scale, made, refs[len(others) : len(others) + HALF])
        outs[3][...] = table
        if ride:
            put_table(table, out, edge_size)
    elif tail == "pass":
        out[edge_size:, :] = got_x[edge_size : edge_size + TAIL, :]


def last_body(atoms, orbits, halo, k, turn, parity, got_x, base, cross, table, *refs):
    out, moments = refs[-2:]
    edge_size = orbits * halo

    def write(o, at, piece):
        rows = slice(o * atoms + at, o * atoms + at + piece.shape[0])
        out[pl.ds(at * orbits + o, piece.shape[0], stride=orbits) if turn else rows, :] = piece

    finish(atoms, orbits, halo, k, parity, got_x, base, cross, write)
    total = table[...]
    for got in refs[:-2]:
        total = total + get_table(got, edge_size)
    moments[...] = total[: STEPS + 1, :]


def per_device(probes, blocks, block_rows, block_cols, counts):
    atoms, orbits, width = probes.shape
    halo = atoms // 2
    size, edge_size = atoms * orbits, halo * orbits
    slots = blocks.shape[0]
    dims = (atoms, orbits, halo)
    turn = width == 128
    ring = lax.axis_size(RING)
    ride = ring == STEPS
    scale = 1.0 / (size * ring)
    parity = lax.axis_index("orb").astype(jnp.int32).reshape(1)
    between = [(i, (i + 1) % ring) for i in range(1, ring, 2)]
    between = between + [(b, a) for a, b in between]
    across = lambda x: lax.ppermute(x, RING, between)
    inside = lambda x: lax.ppermute(x, "orb", [(0, 1), (1, 0)])

    slot = jnp.arange(slots, dtype=jnp.int32)
    pair = jnp.where(slot < counts[0], block_cols * atoms + block_rows, -atoms)
    flat = blocks.transpose(1, 2, 0).reshape(orbits * orbits, slots)
    row_hot = pltpu.VMEM((atoms, slots), BF16)
    (crosst,) = call(
        functools.partial(cross_body, *dims),
        (((edge_size, size), BF16),),
        pair, flat,
        flops=2 * orbits * orbits * slots * atoms * halo,
        scratch=[pltpu.VMEM((orbits // 2, orbits * (halo + PAD), 2 * atoms), F32), row_hot],
        limit=24,
    )
    whole, rounded, message = ((size, width), F32), ((size, width), BF16), ((edge_size, width), BF16)
    longer = ((edge_size + TAIL, width), BF16)
    far_rows = [edge_size + LONGER + (TAIL if ride and k >= HALF else 0) for k in range(STEPS)]
    v, w, send_x, send_i = call(
        functools.partial(first_body, *dims, turn),
        (whole, rounded, ((far_rows[0], width), BF16), message),
        parity,
        (probes if turn else probes.transpose(1, 0, 2)).reshape(size, width),
        crosst,
        smem=1,
    )
    vectors, tables, got = [v], [], []
    for k in range(STEPS):
        got_x = across(send_x)
        if k > 0:
            tail = {HALF: "start", HALF + 2: "pass"}.get(k) if ride or k == HALF else None
            extra, outs = (), (whole, rounded, longer if tail and ride else message)[k == STEPS - 1 :]
            if k == HALF:
                extra, outs = (*(vectors[m] for m in operands_of(HALF)[:-1]), *tables), outs + (((ROWS, width), F32),)
            made = call(
                functools.partial(next_body, *dims, k - 1, tail, scale, ride),
                outs, parity, arrived, base, cross, crosst, send_x, *extra, smem=1,
            )
            if k < STEPS - 1:
                vectors.append(made[0])
            w, send_i = made[k < STEPS - 1 :][:2]
            if k == HALF:
                table = made[3]
        got_i = inside(send_i)
        if k == 0:
            own, cross, gram = call(
                functools.partial(own_body, *dims),
                (((size, size), BF16), ((size, edge_size), BF16), ((edge_size, edge_size), BF16)),
                pair, flat, crosst, send_i,
                scratch=[pltpu.VMEM((orbits // 2, orbits * (atoms + PAD), 2 * atoms), F32), row_hot],
                limit=24,
            )
        dots = ()
        if k < HALF:
            dots = (((len(DOTS[k]), width), F32),)
        made = call(
            functools.partial(local_body, k),
            (whole,) + dots,
            own, w, *((vectors[m] for m in operands_of(k)) if k < HALF else ()),
        )
        local, tables = made[0], tables + list(made[1:])
        base, *pre = call(
            functools.partial(before_body, *dims, k),
            (whole, ((edge_size, width), F32))[: 2 - (k == STEPS - 1)],
            parity, got_i, local, vectors[max(k - 1, 0)], cross, crosst, smem=1,
        )
        arrived = got_x
        if k < STEPS - 1:
            tail = {HALF: "sum", HALF + 2: "pass"}.get(k) if ride else None
            extra = {"sum": (table, got_i), "pass": (got_i,)}[tail] if tail else ()
            (send_x,) = call(
                functools.partial(send_body, k, tail),
                (((far_rows[k + 1], width), BF16),),
                parity, got_x, *pre, gram, *extra, smem=1,
            )
        if ride and k >= HALF:
            got.append(got_i if k % 2 == 0 else got_x)
    last, moments = call(
        functools.partial(last_body, *dims, STEPS - 1, turn),
        (whole, ((STEPS + 1, width), F32)),
        parity, got_x, base, cross, table, *got, smem=1,
    )
    last = last.reshape(atoms, orbits, width) if turn else last.reshape(orbits, atoms, width).transpose(1, 0, 2)
    return last, moments if ride else lax.psum(moments, RING)


def solution(mesh):
    in_specs = (
        P(("groups", "dom", "orb"), None, "probe"),
        P(("groups", "dom", "orb"), None, None),
        P(("groups", "dom", "orb")),
        P(("groups", "dom", "orb")),
        P(("groups", "dom", "orb")),
    )
    out_specs = (P(("groups", "dom", "orb"), None, "probe"), P("groups", "probe"))
    return jax.shard_map(
        per_device, mesh=mesh, in_specs=in_specs, out_specs=out_specs, check_vma=False
    )
```

time: 548 us -> 64.1 us (0.12)
  local copies, waits for them, and re-layouts: 268 us -> 1.09 us
  blocking collectives: 112 us -> 0 us
  other arithmetic: 80 us -> 0.72 us
  matrix products: 44.3 us -> 0 us
  Pallas kernels: 0 us -> 22.2 us
  starting transfers between devices: 8.42 us -> 16.8 us
  waiting for transfers between devices: 27.8 us -> 21.5 us
    convert_element_type x4 -> x0, local copies, waits for them, and re-layouts: 126 us -> none  [the longest x2 63.3 us: per_device(): low = (dense - high.astype(jnp.float32)).astype(jnp.bfloat16)]
    psum x8 -> x0, blocking collectives: 112 us -> none  [moment(): return lax.psum(local_term, ('dom', 'orb'))]
    reshape x3 -> x0, local copies, waits for them, and re-layouts: 50.6 us -> none  [the longest x1 41.2 us: per_device(): dense = dense.reshape(atoms * orbits, columns * orbits)]
    dot_general x32 -> x0, matrix products: 44.3 us -> none  [the longest x8 18.6 us: two_part_t(): jnp.einsum('ac,ap->cp', high, right, preferred_element_type=jnp.float32)]
    while x56 -> x0, local copies, waits for them, and re-layouts: 32.3 us -> none
    transpose x1 -> x0, local copies, waits for them, and re-layouts: 28.8 us -> none  [per_device(): dense = summed.reshape(atoms, columns, orbits, orbits).transpose(0, 2, 1, 3)]
    convert_element_type x11 -> x0, other arithmetic: 26.4 us -> none  [the longest x2 11.1 us: per_device(): low = (dense - high.astype(jnp.float32)).astype(jnp.bfloat16)]
    pallas_call x0 -> x34, Pallas kernels: none -> 22.2 us  [call(): pl.pallas_call(body, out_shape=tuple((jax.ShapeDtypeStruct(s, t) for s, t...]
  transfers between devices with their start and end apart: 16 -> 16, of which waited for: 7 -> 14; matrix products, arithmetic and copies ran while one was open for 56% -> 0% of each run, Pallas kernels for 0% -> 29%
where the time goes in v3:
time: 64.1 us; the launch traced here: 63.8 us
  Pallas kernels  22.2 us (35%)
  waiting for transfers between devices  21.5 us (34%)
  starting transfers between devices  16.8 us (26%)
  between operations  1.6 us (2%)
  local copies, waits for them, and re-layouts  1.09 us (2%)
  other arithmetic  0.72 us (1%)
    pallas_call x34, Pallas kernels, call(): pl.pallas_call(body, out_shape=tuple((jax.ShapeDtypeStruct(s, t) for s, t...  22.2 us
    ppermute x8, waiting for transfers between devices, per_device(): across = lambda x: lax.ppermute(x, RING, between)  17.1 us
    ppermute x8, starting transfers between devices, per_device(): across = lambda x: lax.ppermute(x, RING, between)  16.3 us
    ppermute x8, waiting for transfers between devices, per_device(): inside = lambda x: lax.ppermute(x, 'orb', [(0, 1), (1, 0)])  4.38 us
  transfers between devices with their start and end apart: 16, of which 14 were waited for; matrix products, arithmetic and copies ran while one was open for 0% of the time, Pallas kernels for 29%

profile of v3, /device:TPU:0, one launch (start us, length us, event | category | flops | bytes accessed | tf_op | source)
XLA Modules:
  0.0 63.8 jit_solution(18021022683272336775)
XLA Ops:
  1.3 0.7 %add_select_fusion.pair = s32[1280]{0:T(1024)S(1)} fusion(s32[1280]{0:T(1024)} %param.7, s32[1280]{0:T(1024)} %param.8, s32[]{:T(128)} %bitcast.7), kind=kLoop, calls=%fused_computation | loop fusion | flops 5120 | bytes 15364 | tf_op jit(solution)/shard_map/jit(_where)/select_n | solution.py:297
  2.0 1.1 %copy-done = bf16[1280,16,16]{0,2,1:T(8,128)(2,1)S(1)} copy-done((bf16[1280,16,16]{0,2,1:T(8,128)(2,1)S(1)}, bf16[1280,16,16]{0,2,1:T(8,128)(2,1)}, u32[]{:S(2)}) %copy-start) | copy-done | bytes 655384
  3.1 2.0 %shard_map.68.crosst = bf16[512,1024]{1,0:T(8,128)(2,1)S(1)} custom-call(s32[1280]{0:T(1024)S(1)} %add_select_fusion.pair, bf16[256,1280]{1,0:T(8,128)(2,1)S(1)} %bitcast.8), custom_call_target="tpu_custom_call" | custom-call | flops 1342177280 | bytes 660480 | tf_op jit(solution)/shard_map/pallas_call | solution.py:31
  5.7 4.6 %collective-permute-start = (bf16[528,128]{1,0:T(8,128)(2,1)S(1)}, bf16[528,128]{1,0:T(8,128)(2,1)S(1)}, u32[]{:S(2)}, u32[]{:S(2)}) collective-permute-start(bf16[528,128]{1,0:T(8,128)(2,1)S(1)} %get-tuple-element.54), channel_id=1, source_target_pairs={{1,4},{5,8},{9,12},{13,0},{4,1},{8,5},{12,9},{0,13},{3,6},{7,10},{... | collective-permute-start | bytes 405512 | tf_op jit(solution)/shard_map/ppermute | solution.py:293
  10.3 5.2 %shard_map.70 = (bf16[1024,1024]{1,0:T(8,128)(2,1)S(1)}, bf16[1024,512]{1,0:T(8,128)(2,1)S(1)}, bf16[512,512]{1,0:T(8,128)(2,1)S(1)}) custom-call(s32[1280]{0:T(1024)S(1)} %add_select_fusion.pair, bf16[256,1280]{1,0:T(8,128)(2,1)S(1)} %bitcast.9, bf16[512,1024]{1,0:T(8,128)(2,1)S(1)} %shard_map.68.crosst, bf16[512,128]{1,0:T(8,128)(2,1)S(1)} %get-tuple-element.55._), custom_call_target="tpu_custom_call" | custom-call | tf_op jit(solution)/shard_map/pallas_call | solution.py:31
  16.7 1.1 %collective-permute-start.2 = (bf16[528,128]{1,0:T(8,128)(2,1)S(1)}, bf16[528,128]{1,0:T(8,128)(2,1)S(1)}, u32[]{:S(2)}, u32[]{:S(2)}) collective-permute-start(bf16[528,128]{1,0:T(8,128)(2,1)S(1)} %shard_map.73._), channel_id=1, source_target_pairs={{1,4},{5,8},{9,12},{13,0},{4,1},{8,5},{12,9},{0,13},{3,6},{7,10},{... | collective-permute-start | bytes 405512 | tf_op jit(solution)/shard_map/ppermute | solution.py:293
  18.4 0.7 %shard_map.75 = (f32[1024,128]{1,0:T(8,128)S(1)}, f32[1,128]{1,0:T(1,128)S(1)}) custom-call(bf16[1024,1024]{1,0:T(8,128)(2,1)S(1)} %get-tuple-element.56.own, bf16[1024,128]{1,0:T(8,128)(2,1)S(1)} %get-tuple-element.65.w, f32[1024,128]{1,0:T(8,128)S(1)} %get-tuple-element.58.refs_0_.previous, f32[1024,128]{1,0:T(8,128)S(1)} %get-tuple-element.66.refs_1_.previous), custom_call_target="tpu_custom_call" | custom-call | tf_op jit(solution)/shard_map/pallas_call | solution.py:31
  20.1 3.6 %collective-permute-done.2.got_x = bf16[528,128]{1,0:T(8,128)(2,1)S(1)} collective-permute-done((bf16[528,128]{1,0:T(8,128)(2,1)S(1)}, bf16[528,128]{1,0:T(8,128)(2,1)S(1)}, u32[]{:S(2)}, u32[]{:S(2)}) %collective-permute-start.2) | collective-permute-done | bytes 135200 | tf_op jit(solution)/shard_map/ppermute | solution.py:293
  23.8 1.1 %collective-permute-start.4 = (bf16[528,128]{1,0:T(8,128)(2,1)S(1)}, bf16[528,128]{1,0:T(8,128)(2,1)S(1)}, u32[]{:S(2)}, u32[]{:S(2)}) collective-permute-start(bf16[528,128]{1,0:T(8,128)(2,1)S(1)} %shard_map.77._), channel_id=1, source_target_pairs={{1,4},{5,8},{9,12},{13,0},{4,1},{8,5},{12,9},{0,13},{3,6},{7,10},{... | collective-permute-start | bytes 405512 | tf_op jit(solution)/shard_map/ppermute | solution.py:293
  25.5 0.7 %shard_map.79 = (f32[1024,128]{1,0:T(8,128)S(1)}, f32[1,128]{1,0:T(1,128)S(1)}) custom-call(bf16[1024,1024]{1,0:T(8,128)(2,1)S(1)} %get-tuple-element.56.own, bf16[1024,128]{1,0:T(8,128)(2,1)S(1)} %get-tuple-element.71.w, f32[1024,128]{1,0:T(8,128)S(1)} %get-tuple-element.58.refs_0_.previous, f32[1024,128]{1,0:T(8,128)S(1)} %get-tuple-element.72.refs_1_.previous), custom_call_target="tpu_custom_call" | custom-call | tf_op jit(solution)/shard_map/pallas_call | solution.py:31
  27.3 2.8 %collective-permute-done.4.got_x = bf16[528,128]{1,0:T(8,128)(2,1)S(1)} collective-permute-done((bf16[528,128]{1,0:T(8,128)(2,1)S(1)}, bf16[528,128]{1,0:T(8,128)(2,1)S(1)}, u32[]{:S(2)}, u32[]{:S(2)}) %collective-permute-start.4) | collective-permute-done | bytes 135200 | tf_op jit(solution)/shard_map/ppermute | solution.py:293
  30.2 1.4 %collective-permute-start.6 = (bf16[528,128]{1,0:T(8,128)(2,1)S(1)}, bf16[528,128]{1,0:T(8,128)(2,1)S(1)}, u32[]{:S(2)}, u32[]{:S(2)}) collective-permute-start(bf16[528,128]{1,0:T(8,128)(2,1)S(1)} %shard_map.81._), channel_id=1, source_target_pairs={{1,4},{5,8},{9,12},{13,0},{4,1},{8,5},{12,9},{0,13},{3,6},{7,10},{... | collective-permute-start | bytes 405512 | tf_op jit(solution)/shard_map/ppermute | solution.py:293
  32.3 0.7 %shard_map.83 = (f32[1024,128]{1,0:T(8,128)S(1)}, f32[3,128]{1,0:T(4,128)S(1)}) custom-call(bf16[1024,1024]{1,0:T(8,128)(2,1)S(1)} %get-tuple-element.56.own, bf16[1024,128]{1,0:T(8,128)(2,1)S(1)} %get-tuple-element.77.w, f32[1024,128]{1,0:T(8,128)S(1)} %get-tuple-element.58.refs_0_.previous, f32[1024,128]{1,0:T(8,128)S(1)} %get-tuple-element.72.refs_1_.previous, ...), custom_call_target="tpu_custom_call" | custom-call | tf_op jit(solution)/shard_map/pallas_call | solution.py:31
  34.1 2.5 %collective-permute-done.6.got_x = bf16[528,128]{1,0:T(8,128)(2,1)S(1)} collective-permute-done((bf16[528,128]{1,0:T(8,128)(2,1)S(1)}, bf16[528,128]{1,0:T(8,128)(2,1)S(1)}, u32[]{:S(2)}, u32[]{:S(2)}) %collective-permute-start.6) | collective-permute-done | bytes 135200 | tf_op jit(solution)/shard_map/ppermute | solution.py:293
  36.6 1.7 %collective-permute-start.8 = (bf16[576,128]{1,0:T(8,128)(2,1)S(1)}, bf16[576,128]{1,0:T(8,128)(2,1)S(1)}, u32[]{:S(2)}, u32[]{:S(2)}) collective-permute-start(bf16[576,128]{1,0:T(8,128)(2,1)S(1)} %shard_map.85._), channel_id=1, source_target_pairs={{1,4},{5,8},{9,12},{13,0},{4,1},{8,5},{12,9},{0,13},{3,6},{7,10},{... | collective-permute-start | bytes 442376 | tf_op jit(solution)/shard_map/ppermute | solution.py:293
  38.3 0.7 %shard_map.86 = (f32[1024,128]{1,0:T(8,128)S(1)}, bf16[1024,128]{1,0:T(8,128)(2,1)S(1)}, bf16[560,128]{1,0:T(8,128)(2,1)S(1)}, f32[16,128]{1,0:T(8,128)S(1)}) custom-call(s32[1]{0:T(128)} %bitcast.parity, bf16[528,128]{1,0:T(8,128)(2,1)S(1)} %collective-permute-done.6.got_x, f32[1024,128]{1,0:T(8,128)S(1)} %get-tuple-element.81.base, ...), custom_call_target="tpu_custom_call" | custom-call | tf_op jit(solution)/shard_map/pallas_call | solution.py:31
  40.9 2.3 %collective-permute-done.8.got_x = bf16[576,128]{1,0:T(8,128)(2,1)S(1)} collective-permute-done((bf16[576,128]{1,0:T(8,128)(2,1)S(1)}, bf16[576,128]{1,0:T(8,128)(2,1)S(1)}, u32[]{:S(2)}, u32[]{:S(2)}) %collective-permute-start.8) | collective-permute-done | bytes 147488 | tf_op jit(solution)/shard_map/ppermute | solution.py:293
  43.2 1.9 %collective-permute-start.10 = (bf16[576,128]{1,0:T(8,128)(2,1)S(1)}, bf16[576,128]{1,0:T(8,128)(2,1)S(1)}, u32[]{:S(2)}, u32[]{:S(2)}) collective-permute-start(bf16[576,128]{1,0:T(8,128)(2,1)S(1)} %shard_map.89._), channel_id=1, source_target_pairs={{1,4},{5,8},{9,12},{13,0},{4,1},{8,5},{12,9},{0,13},{3,6},{7,10},{... | collective-permute-start | bytes 442376 | tf_op jit(solution)/shard_map/ppermute | solution.py:293
  47.5 2.2 %collective-permute-done.10.got_x.refs_1_ = bf16[576,128]{1,0:T(8,128)(2,1)S(1)} collective-permute-done((bf16[576,128]{1,0:T(8,128)(2,1)S(1)}, bf16[576,128]{1,0:T(8,128)(2,1)S(1)}, u32[]{:S(2)}, u32[]{:S(2)}) %collective-permute-start.10) | collective-permute-done | bytes 147488 | tf_op jit(solution)/shard_map/ppermute | solution.py:293
  49.8 2.2 %collective-permute-start.12 = (bf16[576,128]{1,0:T(8,128)(2,1)S(1)}, bf16[576,128]{1,0:T(8,128)(2,1)S(1)}, u32[]{:S(2)}, u32[]{:S(2)}) collective-permute-start(bf16[576,128]{1,0:T(8,128)(2,1)S(1)} %shard_map.93._), channel_id=1, source_target_pairs={{1,4},{5,8},{9,12},{13,0},{4,1},{8,5},{12,9},{0,13},{3,6},{7,10},{... | collective-permute-start | bytes 442376 | tf_op jit(solution)/shard_map/ppermute | solution.py:293
  54.4 2.0 %collective-permute-done.12.got_x = bf16[576,128]{1,0:T(8,128)(2,1)S(1)} collective-permute-done((bf16[576,128]{1,0:T(8,128)(2,1)S(1)}, bf16[576,128]{1,0:T(8,128)(2,1)S(1)}, u32[]{:S(2)}, u32[]{:S(2)}) %collective-permute-start.12) | collective-permute-done | bytes 147488 | tf_op jit(solution)/shard_map/ppermute | solution.py:293
  56.4 2.4 %collective-permute-start.14 = (bf16[576,128]{1,0:T(8,128)(2,1)S(1)}, bf16[576,128]{1,0:T(8,128)(2,1)S(1)}, u32[]{:S(2)}, u32[]{:S(2)}) collective-permute-start(bf16[576,128]{1,0:T(8,128)(2,1)S(1)} %shard_map.97._), channel_id=1, source_target_pairs={{1,4},{5,8},{9,12},{13,0},{4,1},{8,5},{12,9},{0,13},{3,6},{7,10},{... | collective-permute-start | bytes 442376 | tf_op jit(solution)/shard_map/ppermute | solution.py:293
  61.2 1.7 %collective-permute-done.14.got_x.refs_3_ = bf16[576,128]{1,0:T(8,128)(2,1)S(1)} collective-permute-done((bf16[576,128]{1,0:T(8,128)(2,1)S(1)}, bf16[576,128]{1,0:T(8,128)(2,1)S(1)}, u32[]{:S(2)}, u32[]{:S(2)}) %collective-permute-start.14) | collective-permute-done | bytes 147488 | tf_op jit(solution)/shard_map/ppermute | solution.py:293
  62.8 1.0 %shard_map.101 = (f32[1024,128]{1,0:T(8,128)}, f32[9,128]{1,0:T(8,128)}) custom-call(s32[1]{0:T(128)} %bitcast.parity, bf16[576,128]{1,0:T(8,128)(2,1)S(1)} %collective-permute-done.14.got_x.refs_3_, f32[1024,128]{1,0:T(8,128)S(1)} %shard_map.100.base, bf16[1024,512]{1,0:T(8,128)(2,1)S(1)} %get-tuple-element.60.cross, ...), custom_call_target="tpu_custom_call" | custom-call | tf_op jit(solution)/shard_map/pallas_call | solution.py:31
  (47 shorter events, 16.0 us)
Async XLA Ops:
  2.0 1.1 %copy-start = (bf16[1280,16,16]{0,2,1:T(8,128)(2,1)S(1)}, bf16[1280,16,16]{0,2,1:T(8,128)(2,1)}, u32[]{:S(2)}) copy-start(bf16[1280,16,16]{0,2,1:T(8,128)(2,1)} %param.6) | copy-start | bytes 1966084
  3.1 2.0 %copy-start.1 = (f32[64,16,128]{2,1,0:T(8,128)S(1)}, f32[64,16,128]{2,1,0:T(8,128)}, u32[]{:S(2)}) copy-start(f32[64,16,128]{2,1,0:T(8,128)} %param.5) | copy-start | bytes 1572868
  5.7 10.9 %collective-permute-start = (bf16[528,128]{1,0:T(8,128)(2,1)S(1)}, bf16[528,128]{1,0:T(8,128)(2,1)S(1)}, u32[]{:S(2)}, u32[]{:S(2)}) collective-permute-start(bf16[528,128]{1,0:T(8,128)(2,1)S(1)} %get-tuple-element.54), channel_id=1, source_target_pairs={{1,4},{5,8},{9,12},{13,0},{4,1},{8,5},{12,9},{0,13},{3,6},{7,10},{... | collective-permute-start | bytes 405512 | tf_op jit(solution)/shard_map/ppermute | solution.py:293
  10.3 5.9 %collective-permute-start.1 = (bf16[512,128]{1,0:T(8,128)(2,1)S(1)}, bf16[512,128]{1,0:T(8,128)(2,1)S(1)}, u32[]{:S(2)}, u32[]{:S(2)}) collective-permute-start(bf16[512,128]{1,0:T(8,128)(2,1)S(1)} %get-tuple-element.55._), channel_id=1, source_target_pairs={{0,1},{1,0},{2,3},{3,2},{4,5},{5,4},{6,7},{7,6},{8,9},{9,8},{10,11... | collective-permute-start | bytes 393224 | tf_op jit(solution)/shard_map/ppermute | solution.py:294
  16.7 7.1 %collective-permute-start.2 = (bf16[528,128]{1,0:T(8,128)(2,1)S(1)}, bf16[528,128]{1,0:T(8,128)(2,1)S(1)}, u32[]{:S(2)}, u32[]{:S(2)}) collective-permute-start(bf16[528,128]{1,0:T(8,128)(2,1)S(1)} %shard_map.73._), channel_id=1, source_target_pairs={{1,4},{5,8},{9,12},{13,0},{4,1},{8,5},{12,9},{0,13},{3,6},{7,10},{... | collective-permute-start | bytes 405512 | tf_op jit(solution)/shard_map/ppermute | solution.py:293
  18.3 1.4 %collective-permute-start.3 = (bf16[512,128]{1,0:T(8,128)(2,1)S(1)}, bf16[512,128]{1,0:T(8,128)(2,1)S(1)}, u32[]{:S(2)}, u32[]{:S(2)}) collective-permute-start(bf16[512,128]{1,0:T(8,128)(2,1)S(1)} %get-tuple-element.64), channel_id=1, source_target_pairs={{0,1},{1,0},{2,3},{3,2},{4,5},{5,4},{6,7},{7,6},{8,9},{9,8},{10,11... | collective-permute-start | bytes 393224 | tf_op jit(solution)/shard_map/ppermute | solution.py:294
  23.8 6.3 %collective-permute-start.4 = (bf16[528,128]{1,0:T(8,128)(2,1)S(1)}, bf16[528,128]{1,0:T(8,128)(2,1)S(1)}, u32[]{:S(2)}, u32[]{:S(2)}) collective-permute-start(bf16[528,128]{1,0:T(8,128)(2,1)S(1)} %shard_map.77._), channel_id=1, source_target_pairs={{1,4},{5,8},{9,12},{13,0},{4,1},{8,5},{12,9},{0,13},{3,6},{7,10},{... | collective-permute-start | bytes 405512 | tf_op jit(solution)/shard_map/ppermute | solution.py:293
  25.4 1.4 %collective-permute-start.5 = (bf16[512,128]{1,0:T(8,128)(2,1)S(1)}, bf16[512,128]{1,0:T(8,128)(2,1)S(1)}, u32[]{:S(2)}, u32[]{:S(2)}) collective-permute-start(bf16[512,128]{1,0:T(8,128)(2,1)S(1)} %get-tuple-element.70), channel_id=1, source_target_pairs={{0,1},{1,0},{2,3},{3,2},{4,5},{5,4},{6,7},{7,6},{8,9},{9,8},{10,11... | collective-permute-start | bytes 393224 | tf_op jit(solution)/shard_map/ppermute | solution.py:294
  30.2 6.4 %collective-permute-start.6 = (bf16[528,128]{1,0:T(8,128)(2,1)S(1)}, bf16[528,128]{1,0:T(8,128)(2,1)S(1)}, u32[]{:S(2)}, u32[]{:S(2)}) collective-permute-start(bf16[528,128]{1,0:T(8,128)(2,1)S(1)} %shard_map.81._), channel_id=1, source_target_pairs={{1,4},{5,8},{9,12},{13,0},{4,1},{8,5},{12,9},{0,13},{3,6},{7,10},{... | collective-permute-start | bytes 405512 | tf_op jit(solution)/shard_map/ppermute | solution.py:293
  32.3 1.4 %collective-permute-start.7 = (bf16[512,128]{1,0:T(8,128)(2,1)S(1)}, bf16[512,128]{1,0:T(8,128)(2,1)S(1)}, u32[]{:S(2)}, u32[]{:S(2)}) collective-permute-start(bf16[512,128]{1,0:T(8,128)(2,1)S(1)} %get-tuple-element.76), channel_id=1, source_target_pairs={{0,1},{1,0},{2,3},{3,2},{4,5},{5,4},{6,7},{7,6},{8,9},{9,8},{10,11... | collective-permute-start | bytes 393224 | tf_op jit(solution)/shard_map/ppermute | solution.py:294
  36.6 6.5 %collective-permute-start.8 = (bf16[576,128]{1,0:T(8,128)(2,1)S(1)}, bf16[576,128]{1,0:T(8,128)(2,1)S(1)}, u32[]{:S(2)}, u32[]{:S(2)}) collective-permute-start(bf16[576,128]{1,0:T(8,128)(2,1)S(1)} %shard_map.85._), channel_id=1, source_target_pairs={{1,4},{5,8},{9,12},{13,0},{4,1},{8,5},{12,9},{0,13},{3,6},{7,10},{... | collective-permute-start | bytes 442376 | tf_op jit(solution)/shard_map/ppermute | solution.py:293
  39.0 1.4 %collective-permute-start.9 = (bf16[560,128]{1,0:T(8,128)(2,1)S(1)}, bf16[560,128]{1,0:T(8,128)(2,1)S(1)}, u32[]{:S(2)}, u32[]{:S(2)}) collective-permute-start(bf16[560,128]{1,0:T(8,128)(2,1)S(1)} %get-tuple-element.86), channel_id=1, source_target_pairs={{0,1},{1,0},{2,3},{3,2},{4,5},{5,4},{6,7},{7,6},{8,9},{9,8},{10,11... | collective-permute-start | bytes 430088 | tf_op jit(solution)/shard_map/ppermute | solution.py:294
  43.2 6.5 %collective-permute-start.10 = (bf16[576,128]{1,0:T(8,128)(2,1)S(1)}, bf16[576,128]{1,0:T(8,128)(2,1)S(1)}, u32[]{:S(2)}, u32[]{:S(2)}) collective-permute-start(bf16[576,128]{1,0:T(8,128)(2,1)S(1)} %shard_map.89._), channel_id=1, source_target_pairs={{1,4},{5,8},{9,12},{13,0},{4,1},{8,5},{12,9},{0,13},{3,6},{7,10},{... | collective-permute-start | bytes 442376 | tf_op jit(solution)/shard_map/ppermute | solution.py:293
  45.7 1.4 %collective-permute-start.11 = (bf16[512,128]{1,0:T(8,128)(2,1)S(1)}, bf16[512,128]{1,0:T(8,128)(2,1)S(1)}, u32[]{:S(2)}, u32[]{:S(2)}) collective-permute-start(bf16[512,128]{1,0:T(8,128)(2,1)S(1)} %get-tuple-element.91), channel_id=1, source_target_pairs={{0,1},{1,0},{2,3},{3,2},{4,5},{5,4},{6,7},{7,6},{8,9},{9,8},{10,11... | collective-permute-start | bytes 393224 | tf_op jit(solution)/shard_map/ppermute | solution.py:294
  49.8 6.5 %collective-permute-start.12 = (bf16[576,128]{1,0:T(8,128)(2,1)S(1)}, bf16[576,128]{1,0:T(8,128)(2,1)S(1)}, u32[]{:S(2)}, u32[]{:S(2)}) collective-permute-start(bf16[576,128]{1,0:T(8,128)(2,1)S(1)} %shard_map.93._), channel_id=1, source_target_pairs={{1,4},{5,8},{9,12},{13,0},{4,1},{8,5},{12,9},{0,13},{3,6},{7,10},{... | collective-permute-start | bytes 442376 | tf_op jit(solution)/shard_map/ppermute | solution.py:293
  52.5 1.4 %collective-permute-start.13 = (bf16[560,128]{1,0:T(8,128)(2,1)S(1)}, bf16[560,128]{1,0:T(8,128)(2,1)S(1)}, u32[]{:S(2)}, u32[]{:S(2)}) collective-permute-start(bf16[560,128]{1,0:T(8,128)(2,1)S(1)} %get-tuple-element.96), channel_id=1, source_target_pairs={{0,1},{1,0},{2,3},{3,2},{4,5},{5,4},{6,7},{7,6},{8,9},{9,8},{10,11... | collective-permute-start | bytes 430088 | tf_op jit(solution)/shard_map/ppermute | solution.py:294
  56.4 6.4 %collective-permute-start.14 = (bf16[576,128]{1,0:T(8,128)(2,1)S(1)}, bf16[576,128]{1,0:T(8,128)(2,1)S(1)}, u32[]{:S(2)}, u32[]{:S(2)}) collective-permute-start(bf16[576,128]{1,0:T(8,128)(2,1)S(1)} %shard_map.97._), channel_id=1, source_target_pairs={{1,4},{5,8},{9,12},{13,0},{4,1},{8,5},{12,9},{0,13},{3,6},{7,10},{... | collective-permute-start | bytes 442376 | tf_op jit(solution)/shard_map/ppermute | solution.py:293
  59.3 1.4 %collective-permute-start.15 = (bf16[512,128]{1,0:T(8,128)(2,1)S(1)}, bf16[512,128]{1,0:T(8,128)(2,1)S(1)}, u32[]{:S(2)}, u32[]{:S(2)}) collective-permute-start(bf16[512,128]{1,0:T(8,128)(2,1)S(1)} %get-tuple-element.101), channel_id=1, source_target_pairs={{0,1},{1,0},{2,3},{3,2},{4,5},{5,4},{6,7},{7,6},{8,9},{9,8},{10,11... | collective-permute-start | bytes 393224 | tf_op jit(solution)/shard_map/ppermute | solution.py:294

commit v4 on v3

--- a/solution.py
+++ b/solution.py
@@ -14,12 +14,12 @@
 VMEM = pl.BlockSpec(memory_space=pltpu.VMEM)
 SMEM = pl.BlockSpec(memory_space=pltpu.SMEM)
 NT = (((1,), (1,)), ((), ()))
-UNROLL = 8
 PAD = 8
 ROWS = 16
 TAIL = 3 * ROWS
 LONGER = ROWS
 DOTS = [[(0, n)] + [(m, n) for m in (n - 1, n) if m > 0 and HALF < m + n] for n in range(HALF + 1)]
+DOTS[:2] = [[], DOTS[0] + DOTS[1]]
 
 
 def operands_of(n):
@@ -67,7 +67,7 @@
                 target[i // 2, pl.ds(col + 1, orbits, stride=total + PAD), :] = high
         return 0
 
-    lax.fori_loop(0, total // 4, one, 0, unroll=UNROLL)
+    lax.fori_loop(0, total // 4, one, 0, unroll=total // 4)
 
 
 def gather_rows(source, piece, total, orbitals):
@@ -83,18 +83,21 @@
         crosst_ref[:, at] = gather_rows(cross_f32, p, halo, range(orbits)).astype(BF16)
 
 
-def own_body(atoms, orbits, halo, pair, blocks, crosst, _, own_ref, cross_ref, gram_ref, own_f32, row_hot):
+def own_body(atoms, orbits, halo, pair, blocks, crosst, w, _, own_ref, cross_ref, gram_ref, local_ref, own_f32, row_hot):
     place(atoms, orbits, 0, atoms, pair, blocks, own_f32, row_hot)
+    gram_ref[...] = lax.dot_general(crosst[...], crosst[...], NT, preferred_element_type=F32).astype(BF16)
     lanes = 2 * atoms
     for p in range(orbits // 2):
         at = slice(p * lanes, (p + 1) * lanes)
         cross_ref[at, :] = crosst[:, at].astype(F32).T.astype(BF16)
         turned = gather_rows(own_f32, p, atoms, range(orbits)).T
+        parts = []
         for n in range(orbits // 2):
-            here = slice(n * lanes, (n + 1) * lanes)
             other = gather_rows(own_f32, n, atoms, (2 * p, 2 * p + 1))
-            own_ref[at, here] = (other + turned[:, here]).astype(BF16)
-    gram_ref[...] = jnp.dot(crosst[...], cross_ref[...], preferred_element_type=F32).astype(BF16)
+            parts.append((other + turned[:, n * lanes : (n + 1) * lanes]).astype(BF16))
+        mine = jnp.concatenate(parts, axis=1)
+        own_ref[at, :] = mine
+        local_ref[at, :] = times(mine, w)
 
 
 def put_edge(atoms, halo, w, out):
@@ -143,7 +146,7 @@
 
 def table_of(scale, made, tables):
     dots = dict(zip(DOTS[HALF], made))
-    for table, pairs in zip(tables, DOTS):
+    for table, pairs in zip(tables, DOTS[1:]):
         dots.update({pair: table[n : n + 1, :] for n, pair in enumerate(pairs)})
     rows = [dots[0, n] for n in range(HALF + 1)]
     for n in range(HALF + 1, STEPS + 1):
@@ -254,7 +257,7 @@
     if tail == "start":
         others = operands_of(HALF)[:-1]
         made = dots_of(HALF, refs[: len(others)] + (v_ref,))
-        table = table_of(scale, made, refs[len(others) : len(others) + HALF])
+        table = table_of(scale, made, refs[len(others) : len(others) + HALF - 1])
         outs[3][...] = table
         if ride:
             put_table(table, out, edge_size)
@@ -335,22 +338,21 @@
                 table = made[3]
         got_i = inside(send_i)
         if k == 0:
-            own, cross, gram = call(
+            own, cross, gram, local = call(
                 functools.partial(own_body, *dims),
-                (((size, size), BF16), ((size, edge_size), BF16), ((edge_size, edge_size), BF16)),
-                pair, flat, crosst, send_i,
+                (((size, size), BF16), ((size, edge_size), BF16), ((edge_size, edge_size), BF16), whole),
+                pair, flat, crosst, w, send_i,
                 scratch=[pltpu.VMEM((orbits // 2, orbits * (atoms + PAD), 2 * atoms), F32), row_hot],
                 limit=24,
             )
-        dots = ()
-        if k < HALF:
-            dots = (((len(DOTS[k]), width), F32),)
-        made = call(
-            functools.partial(local_body, k),
-            (whole,) + dots,
-            own, w, *((vectors[m] for m in operands_of(k)) if k < HALF else ()),
-        )
-        local, tables = made[0], tables + list(made[1:])
+        else:
+            dots = (((len(DOTS[k]), width), F32),) if k < HALF else ()
+            local, *made = call(
+                functools.partial(local_body, k),
+                (whole,) + dots,
+                own, w, *((vectors[m] for m in operands_of(k)) if k < HALF else ()),
+            )
+            tables = tables + made
         base, *pre = call(
             functools.partial(before_body, *dims, k),
             (whole, ((edge_size, width), F32))[: 2 - (k == STEPS - 1)],

time: 64.1 us -> 62.9 us (0.981)
  Pallas kernels: 22.2 us -> 20.8 us
  waiting for transfers between devices: 21.5 us -> 22.2 us
    pallas_call x34 -> x33, Pallas kernels: 22.2 us -> 20.8 us  [call(): pl.pallas_call(body, out_shape=tuple((jax.ShapeDtypeStruct(s, t) for s, t...]
    ppermute x8, waiting for transfers between devices: 17.1 us -> 17.8 us  [per_device(): across = lambda x: lax.ppermute(x, RING, between)]
  transfers between devices with their start and end apart: 16 -> 16, of which waited for: 14 -> 14; matrix products, arithmetic and copies ran while one was open for 0% -> 0% of each run, Pallas kernels for 29% -> 27%
where the time goes in v4:
time: 62.9 us; the launch traced here: 62.7 us
  waiting for transfers between devices  22.2 us (35%)
  Pallas kernels  20.8 us (33%)
  starting transfers between devices  16.2 us (26%)
  between operations  1.59 us (3%)
  local copies, waits for them, and re-layouts  1.09 us (2%)
  other arithmetic  0.72 us (1%)
    pallas_call x33, Pallas kernels, call(): pl.pallas_call(body, out_shape=tuple((jax.ShapeDtypeStruct(s, t) for s, t...  20.8 us
    ppermute x8, waiting for transfers between devices, per_device(): across = lambda x: lax.ppermute(x, RING, between)  17.8 us
    ppermute x8, starting transfers between devices, per_device(): across = lambda x: lax.ppermute(x, RING, between)  15.7 us
    ppermute x8, waiting for transfers between devices, per_device(): inside = lambda x: lax.ppermute(x, 'orb', [(0, 1), (1, 0)])  4.36 us
  transfers between devices with their start and end apart: 16, of which 14 were waited for; matrix products, arithmetic and copies ran while one was open for 0% of the time, Pallas kernels for 27%

profile of v4, /device:TPU:0, one launch (start us, length us, event | category | flops | bytes accessed | tf_op | source)
XLA Modules:
  0.0 62.7 jit_solution(15177904644599321938)
XLA Ops:
  1.3 0.7 %add_select_fusion.pair = s32[1280]{0:T(1024)S(1)} fusion(s32[1280]{0:T(1024)} %param.7, s32[1280]{0:T(1024)} %param.8, s32[]{:T(128)} %bitcast.7), kind=kLoop, calls=%fused_computation | loop fusion | flops 5120 | bytes 15364 | tf_op jit(solution)/shard_map/jit(_where)/select_n | solution.py:300
  2.0 1.1 %copy-done = bf16[1280,16,16]{0,2,1:T(8,128)(2,1)S(1)} copy-done((bf16[1280,16,16]{0,2,1:T(8,128)(2,1)S(1)}, bf16[1280,16,16]{0,2,1:T(8,128)(2,1)}, u32[]{:S(2)}) %copy-start) | copy-done | bytes 655384
  3.1 2.0 %shard_map.68.crosst = bf16[512,1024]{1,0:T(8,128)(2,1)S(1)} custom-call(s32[1280]{0:T(1024)S(1)} %add_select_fusion.pair, bf16[256,1280]{1,0:T(8,128)(2,1)S(1)} %bitcast.8), custom_call_target="tpu_custom_call" | custom-call | flops 1342177280 | bytes 660480 | tf_op jit(solution)/shard_map/pallas_call | solution.py:31
  5.7 4.6 %collective-permute-start = (bf16[528,128]{1,0:T(8,128)(2,1)S(1)}, bf16[528,128]{1,0:T(8,128)(2,1)S(1)}, u32[]{:S(2)}, u32[]{:S(2)}) collective-permute-start(bf16[528,128]{1,0:T(8,128)(2,1)S(1)} %get-tuple-element.53), channel_id=1, source_target_pairs={{1,4},{5,8},{9,12},{13,0},{4,1},{8,5},{12,9},{0,13},{3,6},{7,10},{... | collective-permute-start | bytes 405512 | tf_op jit(solution)/shard_map/ppermute | solution.py:296
  10.3 4.5 %shard_map.70 = (bf16[1024,1024]{1,0:T(8,128)(2,1)S(1)}, bf16[1024,512]{1,0:T(8,128)(2,1)S(1)}, bf16[512,512]{1,0:T(8,128)(2,1)S(1)}, f32[1024,128]{1,0:T(8,128)S(1)}) custom-call(s32[1280]{0:T(1024)S(1)} %add_select_fusion.pair, bf16[256,1280]{1,0:T(8,128)(2,1)S(1)} %bitcast.9, bf16[512,1024]{1,0:T(8,128)(2,1)S(1)} %shard_map.68.crosst, ...), custom_call_target="tpu_custom_call" | custom-call | tf_op jit(solution)/shard_map/pallas_call | solution.py:31
  15.3 1.5 %collective-permute-start.2 = (bf16[528,128]{1,0:T(8,128)(2,1)S(1)}, bf16[528,128]{1,0:T(8,128)(2,1)S(1)}, u32[]{:S(2)}, u32[]{:S(2)}) collective-permute-start(bf16[528,128]{1,0:T(8,128)(2,1)S(1)} %shard_map.72._), channel_id=1, source_target_pairs={{1,4},{5,8},{9,12},{13,0},{4,1},{8,5},{12,9},{0,13},{3,6},{7,10},{... | collective-permute-start | bytes 405512 | tf_op jit(solution)/shard_map/ppermute | solution.py:296
  17.5 0.7 %shard_map.74 = (f32[1024,128]{1,0:T(8,128)S(1)}, f32[2,128]{1,0:T(2,128)S(1)}) custom-call(bf16[1024,1024]{1,0:T(8,128)(2,1)S(1)} %get-tuple-element.63.own, bf16[1024,128]{1,0:T(8,128)(2,1)S(1)} %get-tuple-element.64.w, f32[1024,128]{1,0:T(8,128)S(1)} %get-tuple-element.57.previous.refs_0_, f32[1024,128]{1,0:T(8,128)S(1)} %get-tuple-element.65.refs_1_.previous), custom_call_target="tpu_custom_call" | custom-call | tf_op jit(solution)/shard_map/pallas_call | solution.py:31
  19.2 3.2 %collective-permute-done.2.got_x = bf16[528,128]{1,0:T(8,128)(2,1)S(1)} collective-permute-done((bf16[528,128]{1,0:T(8,128)(2,1)S(1)}, bf16[528,128]{1,0:T(8,128)(2,1)S(1)}, u32[]{:S(2)}, u32[]{:S(2)}) %collective-permute-start.2) | collective-permute-done | bytes 135200 | tf_op jit(solution)/shard_map/ppermute | solution.py:296
  22.5 1.1 %collective-permute-start.4 = (bf16[528,128]{1,0:T(8,128)(2,1)S(1)}, bf16[528,128]{1,0:T(8,128)(2,1)S(1)}, u32[]{:S(2)}, u32[]{:S(2)}) collective-permute-start(bf16[528,128]{1,0:T(8,128)(2,1)S(1)} %shard_map.76._), channel_id=1, source_target_pairs={{1,4},{5,8},{9,12},{13,0},{4,1},{8,5},{12,9},{0,13},{3,6},{7,10},{... | collective-permute-start | bytes 405512 | tf_op jit(solution)/shard_map/ppermute | solution.py:296
  24.2 0.7 %shard_map.78 = (f32[1024,128]{1,0:T(8,128)S(1)}, f32[1,128]{1,0:T(1,128)S(1)}) custom-call(bf16[1024,1024]{1,0:T(8,128)(2,1)S(1)} %get-tuple-element.63.own, bf16[1024,128]{1,0:T(8,128)(2,1)S(1)} %get-tuple-element.70.w, f32[1024,128]{1,0:T(8,128)S(1)} %get-tuple-element.57.previous.refs_0_, f32[1024,128]{1,0:T(8,128)S(1)} %get-tuple-element.71.refs_1_.previous), custom_call_target="tpu_custom_call" | custom-call | tf_op jit(solution)/shard_map/pallas_call | solution.py:31
  25.9 2.8 %collective-permute-done.4.got_x = bf16[528,128]{1,0:T(8,128)(2,1)S(1)} collective-permute-done((bf16[528,128]{1,0:T(8,128)(2,1)S(1)}, bf16[528,128]{1,0:T(8,128)(2,1)S(1)}, u32[]{:S(2)}, u32[]{:S(2)}) %collective-permute-start.4) | collective-permute-done | bytes 135200 | tf_op jit(solution)/shard_map/ppermute | solution.py:296
  29.0 1.2 %collective-permute-start.6 = (bf16[528,128]{1,0:T(8,128)(2,1)S(1)}, bf16[528,128]{1,0:T(8,128)(2,1)S(1)}, u32[]{:S(2)}, u32[]{:S(2)}) collective-permute-start(bf16[528,128]{1,0:T(8,128)(2,1)S(1)} %shard_map.80._), channel_id=1, source_target_pairs={{1,4},{5,8},{9,12},{13,0},{4,1},{8,5},{12,9},{0,13},{3,6},{7,10},{... | collective-permute-start | bytes 405512 | tf_op jit(solution)/shard_map/ppermute | solution.py:296
  30.8 0.7 %shard_map.82 = (f32[1024,128]{1,0:T(8,128)S(1)}, f32[3,128]{1,0:T(4,128)S(1)}) custom-call(bf16[1024,1024]{1,0:T(8,128)(2,1)S(1)} %get-tuple-element.63.own, bf16[1024,128]{1,0:T(8,128)(2,1)S(1)} %get-tuple-element.76.w, f32[1024,128]{1,0:T(8,128)S(1)} %get-tuple-element.57.previous.refs_0_, f32[1024,128]{1,0:T(8,128)S(1)} %get-tuple-element.71.refs_1_.previous, ...), custom_call_target="tpu_custom_call" | custom-call | tf_op jit(solution)/shard_map/pallas_call | solution.py:31
  32.6 2.8 %collective-permute-done.6.got_x = bf16[528,128]{1,0:T(8,128)(2,1)S(1)} collective-permute-done((bf16[528,128]{1,0:T(8,128)(2,1)S(1)}, bf16[528,128]{1,0:T(8,128)(2,1)S(1)}, u32[]{:S(2)}, u32[]{:S(2)}) %collective-permute-start.6) | collective-permute-done | bytes 135200 | tf_op jit(solution)/shard_map/ppermute | solution.py:296
  35.5 1.5 %collective-permute-start.8 = (bf16[576,128]{1,0:T(8,128)(2,1)S(1)}, bf16[576,128]{1,0:T(8,128)(2,1)S(1)}, u32[]{:S(2)}, u32[]{:S(2)}) collective-permute-start(bf16[576,128]{1,0:T(8,128)(2,1)S(1)} %shard_map.84._), channel_id=1, source_target_pairs={{1,4},{5,8},{9,12},{13,0},{4,1},{8,5},{12,9},{0,13},{3,6},{7,10},{... | collective-permute-start | bytes 442376 | tf_op jit(solution)/shard_map/ppermute | solution.py:296
  36.9 0.7 %shard_map.85 = (f32[1024,128]{1,0:T(8,128)S(1)}, bf16[1024,128]{1,0:T(8,128)(2,1)S(1)}, bf16[560,128]{1,0:T(8,128)(2,1)S(1)}, f32[16,128]{1,0:T(8,128)S(1)}) custom-call(s32[1]{0:T(128)} %bitcast.parity, bf16[528,128]{1,0:T(8,128)(2,1)S(1)} %collective-permute-done.6.got_x, f32[1024,128]{1,0:T(8,128)S(1)} %get-tuple-element.80.base, ...), custom_call_target="tpu_custom_call" | custom-call | tf_op jit(solution)/shard_map/pallas_call | solution.py:31
  39.5 2.5 %collective-permute-done.8.got_x = bf16[576,128]{1,0:T(8,128)(2,1)S(1)} collective-permute-done((bf16[576,128]{1,0:T(8,128)(2,1)S(1)}, bf16[576,128]{1,0:T(8,128)(2,1)S(1)}, u32[]{:S(2)}, u32[]{:S(2)}) %collective-permute-start.8) | collective-permute-done | bytes 147488 | tf_op jit(solution)/shard_map/ppermute | solution.py:296
  42.0 1.7 %collective-permute-start.10 = (bf16[576,128]{1,0:T(8,128)(2,1)S(1)}, bf16[576,128]{1,0:T(8,128)(2,1)S(1)}, u32[]{:S(2)}, u32[]{:S(2)}) collective-permute-start(bf16[576,128]{1,0:T(8,128)(2,1)S(1)} %shard_map.88._), channel_id=1, source_target_pairs={{1,4},{5,8},{9,12},{13,0},{4,1},{8,5},{12,9},{0,13},{3,6},{7,10},{... | collective-permute-start | bytes 442376 | tf_op jit(solution)/shard_map/ppermute | solution.py:296
  46.1 2.5 %collective-permute-done.10.got_x.refs_1_ = bf16[576,128]{1,0:T(8,128)(2,1)S(1)} collective-permute-done((bf16[576,128]{1,0:T(8,128)(2,1)S(1)}, bf16[576,128]{1,0:T(8,128)(2,1)S(1)}, u32[]{:S(2)}, u32[]{:S(2)}) %collective-permute-start.10) | collective-permute-done | bytes 147488 | tf_op jit(solution)/shard_map/ppermute | solution.py:296
  48.6 2.0 %collective-permute-start.12 = (bf16[576,128]{1,0:T(8,128)(2,1)S(1)}, bf16[576,128]{1,0:T(8,128)(2,1)S(1)}, u32[]{:S(2)}, u32[]{:S(2)}) collective-permute-start(bf16[576,128]{1,0:T(8,128)(2,1)S(1)} %shard_map.92._), channel_id=1, source_target_pairs={{1,4},{5,8},{9,12},{13,0},{4,1},{8,5},{12,9},{0,13},{3,6},{7,10},{... | collective-permute-start | bytes 442376 | tf_op jit(solution)/shard_map/ppermute | solution.py:296
  53.0 2.2 %collective-permute-done.12.got_x = bf16[576,128]{1,0:T(8,128)(2,1)S(1)} collective-permute-done((bf16[576,128]{1,0:T(8,128)(2,1)S(1)}, bf16[576,128]{1,0:T(8,128)(2,1)S(1)}, u32[]{:S(2)}, u32[]{:S(2)}) %collective-permute-start.12) | collective-permute-done | bytes 147488 | tf_op jit(solution)/shard_map/ppermute | solution.py:296
  55.2 2.2 %collective-permute-start.14 = (bf16[576,128]{1,0:T(8,128)(2,1)S(1)}, bf16[576,128]{1,0:T(8,128)(2,1)S(1)}, u32[]{:S(2)}, u32[]{:S(2)}) collective-permute-start(bf16[576,128]{1,0:T(8,128)(2,1)S(1)} %shard_map.96._), channel_id=1, source_target_pairs={{1,4},{5,8},{9,12},{13,0},{4,1},{8,5},{12,9},{0,13},{3,6},{7,10},{... | collective-permute-start | bytes 442376 | tf_op jit(solution)/shard_map/ppermute | solution.py:296
  59.8 1.9 %collective-permute-done.14.got_x.refs_3_ = bf16[576,128]{1,0:T(8,128)(2,1)S(1)} collective-permute-done((bf16[576,128]{1,0:T(8,128)(2,1)S(1)}, bf16[576,128]{1,0:T(8,128)(2,1)S(1)}, u32[]{:S(2)}, u32[]{:S(2)}) %collective-permute-start.14) | collective-permute-done | bytes 147488 | tf_op jit(solution)/shard_map/ppermute | solution.py:296
  61.6 1.0 %shard_map.100 = (f32[1024,128]{1,0:T(8,128)}, f32[9,128]{1,0:T(8,128)}) custom-call(s32[1]{0:T(128)} %bitcast.parity, bf16[576,128]{1,0:T(8,128)(2,1)S(1)} %collective-permute-done.14.got_x.refs_3_, f32[1024,128]{1,0:T(8,128)S(1)} %shard_map.99.base, bf16[1024,512]{1,0:T(8,128)(2,1)S(1)} %get-tuple-element.58.cross, ...), custom_call_target="tpu_custom_call" | custom-call | tf_op jit(solution)/shard_map/pallas_call | solution.py:31
  (46 shorter events, 15.3 us)
Async XLA Ops:
  2.0 1.1 %copy-start = (bf16[1280,16,16]{0,2,1:T(8,128)(2,1)S(1)}, bf16[1280,16,16]{0,2,1:T(8,128)(2,1)}, u32[]{:S(2)}) copy-start(bf16[1280,16,16]{0,2,1:T(8,128)(2,1)} %param.6) | copy-start | bytes 1966084
  3.1 2.0 %copy-start.1 = (f32[64,16,128]{2,1,0:T(8,128)S(1)}, f32[64,16,128]{2,1,0:T(8,128)}, u32[]{:S(2)}) copy-start(f32[64,16,128]{2,1,0:T(8,128)} %param.5) | copy-start | bytes 1572868
  5.7 9.6 %collective-permute-start = (bf16[528,128]{1,0:T(8,128)(2,1)S(1)}, bf16[528,128]{1,0:T(8,128)(2,1)S(1)}, u32[]{:S(2)}, u32[]{:S(2)}) collective-permute-start(bf16[528,128]{1,0:T(8,128)(2,1)S(1)} %get-tuple-element.53), channel_id=1, source_target_pairs={{1,4},{5,8},{9,12},{13,0},{4,1},{8,5},{12,9},{0,13},{3,6},{7,10},{... | collective-permute-start | bytes 405512 | tf_op jit(solution)/shard_map/ppermute | solution.py:296
  10.3 4.6 %collective-permute-start.1 = (bf16[512,128]{1,0:T(8,128)(2,1)S(1)}, bf16[512,128]{1,0:T(8,128)(2,1)S(1)}, u32[]{:S(2)}, u32[]{:S(2)}) collective-permute-start(bf16[512,128]{1,0:T(8,128)(2,1)S(1)} %get-tuple-element.54._), channel_id=1, source_target_pairs={{0,1},{1,0},{2,3},{3,2},{4,5},{5,4},{6,7},{7,6},{8,9},{9,8},{10,11... | collective-permute-start | bytes 393224 | tf_op jit(solution)/shard_map/ppermute | solution.py:297
  15.3 7.1 %collective-permute-start.2 = (bf16[528,128]{1,0:T(8,128)(2,1)S(1)}, bf16[528,128]{1,0:T(8,128)(2,1)S(1)}, u32[]{:S(2)}, u32[]{:S(2)}) collective-permute-start(bf16[528,128]{1,0:T(8,128)(2,1)S(1)} %shard_map.72._), channel_id=1, source_target_pairs={{1,4},{5,8},{9,12},{13,0},{4,1},{8,5},{12,9},{0,13},{3,6},{7,10},{... | collective-permute-start | bytes 405512 | tf_op jit(solution)/shard_map/ppermute | solution.py:296
  17.4 1.4 %collective-permute-start.3 = (bf16[512,128]{1,0:T(8,128)(2,1)S(1)}, bf16[512,128]{1,0:T(8,128)(2,1)S(1)}, u32[]{:S(2)}, u32[]{:S(2)}) collective-permute-start(bf16[512,128]{1,0:T(8,128)(2,1)S(1)} %get-tuple-element.62), channel_id=1, source_target_pairs={{0,1},{1,0},{2,3},{3,2},{4,5},{5,4},{6,7},{7,6},{8,9},{9,8},{10,11... | collective-permute-start | bytes 393224 | tf_op jit(solution)/shard_map/ppermute | solution.py:297
  22.5 6.3 %collective-permute-start.4 = (bf16[528,128]{1,0:T(8,128)(2,1)S(1)}, bf16[528,128]{1,0:T(8,128)(2,1)S(1)}, u32[]{:S(2)}, u32[]{:S(2)}) collective-permute-start(bf16[528,128]{1,0:T(8,128)(2,1)S(1)} %shard_map.76._), channel_id=1, source_target_pairs={{1,4},{5,8},{9,12},{13,0},{4,1},{8,5},{12,9},{0,13},{3,6},{7,10},{... | collective-permute-start | bytes 405512 | tf_op jit(solution)/shard_map/ppermute | solution.py:296
  24.1 1.4 %collective-permute-start.5 = (bf16[512,128]{1,0:T(8,128)(2,1)S(1)}, bf16[512,128]{1,0:T(8,128)(2,1)S(1)}, u32[]{:S(2)}, u32[]{:S(2)}) collective-permute-start(bf16[512,128]{1,0:T(8,128)(2,1)S(1)} %get-tuple-element.69), channel_id=1, source_target_pairs={{0,1},{1,0},{2,3},{3,2},{4,5},{5,4},{6,7},{7,6},{8,9},{9,8},{10,11... | collective-permute-start | bytes 393224 | tf_op jit(solution)/shard_map/ppermute | solution.py:297
  29.0 6.4 %collective-permute-start.6 = (bf16[528,128]{1,0:T(8,128)(2,1)S(1)}, bf16[528,128]{1,0:T(8,128)(2,1)S(1)}, u32[]{:S(2)}, u32[]{:S(2)}) collective-permute-start(bf16[528,128]{1,0:T(8,128)(2,1)S(1)} %shard_map.80._), channel_id=1, source_target_pairs={{1,4},{5,8},{9,12},{13,0},{4,1},{8,5},{12,9},{0,13},{3,6},{7,10},{... | collective-permute-start | bytes 405512 | tf_op jit(solution)/shard_map/ppermute | solution.py:296
  30.7 1.4 %collective-permute-start.7 = (bf16[512,128]{1,0:T(8,128)(2,1)S(1)}, bf16[512,128]{1,0:T(8,128)(2,1)S(1)}, u32[]{:S(2)}, u32[]{:S(2)}) collective-permute-start(bf16[512,128]{1,0:T(8,128)(2,1)S(1)} %get-tuple-element.75), channel_id=1, source_target_pairs={{0,1},{1,0},{2,3},{3,2},{4,5},{5,4},{6,7},{7,6},{8,9},{9,8},{10,11... | collective-permute-start | bytes 393224 | tf_op jit(solution)/shard_map/ppermute | solution.py:297
  35.5 6.5 %collective-permute-start.8 = (bf16[576,128]{1,0:T(8,128)(2,1)S(1)}, bf16[576,128]{1,0:T(8,128)(2,1)S(1)}, u32[]{:S(2)}, u32[]{:S(2)}) collective-permute-start(bf16[576,128]{1,0:T(8,128)(2,1)S(1)} %shard_map.84._), channel_id=1, source_target_pairs={{1,4},{5,8},{9,12},{13,0},{4,1},{8,5},{12,9},{0,13},{3,6},{7,10},{... | collective-permute-start | bytes 442376 | tf_op jit(solution)/shard_map/ppermute | solution.py:296
  37.6 1.4 %collective-permute-start.9 = (bf16[560,128]{1,0:T(8,128)(2,1)S(1)}, bf16[560,128]{1,0:T(8,128)(2,1)S(1)}, u32[]{:S(2)}, u32[]{:S(2)}) collective-permute-start(bf16[560,128]{1,0:T(8,128)(2,1)S(1)} %get-tuple-element.84), channel_id=1, source_target_pairs={{0,1},{1,0},{2,3},{3,2},{4,5},{5,4},{6,7},{7,6},{8,9},{9,8},{10,11... | collective-permute-start | bytes 430088 | tf_op jit(solution)/shard_map/ppermute | solution.py:297
  42.0 6.5 %collective-permute-start.10 = (bf16[576,128]{1,0:T(8,128)(2,1)S(1)}, bf16[576,128]{1,0:T(8,128)(2,1)S(1)}, u32[]{:S(2)}, u32[]{:S(2)}) collective-permute-start(bf16[576,128]{1,0:T(8,128)(2,1)S(1)} %shard_map.88._), channel_id=1, source_target_pairs={{1,4},{5,8},{9,12},{13,0},{4,1},{8,5},{12,9},{0,13},{3,6},{7,10},{... | collective-permute-start | bytes 442376 | tf_op jit(solution)/shard_map/ppermute | solution.py:296
  44.3 1.4 %collective-permute-start.11 = (bf16[512,128]{1,0:T(8,128)(2,1)S(1)}, bf16[512,128]{1,0:T(8,128)(2,1)S(1)}, u32[]{:S(2)}, u32[]{:S(2)}) collective-permute-start(bf16[512,128]{1,0:T(8,128)(2,1)S(1)} %get-tuple-element.89), channel_id=1, source_target_pairs={{0,1},{1,0},{2,3},{3,2},{4,5},{5,4},{6,7},{7,6},{8,9},{9,8},{10,11... | collective-permute-start | bytes 393224 | tf_op jit(solution)/shard_map/ppermute | solution.py:297
  48.6 6.5 %collective-permute-start.12 = (bf16[576,128]{1,0:T(8,128)(2,1)S(1)}, bf16[576,128]{1,0:T(8,128)(2,1)S(1)}, u32[]{:S(2)}, u32[]{:S(2)}) collective-permute-start(bf16[576,128]{1,0:T(8,128)(2,1)S(1)} %shard_map.92._), channel_id=1, source_target_pairs={{1,4},{5,8},{9,12},{13,0},{4,1},{8,5},{12,9},{0,13},{3,6},{7,10},{... | collective-permute-start | bytes 442376 | tf_op jit(solution)/shard_map/ppermute | solution.py:296
  51.1 1.4 %collective-permute-start.13 = (bf16[560,128]{1,0:T(8,128)(2,1)S(1)}, bf16[560,128]{1,0:T(8,128)(2,1)S(1)}, u32[]{:S(2)}, u32[]{:S(2)}) collective-permute-start(bf16[560,128]{1,0:T(8,128)(2,1)S(1)} %get-tuple-element.94), channel_id=1, source_target_pairs={{0,1},{1,0},{2,3},{3,2},{4,5},{5,4},{6,7},{7,6},{8,9},{9,8},{10,11... | collective-permute-start | bytes 430088 | tf_op jit(solution)/shard_map/ppermute | solution.py:297
  55.2 6.4 %collective-permute-start.14 = (bf16[576,128]{1,0:T(8,128)(2,1)S(1)}, bf16[576,128]{1,0:T(8,128)(2,1)S(1)}, u32[]{:S(2)}, u32[]{:S(2)}) collective-permute-start(bf16[576,128]{1,0:T(8,128)(2,1)S(1)} %shard_map.96._), channel_id=1, source_target_pairs={{1,4},{5,8},{9,12},{13,0},{4,1},{8,5},{12,9},{0,13},{3,6},{7,10},{... | collective-permute-start | bytes 442376 | tf_op jit(solution)/shard_map/ppermute | solution.py:296
  57.9 1.4 %collective-permute-start.15 = (bf16[512,128]{1,0:T(8,128)(2,1)S(1)}, bf16[512,128]{1,0:T(8,128)(2,1)S(1)}, u32[]{:S(2)}, u32[]{:S(2)}) collective-permute-start(bf16[512,128]{1,0:T(8,128)(2,1)S(1)} %get-tuple-element.99), channel_id=1, source_target_pairs={{0,1},{1,0},{2,3},{3,2},{4,5},{5,4},{6,7},{7,6},{8,9},{9,8},{10,11... | collective-permute-start | bytes 393224 | tf_op jit(solution)/shard_map/ppermute | solution.py:297

commit v5 on v4

--- a/solution.py
+++ b/solution.py
@@ -14,6 +14,7 @@
 VMEM = pl.BlockSpec(memory_space=pltpu.VMEM)
 SMEM = pl.BlockSpec(memory_space=pltpu.SMEM)
 NT = (((1,), (1,)), ((), ()))
+AHEAD = 1_000_000_000
 PAD = 8
 ROWS = 16
 TAIL = 3 * ROWS
@@ -39,12 +40,17 @@
     )(*operands)
 
 
-def place(atoms, orbits, first, total, pair, blocks, target, row_hot):
-    slots = blocks.shape[1]
+def hot_body(atoms, pair, row_hot, col_ref):
+    slots = pair.shape[0]
     pair_id = pair[...].reshape(1, slots)
     col_id = lax.div(pair_id, atoms)
     row_id = pair_id - col_id * atoms
     row_hot[...] = jnp.where(lax.broadcasted_iota(jnp.int32, (atoms, slots), 0) == row_id, 1.0, 0.0).astype(BF16)
+    col_ref[...] = col_id
+
+
+def place(atoms, orbits, first, total, row_hot, cols, blocks, target):
+    col_id = cols[...]
     lanes = 2 * atoms
     lane = lax.broadcasted_iota(jnp.int32, (orbits, lanes), 1)
 
@@ -75,16 +81,16 @@
     return jnp.concatenate([source[piece, start : start + total, :] for start in starts], axis=0)
 
 
-def cross_body(atoms, orbits, halo, pair, blocks, crosst_ref, cross_f32, row_hot):
-    place(atoms, orbits, atoms, halo, pair, blocks, cross_f32, row_hot)
+def cross_body(atoms, orbits, halo, row_hot, cols, blocks, crosst_ref, cross_f32):
+    place(atoms, orbits, atoms, halo, row_hot, cols, blocks, cross_f32)
     lanes = 2 * atoms
     for p in range(orbits // 2):
         at = slice(p * lanes, (p + 1) * lanes)
         crosst_ref[:, at] = gather_rows(cross_f32, p, halo, range(orbits)).astype(BF16)
 
 
-def own_body(atoms, orbits, halo, pair, blocks, crosst, w, _, own_ref, cross_ref, gram_ref, local_ref, own_f32, row_hot):
-    place(atoms, orbits, 0, atoms, pair, blocks, own_f32, row_hot)
+def own_body(atoms, orbits, halo, row_hot, cols, blocks, crosst, w, _, own_ref, cross_ref, gram_ref, local_ref, own_f32):
+    place(atoms, orbits, 0, atoms, row_hot, cols, blocks, own_f32)
     gram_ref[...] = lax.dot_general(crosst[...], crosst[...], NT, preferred_element_type=F32).astype(BF16)
     lanes = 2 * atoms
     for p in range(orbits // 2):
@@ -299,13 +305,18 @@
     slot = jnp.arange(slots, dtype=jnp.int32)
     pair = jnp.where(slot < counts[0], block_cols * atoms + block_rows, -atoms)
     flat = blocks.transpose(1, 2, 0).reshape(orbits * orbits, slots)
-    row_hot = pltpu.VMEM((atoms, slots), BF16)
+    row_hot, cols = call(
+        functools.partial(hot_body, atoms),
+        (((atoms, slots), BF16), ((1, slots), jnp.int32)),
+        pair,
+        flops=AHEAD,
+    )
     (crosst,) = call(
         functools.partial(cross_body, *dims),
         (((edge_size, size), BF16),),
-        pair, flat,
+        row_hot, cols, flat,
         flops=2 * orbits * orbits * slots * atoms * halo,
-        scratch=[pltpu.VMEM((orbits // 2, orbits * (halo + PAD), 2 * atoms), F32), row_hot],
+        scratch=[pltpu.VMEM((orbits // 2, orbits * (halo + PAD), 2 * atoms), F32)],
         limit=24,
     )
     whole, rounded, message = ((size, width), F32), ((size, width), BF16), ((edge_size, width), BF16)
@@ -341,8 +352,8 @@
             own, cross, gram, local = call(
                 functools.partial(own_body, *dims),
                 (((size, size), BF16), ((size, edge_size), BF16), ((edge_size, edge_size), BF16), whole),
-                pair, flat, crosst, w, send_i,
-                scratch=[pltpu.VMEM((orbits // 2, orbits * (atoms + PAD), 2 * atoms), F32), row_hot],
+                row_hot, cols, flat, crosst, w, send_i,
+                scratch=[pltpu.VMEM((orbits // 2, orbits * (atoms + PAD), 2 * atoms), F32)],
                 limit=24,
             )
         else:

time: 62.9 us -> 61.9 us (0.984)
  local copies, waits for them, and re-layouts: 1.09 us -> 0.01 us
    unnamed x4, local copies, waits for them, and re-layouts: 1.09 us -> 0.01 us
    pallas_call x33 -> x34, Pallas kernels: 20.8 us -> 20.8 us  [call(): pl.pallas_call(body, out_shape=tuple((jax.ShapeDtypeStruct(s, t) for s, t...]
where the time goes in v5:
time: 61.9 us; the launch traced here: 61.6 us
  waiting for transfers between devices  22.2 us (36%)
  Pallas kernels  20.8 us (34%)
  starting transfers between devices  16.3 us (26%)
  between operations  1.68 us (3%)
  other arithmetic  0.72 us (1%)
    pallas_call x34, Pallas kernels, call(): pl.pallas_call(body, out_shape=tuple((jax.ShapeDtypeStruct(s, t) for s, t...  20.8 us
    ppermute x8, waiting for transfers between devices, per_device(): across = lambda x: lax.ppermute(x, RING, between)  17.8 us
    ppermute x8, starting transfers between devices, per_device(): across = lambda x: lax.ppermute(x, RING, between)  15.8 us
    ppermute x8, waiting for transfers between devices, per_device(): inside = lambda x: lax.ppermute(x, 'orb', [(0, 1), (1, 0)])  4.36 us
  transfers between devices with their start and end apart: 16, of which 14 were waited for; matrix products, arithmetic and copies ran while one was open for 0% of the time, Pallas kernels for 27%

profile of v5, /device:TPU:0, one launch (start us, length us, event | category | flops | bytes accessed | tf_op | source)
XLA Modules:
  0.0 61.6 jit_solution(1485381136226666736)
XLA Ops:
  1.4 0.7 %add_select_fusion.pair = s32[1280]{0:T(1024)S(1)} fusion(s32[1280]{0:T(1024)} %param.7, s32[1280]{0:T(1024)} %param.8, s32[]{:T(128)} %bitcast.7), kind=kLoop, calls=%fused_computation | loop fusion | flops 5120 | bytes 15364 | tf_op jit(solution)/shard_map/jit(_where)/select_n | solution.py:306
  2.1 1.9 %shard_map.69.crosst = bf16[512,1024]{1,0:T(8,128)(2,1)S(1)} custom-call(bf16[64,1280]{1,0:T(8,128)(2,1)S(1)} %get-tuple-element.55.row_hot, s32[1,1280]{1,0:T(1,128)S(1)} %get-tuple-element.56.cols, bf16[256,1280]{1,0:T(8,128)(2,1)S(1)} %bitcast.8), custom_call_target="tpu_custom_call" | custom-call | flops 1342177280 | bytes 824320 | tf_op jit(solution)/shard_map/pallas_call | solution.py:32
  4.7 4.6 %collective-permute-start = (bf16[528,128]{1,0:T(8,128)(2,1)S(1)}, bf16[528,128]{1,0:T(8,128)(2,1)S(1)}, u32[]{:S(2)}, u32[]{:S(2)}) collective-permute-start(bf16[528,128]{1,0:T(8,128)(2,1)S(1)} %get-tuple-element.57), channel_id=1, source_target_pairs={{1,4},{5,8},{9,12},{13,0},{4,1},{8,5},{12,9},{0,13},{3,6},{7,10},{... | collective-permute-start | bytes 405512 | tf_op jit(solution)/shard_map/ppermute | solution.py:302
  9.3 4.5 %shard_map.71 = (bf16[1024,1024]{1,0:T(8,128)(2,1)S(1)}, bf16[1024,512]{1,0:T(8,128)(2,1)S(1)}, bf16[512,512]{1,0:T(8,128)(2,1)S(1)}, f32[1024,128]{1,0:T(8,128)S(1)}) custom-call(bf16[64,1280]{1,0:T(8,128)(2,1)S(1)} %get-tuple-element.55.row_hot, s32[1,1280]{1,0:T(1,128)S(1)} %get-tuple-element.56.cols, bf16[256,1280]{1,0:T(8,128)(2,1)S(1)} %bitcast.9, ...), custom_call_target="tpu_custom_call" | custom-call | tf_op jit(solution)/shard_map/pallas_call | solution.py:32
  14.3 1.6 %collective-permute-start.2 = (bf16[528,128]{1,0:T(8,128)(2,1)S(1)}, bf16[528,128]{1,0:T(8,128)(2,1)S(1)}, u32[]{:S(2)}, u32[]{:S(2)}) collective-permute-start(bf16[528,128]{1,0:T(8,128)(2,1)S(1)} %shard_map.73._), channel_id=1, source_target_pairs={{1,4},{5,8},{9,12},{13,0},{4,1},{8,5},{12,9},{0,13},{3,6},{7,10},{... | collective-permute-start | bytes 405512 | tf_op jit(solution)/shard_map/ppermute | solution.py:302
  16.5 0.7 %shard_map.75 = (f32[1024,128]{1,0:T(8,128)S(1)}, f32[2,128]{1,0:T(2,128)S(1)}) custom-call(bf16[1024,1024]{1,0:T(8,128)(2,1)S(1)} %get-tuple-element.67.own, bf16[1024,128]{1,0:T(8,128)(2,1)S(1)} %get-tuple-element.68.w, f32[1024,128]{1,0:T(8,128)S(1)} %get-tuple-element.61.previous.refs_0_, f32[1024,128]{1,0:T(8,128)S(1)} %get-tuple-element.69.refs_1_.previous), custom_call_target="tpu_custom_call" | custom-call | tf_op jit(solution)/shard_map/pallas_call | solution.py:32
  18.3 3.1 %collective-permute-done.2.got_x = bf16[528,128]{1,0:T(8,128)(2,1)S(1)} collective-permute-done((bf16[528,128]{1,0:T(8,128)(2,1)S(1)}, bf16[528,128]{1,0:T(8,128)(2,1)S(1)}, u32[]{:S(2)}, u32[]{:S(2)}) %collective-permute-start.2) | collective-permute-done | bytes 135200 | tf_op jit(solution)/shard_map/ppermute | solution.py:302
  21.4 1.1 %collective-permute-start.4 = (bf16[528,128]{1,0:T(8,128)(2,1)S(1)}, bf16[528,128]{1,0:T(8,128)(2,1)S(1)}, u32[]{:S(2)}, u32[]{:S(2)}) collective-permute-start(bf16[528,128]{1,0:T(8,128)(2,1)S(1)} %shard_map.77._), channel_id=1, source_target_pairs={{1,4},{5,8},{9,12},{13,0},{4,1},{8,5},{12,9},{0,13},{3,6},{7,10},{... | collective-permute-start | bytes 405512 | tf_op jit(solution)/shard_map/ppermute | solution.py:302
  23.1 0.7 %shard_map.79 = (f32[1024,128]{1,0:T(8,128)S(1)}, f32[1,128]{1,0:T(1,128)S(1)}) custom-call(bf16[1024,1024]{1,0:T(8,128)(2,1)S(1)} %get-tuple-element.67.own, bf16[1024,128]{1,0:T(8,128)(2,1)S(1)} %get-tuple-element.74.w, f32[1024,128]{1,0:T(8,128)S(1)} %get-tuple-element.61.previous.refs_0_, f32[1024,128]{1,0:T(8,128)S(1)} %get-tuple-element.75.refs_1_.previous), custom_call_target="tpu_custom_call" | custom-call | tf_op jit(solution)/shard_map/pallas_call | solution.py:32
  24.9 2.8 %collective-permute-done.4.got_x = bf16[528,128]{1,0:T(8,128)(2,1)S(1)} collective-permute-done((bf16[528,128]{1,0:T(8,128)(2,1)S(1)}, bf16[528,128]{1,0:T(8,128)(2,1)S(1)}, u32[]{:S(2)}, u32[]{:S(2)}) %collective-permute-start.4) | collective-permute-done | bytes 135200 | tf_op jit(solution)/shard_map/ppermute | solution.py:302
  28.0 1.2 %collective-permute-start.6 = (bf16[528,128]{1,0:T(8,128)(2,1)S(1)}, bf16[528,128]{1,0:T(8,128)(2,1)S(1)}, u32[]{:S(2)}, u32[]{:S(2)}) collective-permute-start(bf16[528,128]{1,0:T(8,128)(2,1)S(1)} %shard_map.81._), channel_id=1, source_target_pairs={{1,4},{5,8},{9,12},{13,0},{4,1},{8,5},{12,9},{0,13},{3,6},{7,10},{... | collective-permute-start | bytes 405512 | tf_op jit(solution)/shard_map/ppermute | solution.py:302
  29.7 0.7 %shard_map.83 = (f32[1024,128]{1,0:T(8,128)S(1)}, f32[3,128]{1,0:T(4,128)S(1)}) custom-call(bf16[1024,1024]{1,0:T(8,128)(2,1)S(1)} %get-tuple-element.67.own, bf16[1024,128]{1,0:T(8,128)(2,1)S(1)} %get-tuple-element.80.w, f32[1024,128]{1,0:T(8,128)S(1)} %get-tuple-element.61.previous.refs_0_, f32[1024,128]{1,0:T(8,128)S(1)} %get-tuple-element.75.refs_1_.previous, ...), custom_call_target="tpu_custom_call" | custom-call | tf_op jit(solution)/shard_map/pallas_call | solution.py:32
  31.5 2.8 %collective-permute-done.6.got_x = bf16[528,128]{1,0:T(8,128)(2,1)S(1)} collective-permute-done((bf16[528,128]{1,0:T(8,128)(2,1)S(1)}, bf16[528,128]{1,0:T(8,128)(2,1)S(1)}, u32[]{:S(2)}, u32[]{:S(2)}) %collective-permute-start.6) | collective-permute-done | bytes 135200 | tf_op jit(solution)/shard_map/ppermute | solution.py:302
  34.4 1.4 %collective-permute-start.8 = (bf16[576,128]{1,0:T(8,128)(2,1)S(1)}, bf16[576,128]{1,0:T(8,128)(2,1)S(1)}, u32[]{:S(2)}, u32[]{:S(2)}) collective-permute-start(bf16[576,128]{1,0:T(8,128)(2,1)S(1)} %shard_map.85._), channel_id=1, source_target_pairs={{1,4},{5,8},{9,12},{13,0},{4,1},{8,5},{12,9},{0,13},{3,6},{7,10},{... | collective-permute-start | bytes 442376 | tf_op jit(solution)/shard_map/ppermute | solution.py:302
  35.9 0.7 %shard_map.86 = (f32[1024,128]{1,0:T(8,128)S(1)}, bf16[1024,128]{1,0:T(8,128)(2,1)S(1)}, bf16[560,128]{1,0:T(8,128)(2,1)S(1)}, f32[16,128]{1,0:T(8,128)S(1)}) custom-call(s32[1]{0:T(128)} %bitcast.parity, bf16[528,128]{1,0:T(8,128)(2,1)S(1)} %collective-permute-done.6.got_x, f32[1024,128]{1,0:T(8,128)S(1)} %get-tuple-element.84.base, ...), custom_call_target="tpu_custom_call" | custom-call | tf_op jit(solution)/shard_map/pallas_call | solution.py:32
  36.7 0.7 %shard_map.87.local = f32[1024,128]{1,0:T(8,128)S(1)} custom-call(bf16[1024,1024]{1,0:T(8,128)(2,1)S(1)} %get-tuple-element.67.own, bf16[1024,128]{1,0:T(8,128)(2,1)S(1)} %get-tuple-element.89.w), custom_call_target="tpu_custom_call" | custom-call | tf_op jit(solution)/shard_map/pallas_call | solution.py:32
  38.4 2.5 %collective-permute-done.8.got_x = bf16[576,128]{1,0:T(8,128)(2,1)S(1)} collective-permute-done((bf16[576,128]{1,0:T(8,128)(2,1)S(1)}, bf16[576,128]{1,0:T(8,128)(2,1)S(1)}, u32[]{:S(2)}, u32[]{:S(2)}) %collective-permute-start.8) | collective-permute-done | bytes 147488 | tf_op jit(solution)/shard_map/ppermute | solution.py:302
  41.0 1.7 %collective-permute-start.10 = (bf16[576,128]{1,0:T(8,128)(2,1)S(1)}, bf16[576,128]{1,0:T(8,128)(2,1)S(1)}, u32[]{:S(2)}, u32[]{:S(2)}) collective-permute-start(bf16[576,128]{1,0:T(8,128)(2,1)S(1)} %shard_map.89._), channel_id=1, source_target_pairs={{1,4},{5,8},{9,12},{13,0},{4,1},{8,5},{12,9},{0,13},{3,6},{7,10},{... | collective-permute-start | bytes 442376 | tf_op jit(solution)/shard_map/ppermute | solution.py:302
  45.1 2.5 %collective-permute-done.10.got_x.refs_1_ = bf16[576,128]{1,0:T(8,128)(2,1)S(1)} collective-permute-done((bf16[576,128]{1,0:T(8,128)(2,1)S(1)}, bf16[576,128]{1,0:T(8,128)(2,1)S(1)}, u32[]{:S(2)}, u32[]{:S(2)}) %collective-permute-start.10) | collective-permute-done | bytes 147488 | tf_op jit(solution)/shard_map/ppermute | solution.py:302
  47.6 2.0 %collective-permute-start.12 = (bf16[576,128]{1,0:T(8,128)(2,1)S(1)}, bf16[576,128]{1,0:T(8,128)(2,1)S(1)}, u32[]{:S(2)}, u32[]{:S(2)}) collective-permute-start(bf16[576,128]{1,0:T(8,128)(2,1)S(1)} %shard_map.93._), channel_id=1, source_target_pairs={{1,4},{5,8},{9,12},{13,0},{4,1},{8,5},{12,9},{0,13},{3,6},{7,10},{... | collective-permute-start | bytes 442376 | tf_op jit(solution)/shard_map/ppermute | solution.py:302
  51.9 2.2 %collective-permute-done.12.got_x = bf16[576,128]{1,0:T(8,128)(2,1)S(1)} collective-permute-done((bf16[576,128]{1,0:T(8,128)(2,1)S(1)}, bf16[576,128]{1,0:T(8,128)(2,1)S(1)}, u32[]{:S(2)}, u32[]{:S(2)}) %collective-permute-start.12) | collective-permute-done | bytes 147488 | tf_op jit(solution)/shard_map/ppermute | solution.py:302
  54.2 2.2 %collective-permute-start.14 = (bf16[576,128]{1,0:T(8,128)(2,1)S(1)}, bf16[576,128]{1,0:T(8,128)(2,1)S(1)}, u32[]{:S(2)}, u32[]{:S(2)}) collective-permute-start(bf16[576,128]{1,0:T(8,128)(2,1)S(1)} %shard_map.97._), channel_id=1, source_target_pairs={{1,4},{5,8},{9,12},{13,0},{4,1},{8,5},{12,9},{0,13},{3,6},{7,10},{... | collective-permute-start | bytes 442376 | tf_op jit(solution)/shard_map/ppermute | solution.py:302
  58.7 1.9 %collective-permute-done.14.got_x.refs_3_ = bf16[576,128]{1,0:T(8,128)(2,1)S(1)} collective-permute-done((bf16[576,128]{1,0:T(8,128)(2,1)S(1)}, bf16[576,128]{1,0:T(8,128)(2,1)S(1)}, u32[]{:S(2)}, u32[]{:S(2)}) %collective-permute-start.14) | collective-permute-done | bytes 147488 | tf_op jit(solution)/shard_map/ppermute | solution.py:302
  60.6 1.0 %shard_map.101 = (f32[1024,128]{1,0:T(8,128)}, f32[9,128]{1,0:T(8,128)}) custom-call(s32[1]{0:T(128)} %bitcast.parity, bf16[576,128]{1,0:T(8,128)(2,1)S(1)} %collective-permute-done.14.got_x.refs_3_, f32[1024,128]{1,0:T(8,128)S(1)} %shard_map.100.base, bf16[1024,512]{1,0:T(8,128)(2,1)S(1)} %get-tuple-element.62.cross, ...), custom_call_target="tpu_custom_call" | custom-call | tf_op jit(solution)/shard_map/pallas_call | solution.py:32
  (47 shorter events, 14.6 us)
Async XLA Ops:
  0.6 1.5 %copy-start = (bf16[1280,16,16]{0,2,1:T(8,128)(2,1)S(1)}, bf16[1280,16,16]{0,2,1:T(8,128)(2,1)}, u32[]{:S(2)}) copy-start(bf16[1280,16,16]{0,2,1:T(8,128)(2,1)} %param.6) | copy-start | bytes 1966084
  2.1 2.0 %copy-start.1 = (f32[64,16,128]{2,1,0:T(8,128)S(1)}, f32[64,16,128]{2,1,0:T(8,128)}, u32[]{:S(2)}) copy-start(f32[64,16,128]{2,1,0:T(8,128)} %param.5) | copy-start | bytes 1572868
  4.7 9.5 %collective-permute-start = (bf16[528,128]{1,0:T(8,128)(2,1)S(1)}, bf16[528,128]{1,0:T(8,128)(2,1)S(1)}, u32[]{:S(2)}, u32[]{:S(2)}) collective-permute-start(bf16[528,128]{1,0:T(8,128)(2,1)S(1)} %get-tuple-element.57), channel_id=1, source_target_pairs={{1,4},{5,8},{9,12},{13,0},{4,1},{8,5},{12,9},{0,13},{3,6},{7,10},{... | collective-permute-start | bytes 405512 | tf_op jit(solution)/shard_map/ppermute | solution.py:302
  9.3 4.5 %collective-permute-start.1 = (bf16[512,128]{1,0:T(8,128)(2,1)S(1)}, bf16[512,128]{1,0:T(8,128)(2,1)S(1)}, u32[]{:S(2)}, u32[]{:S(2)}) collective-permute-start(bf16[512,128]{1,0:T(8,128)(2,1)S(1)} %get-tuple-element.58._), channel_id=1, source_target_pairs={{0,1},{1,0},{2,3},{3,2},{4,5},{5,4},{6,7},{7,6},{8,9},{9,8},{10,11... | collective-permute-start | bytes 393224 | tf_op jit(solution)/shard_map/ppermute | solution.py:303
  14.3 7.1 %collective-permute-start.2 = (bf16[528,128]{1,0:T(8,128)(2,1)S(1)}, bf16[528,128]{1,0:T(8,128)(2,1)S(1)}, u32[]{:S(2)}, u32[]{:S(2)}) collective-permute-start(bf16[528,128]{1,0:T(8,128)(2,1)S(1)} %shard_map.73._), channel_id=1, source_target_pairs={{1,4},{5,8},{9,12},{13,0},{4,1},{8,5},{12,9},{0,13},{3,6},{7,10},{... | collective-permute-start | bytes 405512 | tf_op jit(solution)/shard_map/ppermute | solution.py:302
  16.4 1.4 %collective-permute-start.3 = (bf16[512,128]{1,0:T(8,128)(2,1)S(1)}, bf16[512,128]{1,0:T(8,128)(2,1)S(1)}, u32[]{:S(2)}, u32[]{:S(2)}) collective-permute-start(bf16[512,128]{1,0:T(8,128)(2,1)S(1)} %get-tuple-element.66), channel_id=1, source_target_pairs={{0,1},{1,0},{2,3},{3,2},{4,5},{5,4},{6,7},{7,6},{8,9},{9,8},{10,11... | collective-permute-start | bytes 393224 | tf_op jit(solution)/shard_map/ppermute | solution.py:303
  21.4 6.3 %collective-permute-start.4 = (bf16[528,128]{1,0:T(8,128)(2,1)S(1)}, bf16[528,128]{1,0:T(8,128)(2,1)S(1)}, u32[]{:S(2)}, u32[]{:S(2)}) collective-permute-start(bf16[528,128]{1,0:T(8,128)(2,1)S(1)} %shard_map.77._), channel_id=1, source_target_pairs={{1,4},{5,8},{9,12},{13,0},{4,1},{8,5},{12,9},{0,13},{3,6},{7,10},{... | collective-permute-start | bytes 405512 | tf_op jit(solution)/shard_map/ppermute | solution.py:302
  23.0 1.4 %collective-permute-start.5 = (bf16[512,128]{1,0:T(8,128)(2,1)S(1)}, bf16[512,128]{1,0:T(8,128)(2,1)S(1)}, u32[]{:S(2)}, u32[]{:S(2)}) collective-permute-start(bf16[512,128]{1,0:T(8,128)(2,1)S(1)} %get-tuple-element.73), channel_id=1, source_target_pairs={{0,1},{1,0},{2,3},{3,2},{4,5},{5,4},{6,7},{7,6},{8,9},{9,8},{10,11... | collective-permute-start | bytes 393224 | tf_op jit(solution)/shard_map/ppermute | solution.py:303
  28.0 6.4 %collective-permute-start.6 = (bf16[528,128]{1,0:T(8,128)(2,1)S(1)}, bf16[528,128]{1,0:T(8,128)(2,1)S(1)}, u32[]{:S(2)}, u32[]{:S(2)}) collective-permute-start(bf16[528,128]{1,0:T(8,128)(2,1)S(1)} %shard_map.81._), channel_id=1, source_target_pairs={{1,4},{5,8},{9,12},{13,0},{4,1},{8,5},{12,9},{0,13},{3,6},{7,10},{... | collective-permute-start | bytes 405512 | tf_op jit(solution)/shard_map/ppermute | solution.py:302
  29.7 1.4 %collective-permute-start.7 = (bf16[512,128]{1,0:T(8,128)(2,1)S(1)}, bf16[512,128]{1,0:T(8,128)(2,1)S(1)}, u32[]{:S(2)}, u32[]{:S(2)}) collective-permute-start(bf16[512,128]{1,0:T(8,128)(2,1)S(1)} %get-tuple-element.79), channel_id=1, source_target_pairs={{0,1},{1,0},{2,3},{3,2},{4,5},{5,4},{6,7},{7,6},{8,9},{9,8},{10,11... | collective-permute-start | bytes 393224 | tf_op jit(solution)/shard_map/ppermute | solution.py:303
  34.4 6.5 %collective-permute-start.8 = (bf16[576,128]{1,0:T(8,128)(2,1)S(1)}, bf16[576,128]{1,0:T(8,128)(2,1)S(1)}, u32[]{:S(2)}, u32[]{:S(2)}) collective-permute-start(bf16[576,128]{1,0:T(8,128)(2,1)S(1)} %shard_map.85._), channel_id=1, source_target_pairs={{1,4},{5,8},{9,12},{13,0},{4,1},{8,5},{12,9},{0,13},{3,6},{7,10},{... | collective-permute-start | bytes 442376 | tf_op jit(solution)/shard_map/ppermute | solution.py:302
  36.6 1.4 %collective-permute-start.9 = (bf16[560,128]{1,0:T(8,128)(2,1)S(1)}, bf16[560,128]{1,0:T(8,128)(2,1)S(1)}, u32[]{:S(2)}, u32[]{:S(2)}) collective-permute-start(bf16[560,128]{1,0:T(8,128)(2,1)S(1)} %get-tuple-element.88), channel_id=1, source_target_pairs={{0,1},{1,0},{2,3},{3,2},{4,5},{5,4},{6,7},{7,6},{8,9},{9,8},{10,11... | collective-permute-start | bytes 430088 | tf_op jit(solution)/shard_map/ppermute | solution.py:303
  41.0 6.5 %collective-permute-start.10 = (bf16[576,128]{1,0:T(8,128)(2,1)S(1)}, bf16[576,128]{1,0:T(8,128)(2,1)S(1)}, u32[]{:S(2)}, u32[]{:S(2)}) collective-permute-start(bf16[576,128]{1,0:T(8,128)(2,1)S(1)} %shard_map.89._), channel_id=1, source_target_pairs={{1,4},{5,8},{9,12},{13,0},{4,1},{8,5},{12,9},{0,13},{3,6},{7,10},{... | collective-permute-start | bytes 442376 | tf_op jit(solution)/shard_map/ppermute | solution.py:302
  43.2 1.4 %collective-permute-start.11 = (bf16[512,128]{1,0:T(8,128)(2,1)S(1)}, bf16[512,128]{1,0:T(8,128)(2,1)S(1)}, u32[]{:S(2)}, u32[]{:S(2)}) collective-permute-start(bf16[512,128]{1,0:T(8,128)(2,1)S(1)} %get-tuple-element.93), channel_id=1, source_target_pairs={{0,1},{1,0},{2,3},{3,2},{4,5},{5,4},{6,7},{7,6},{8,9},{9,8},{10,11... | collective-permute-start | bytes 393224 | tf_op jit(solution)/shard_map/ppermute | solution.py:303
  47.6 6.5 %collective-permute-start.12 = (bf16[576,128]{1,0:T(8,128)(2,1)S(1)}, bf16[576,128]{1,0:T(8,128)(2,1)S(1)}, u32[]{:S(2)}, u32[]{:S(2)}) collective-permute-start(bf16[576,128]{1,0:T(8,128)(2,1)S(1)} %shard_map.93._), channel_id=1, source_target_pairs={{1,4},{5,8},{9,12},{13,0},{4,1},{8,5},{12,9},{0,13},{3,6},{7,10},{... | collective-permute-start | bytes 442376 | tf_op jit(solution)/shard_map/ppermute | solution.py:302
  50.1 1.4 %collective-permute-start.13 = (bf16[560,128]{1,0:T(8,128)(2,1)S(1)}, bf16[560,128]{1,0:T(8,128)(2,1)S(1)}, u32[]{:S(2)}, u32[]{:S(2)}) collective-permute-start(bf16[560,128]{1,0:T(8,128)(2,1)S(1)} %get-tuple-element.98), channel_id=1, source_target_pairs={{0,1},{1,0},{2,3},{3,2},{4,5},{5,4},{6,7},{7,6},{8,9},{9,8},{10,11... | collective-permute-start | bytes 430088 | tf_op jit(solution)/shard_map/ppermute | solution.py:303
  54.2 6.4 %collective-permute-start.14 = (bf16[576,128]{1,0:T(8,128)(2,1)S(1)}, bf16[576,128]{1,0:T(8,128)(2,1)S(1)}, u32[]{:S(2)}, u32[]{:S(2)}) collective-permute-start(bf16[576,128]{1,0:T(8,128)(2,1)S(1)} %shard_map.97._), channel_id=1, source_target_pairs={{1,4},{5,8},{9,12},{13,0},{4,1},{8,5},{12,9},{0,13},{3,6},{7,10},{... | collective-permute-start | bytes 442376 | tf_op jit(solution)/shard_map/ppermute | solution.py:302
  56.9 1.4 %collective-permute-start.15 = (bf16[512,128]{1,0:T(8,128)(2,1)S(1)}, bf16[512,128]{1,0:T(8,128)(2,1)S(1)}, u32[]{:S(2)}, u32[]{:S(2)}) collective-permute-start(bf16[512,128]{1,0:T(8,128)(2,1)S(1)} %get-tuple-element.103), channel_id=1, source_target_pairs={{0,1},{1,0},{2,3},{3,2},{4,5},{5,4},{6,7},{7,6},{8,9},{9,8},{10,11... | collective-permute-start | bytes 393224 | tf_op jit(solution)/shard_map/ppermute | solution.py:303

commit v6 on v5

--- a/solution.py
+++ b/solution.py
@@ -16,9 +16,9 @@
 NT = (((1,), (1,)), ((), ()))
 AHEAD = 1_000_000_000
 PAD = 8
-ROWS = 16
-TAIL = 3 * ROWS
-LONGER = ROWS
+ROWS = STEPS + 1
+LONGER = 16
+TAIL = -(-3 * ROWS // 16) * 16
 DOTS = [[(0, n)] + [(m, n) for m in (n - 1, n) if m > 0 and HALF < m + n] for n in range(HALF + 1)]
 DOTS[:2] = [[], DOTS[0] + DOTS[1]]
 
@@ -112,7 +112,8 @@
 
 
 def blank(out, start):
-    out[start:, :] = jnp.zeros((out.shape[0] - start, out.shape[1]), out.dtype)
+    if start < out.shape[0]:
+        out[start:, :] = jnp.zeros((out.shape[0] - start, out.shape[1]), out.dtype)
 
 
 def times(left, right):
@@ -157,20 +158,21 @@
     rows = [dots[0, n] for n in range(HALF + 1)]
     for n in range(HALF + 1, STEPS + 1):
         rows.append(2.0 * dots[n // 2, n - n // 2] - dots[0, n % 2])
-    rows.append(jnp.zeros((ROWS - STEPS - 1, rows[0].shape[1]), F32))
     return jnp.concatenate(rows, axis=0) * scale
 
 
 def put_table(table, out, start):
-    for n in range(3):
-        piece = table.astype(BF16)
-        out[start + n * ROWS : start + (n + 1) * ROWS, :] = piece
-        table = table - piece.astype(F32)
+    pieces = []
+    for _ in range(3):
+        pieces.append(table.astype(BF16).astype(F32))
+        table = table - pieces[-1]
+    pieces.append(jnp.zeros((TAIL - 3 * ROWS, table.shape[1]), F32))
+    out[start : start + TAIL, :] = jnp.concatenate(pieces, axis=0).astype(BF16)
 
 
 def get_table(got, start):
-    pieces = [got[start + n * ROWS : start + (n + 1) * ROWS, :].astype(F32) for n in range(3)]
-    return pieces[0] + (pieces[1] + pieces[2])
+    pieces = got[start : start + TAIL, :].astype(F32)
+    return pieces[:ROWS] + (pieces[ROWS : 2 * ROWS] + pieces[2 * ROWS : 3 * ROWS])
 
 
 def before_body(atoms, orbits, halo, k, parity, got_i, local, previous, cross, crosst, base_ref, pre_ref=None):
@@ -283,7 +285,7 @@
     total = table[...]
     for got in refs[:-2]:
         total = total + get_table(got, edge_size)
-    moments[...] = total[: STEPS + 1, :]
+    moments[...] = total
 
 
 def per_device(probes, blocks, block_rows, block_cols, counts):
@@ -321,7 +323,8 @@
     )
     whole, rounded, message = ((size, width), F32), ((size, width), BF16), ((edge_size, width), BF16)
     longer = ((edge_size + TAIL, width), BF16)
-    far_rows = [edge_size + LONGER + (TAIL if ride and k >= HALF else 0) for k in range(STEPS)]
+    riding = [ride and k >= HALF for k in range(STEPS)]
+    far_rows = [edge_size + (TAIL if riding[k] else 0) + (0 if riding[k] and k % 2 else LONGER) for k in range(STEPS)]
     v, w, send_x, send_i = call(
         functools.partial(first_body, *dims, turn),
         (whole, rounded, ((far_rows[0], width), BF16), message),

time: 61.9 us -> 61.6 us (level)
  no operation moved by 1% of the time
where the time goes in v6:
time: 61.6 us; the launch traced here: 61.3 us
  waiting for transfers between devices  21.8 us (35%)
  Pallas kernels  20.8 us (34%)
  starting transfers between devices  16.3 us (26%)
  between operations  1.68 us (3%)
  other arithmetic  0.72 us (1%)
    pallas_call x34, Pallas kernels, call(): pl.pallas_call(body, out_shape=tuple((jax.ShapeDtypeStruct(s, t) for s, t...  20.8 us
    ppermute x8, waiting for transfers between devices, per_device(): across = lambda x: lax.ppermute(x, RING, between)  17.5 us
    ppermute x8, starting transfers between devices, per_device(): across = lambda x: lax.ppermute(x, RING, between)  15.8 us
    ppermute x8, waiting for transfers between devices, per_device(): inside = lambda x: lax.ppermute(x, 'orb', [(0, 1), (1, 0)])  4.34 us
  transfers between devices with their start and end apart: 16, of which 14 were waited for; matrix products, arithmetic and copies ran while one was open for 0% of the time, Pallas kernels for 27%

profile of v6, /device:TPU:0, one launch (start us, length us, event | category | flops | bytes accessed | tf_op | source)
XLA Modules:
  0.0 61.3 jit_solution(452534452851846329)
XLA Ops:
  1.4 0.7 %add_select_fusion.pair = s32[1280]{0:T(1024)S(1)} fusion(s32[1280]{0:T(1024)} %param.7, s32[1280]{0:T(1024)} %param.8, s32[]{:T(128)} %bitcast.7), kind=kLoop, calls=%fused_computation | loop fusion | flops 5120 | bytes 15364 | tf_op jit(solution)/shard_map/jit(_where)/select_n | solution.py:308
  2.1 1.9 %shard_map.69.crosst = bf16[512,1024]{1,0:T(8,128)(2,1)S(1)} custom-call(bf16[64,1280]{1,0:T(8,128)(2,1)S(1)} %get-tuple-element.55.row_hot, s32[1,1280]{1,0:T(1,128)S(1)} %get-tuple-element.56.cols, bf16[256,1280]{1,0:T(8,128)(2,1)S(1)} %bitcast.8), custom_call_target="tpu_custom_call" | custom-call | flops 1342177280 | bytes 824320 | tf_op jit(solution)/shard_map/pallas_call | solution.py:32
  4.7 4.6 %collective-permute-start = (bf16[528,128]{1,0:T(8,128)(2,1)S(1)}, bf16[528,128]{1,0:T(8,128)(2,1)S(1)}, u32[]{:S(2)}, u32[]{:S(2)}) collective-permute-start(bf16[528,128]{1,0:T(8,128)(2,1)S(1)} %get-tuple-element.57), channel_id=1, source_target_pairs={{1,4},{5,8},{9,12},{13,0},{4,1},{8,5},{12,9},{0,13},{3,6},{7,10},{... | collective-permute-start | bytes 405512 | tf_op jit(solution)/shard_map/ppermute | solution.py:304
  9.3 4.5 %shard_map.71 = (bf16[1024,1024]{1,0:T(8,128)(2,1)S(1)}, bf16[1024,512]{1,0:T(8,128)(2,1)S(1)}, bf16[512,512]{1,0:T(8,128)(2,1)S(1)}, f32[1024,128]{1,0:T(8,128)S(1)}) custom-call(bf16[64,1280]{1,0:T(8,128)(2,1)S(1)} %get-tuple-element.55.row_hot, s32[1,1280]{1,0:T(1,128)S(1)} %get-tuple-element.56.cols, bf16[256,1280]{1,0:T(8,128)(2,1)S(1)} %bitcast.9, ...), custom_call_target="tpu_custom_call" | custom-call | tf_op jit(solution)/shard_map/pallas_call | solution.py:32
  14.3 1.6 %collective-permute-start.2 = (bf16[528,128]{1,0:T(8,128)(2,1)S(1)}, bf16[528,128]{1,0:T(8,128)(2,1)S(1)}, u32[]{:S(2)}, u32[]{:S(2)}) collective-permute-start(bf16[528,128]{1,0:T(8,128)(2,1)S(1)} %shard_map.73._), channel_id=1, source_target_pairs={{1,4},{5,8},{9,12},{13,0},{4,1},{8,5},{12,9},{0,13},{3,6},{7,10},{... | collective-permute-start | bytes 405512 | tf_op jit(solution)/shard_map/ppermute | solution.py:304
  16.5 0.7 %shard_map.75 = (f32[1024,128]{1,0:T(8,128)S(1)}, f32[2,128]{1,0:T(2,128)S(1)}) custom-call(bf16[1024,1024]{1,0:T(8,128)(2,1)S(1)} %get-tuple-element.67.own, bf16[1024,128]{1,0:T(8,128)(2,1)S(1)} %get-tuple-element.68.w, f32[1024,128]{1,0:T(8,128)S(1)} %get-tuple-element.61.previous.refs_0_, f32[1024,128]{1,0:T(8,128)S(1)} %get-tuple-element.69.refs_1_.previous), custom_call_target="tpu_custom_call" | custom-call | tf_op jit(solution)/shard_map/pallas_call | solution.py:32
  18.3 3.1 %collective-permute-done.2.got_x = bf16[528,128]{1,0:T(8,128)(2,1)S(1)} collective-permute-done((bf16[528,128]{1,0:T(8,128)(2,1)S(1)}, bf16[528,128]{1,0:T(8,128)(2,1)S(1)}, u32[]{:S(2)}, u32[]{:S(2)}) %collective-permute-start.2) | collective-permute-done | bytes 135200 | tf_op jit(solution)/shard_map/ppermute | solution.py:304
  21.4 1.1 %collective-permute-start.4 = (bf16[528,128]{1,0:T(8,128)(2,1)S(1)}, bf16[528,128]{1,0:T(8,128)(2,1)S(1)}, u32[]{:S(2)}, u32[]{:S(2)}) collective-permute-start(bf16[528,128]{1,0:T(8,128)(2,1)S(1)} %shard_map.77._), channel_id=1, source_target_pairs={{1,4},{5,8},{9,12},{13,0},{4,1},{8,5},{12,9},{0,13},{3,6},{7,10},{... | collective-permute-start | bytes 405512 | tf_op jit(solution)/shard_map/ppermute | solution.py:304
  23.1 0.7 %shard_map.79 = (f32[1024,128]{1,0:T(8,128)S(1)}, f32[1,128]{1,0:T(1,128)S(1)}) custom-call(bf16[1024,1024]{1,0:T(8,128)(2,1)S(1)} %get-tuple-element.67.own, bf16[1024,128]{1,0:T(8,128)(2,1)S(1)} %get-tuple-element.74.w, f32[1024,128]{1,0:T(8,128)S(1)} %get-tuple-element.61.previous.refs_0_, f32[1024,128]{1,0:T(8,128)S(1)} %get-tuple-element.75.refs_1_.previous), custom_call_target="tpu_custom_call" | custom-call | tf_op jit(solution)/shard_map/pallas_call | solution.py:32
  24.9 2.8 %collective-permute-done.4.got_x = bf16[528,128]{1,0:T(8,128)(2,1)S(1)} collective-permute-done((bf16[528,128]{1,0:T(8,128)(2,1)S(1)}, bf16[528,128]{1,0:T(8,128)(2,1)S(1)}, u32[]{:S(2)}, u32[]{:S(2)}) %collective-permute-start.4) | collective-permute-done | bytes 135200 | tf_op jit(solution)/shard_map/ppermute | solution.py:304
  28.0 1.2 %collective-permute-start.6 = (bf16[528,128]{1,0:T(8,128)(2,1)S(1)}, bf16[528,128]{1,0:T(8,128)(2,1)S(1)}, u32[]{:S(2)}, u32[]{:S(2)}) collective-permute-start(bf16[528,128]{1,0:T(8,128)(2,1)S(1)} %shard_map.81._), channel_id=1, source_target_pairs={{1,4},{5,8},{9,12},{13,0},{4,1},{8,5},{12,9},{0,13},{3,6},{7,10},{... | collective-permute-start | bytes 405512 | tf_op jit(solution)/shard_map/ppermute | solution.py:304
  29.7 0.7 %shard_map.83 = (f32[1024,128]{1,0:T(8,128)S(1)}, f32[3,128]{1,0:T(4,128)S(1)}) custom-call(bf16[1024,1024]{1,0:T(8,128)(2,1)S(1)} %get-tuple-element.67.own, bf16[1024,128]{1,0:T(8,128)(2,1)S(1)} %get-tuple-element.80.w, f32[1024,128]{1,0:T(8,128)S(1)} %get-tuple-element.61.previous.refs_0_, f32[1024,128]{1,0:T(8,128)S(1)} %get-tuple-element.75.refs_1_.previous, ...), custom_call_target="tpu_custom_call" | custom-call | tf_op jit(solution)/shard_map/pallas_call | solution.py:32
  31.5 2.8 %collective-permute-done.6.got_x = bf16[528,128]{1,0:T(8,128)(2,1)S(1)} collective-permute-done((bf16[528,128]{1,0:T(8,128)(2,1)S(1)}, bf16[528,128]{1,0:T(8,128)(2,1)S(1)}, u32[]{:S(2)}, u32[]{:S(2)}) %collective-permute-start.6) | collective-permute-done | bytes 135200 | tf_op jit(solution)/shard_map/ppermute | solution.py:304
  34.4 1.5 %collective-permute-start.8 = (bf16[560,128]{1,0:T(8,128)(2,1)S(1)}, bf16[560,128]{1,0:T(8,128)(2,1)S(1)}, u32[]{:S(2)}, u32[]{:S(2)}) collective-permute-start(bf16[560,128]{1,0:T(8,128)(2,1)S(1)} %shard_map.85._), channel_id=1, source_target_pairs={{1,4},{5,8},{9,12},{13,0},{4,1},{8,5},{12,9},{0,13},{3,6},{7,10},{... | collective-permute-start | bytes 430088 | tf_op jit(solution)/shard_map/ppermute | solution.py:304
  35.9 0.7 %shard_map.86 = (f32[1024,128]{1,0:T(8,128)S(1)}, bf16[1024,128]{1,0:T(8,128)(2,1)S(1)}, bf16[544,128]{1,0:T(8,128)(2,1)S(1)}, f32[9,128]{1,0:T(8,128)S(1)}) custom-call(s32[1]{0:T(128)} %bitcast.parity, bf16[528,128]{1,0:T(8,128)(2,1)S(1)} %collective-permute-done.6.got_x, f32[1024,128]{1,0:T(8,128)S(1)} %get-tuple-element.84.base, ...), custom_call_target="tpu_custom_call" | custom-call | tf_op jit(solution)/shard_map/pallas_call | solution.py:32
  38.4 2.4 %collective-permute-done.8.got_x = bf16[560,128]{1,0:T(8,128)(2,1)S(1)} collective-permute-done((bf16[560,128]{1,0:T(8,128)(2,1)S(1)}, bf16[560,128]{1,0:T(8,128)(2,1)S(1)}, u32[]{:S(2)}, u32[]{:S(2)}) %collective-permute-start.8) | collective-permute-done | bytes 143392 | tf_op jit(solution)/shard_map/ppermute | solution.py:304
  41.0 1.7 %collective-permute-start.10 = (bf16[544,128]{1,0:T(8,128)(2,1)S(1)}, bf16[544,128]{1,0:T(8,128)(2,1)S(1)}, u32[]{:S(2)}, u32[]{:S(2)}) collective-permute-start(bf16[544,128]{1,0:T(8,128)(2,1)S(1)} %shard_map.89._), channel_id=1, source_target_pairs={{1,4},{5,8},{9,12},{13,0},{4,1},{8,5},{12,9},{0,13},{3,6},{7,10},{... | collective-permute-start | bytes 417800 | tf_op jit(solution)/shard_map/ppermute | solution.py:304
  43.3 0.7 %shard_map.91.local = f32[1024,128]{1,0:T(8,128)S(1)} custom-call(bf16[1024,1024]{1,0:T(8,128)(2,1)S(1)} %get-tuple-element.67.own, bf16[1024,128]{1,0:T(8,128)(2,1)S(1)} %get-tuple-element.94.w), custom_call_target="tpu_custom_call" | custom-call | tf_op jit(solution)/shard_map/pallas_call | solution.py:32
  45.1 2.4 %collective-permute-done.10.got_x.refs_1_ = bf16[544,128]{1,0:T(8,128)(2,1)S(1)} collective-permute-done((bf16[544,128]{1,0:T(8,128)(2,1)S(1)}, bf16[544,128]{1,0:T(8,128)(2,1)S(1)}, u32[]{:S(2)}, u32[]{:S(2)}) %collective-permute-start.10) | collective-permute-done | bytes 139296 | tf_op jit(solution)/shard_map/ppermute | solution.py:304
  47.5 2.0 %collective-permute-start.12 = (bf16[560,128]{1,0:T(8,128)(2,1)S(1)}, bf16[560,128]{1,0:T(8,128)(2,1)S(1)}, u32[]{:S(2)}, u32[]{:S(2)}) collective-permute-start(bf16[560,128]{1,0:T(8,128)(2,1)S(1)} %shard_map.93._), channel_id=1, source_target_pairs={{1,4},{5,8},{9,12},{13,0},{4,1},{8,5},{12,9},{0,13},{3,6},{7,10},{... | collective-permute-start | bytes 430088 | tf_op jit(solution)/shard_map/ppermute | solution.py:304
  51.8 2.1 %collective-permute-done.12.got_x = bf16[560,128]{1,0:T(8,128)(2,1)S(1)} collective-permute-done((bf16[560,128]{1,0:T(8,128)(2,1)S(1)}, bf16[560,128]{1,0:T(8,128)(2,1)S(1)}, u32[]{:S(2)}, u32[]{:S(2)}) %collective-permute-start.12) | collective-permute-done | bytes 143392 | tf_op jit(solution)/shard_map/ppermute | solution.py:304
  54.0 2.2 %collective-permute-start.14 = (bf16[544,128]{1,0:T(8,128)(2,1)S(1)}, bf16[544,128]{1,0:T(8,128)(2,1)S(1)}, u32[]{:S(2)}, u32[]{:S(2)}) collective-permute-start(bf16[544,128]{1,0:T(8,128)(2,1)S(1)} %shard_map.97._), channel_id=1, source_target_pairs={{1,4},{5,8},{9,12},{13,0},{4,1},{8,5},{12,9},{0,13},{3,6},{7,10},{... | collective-permute-start | bytes 417800 | tf_op jit(solution)/shard_map/ppermute | solution.py:304
  58.6 1.8 %collective-permute-done.14.got_x.refs_3_ = bf16[544,128]{1,0:T(8,128)(2,1)S(1)} collective-permute-done((bf16[544,128]{1,0:T(8,128)(2,1)S(1)}, bf16[544,128]{1,0:T(8,128)(2,1)S(1)}, u32[]{:S(2)}, u32[]{:S(2)}) %collective-permute-start.14) | collective-permute-done | bytes 139296 | tf_op jit(solution)/shard_map/ppermute | solution.py:304
  60.3 1.0 %shard_map.101 = (f32[1024,128]{1,0:T(8,128)}, f32[9,128]{1,0:T(8,128)}) custom-call(s32[1]{0:T(128)} %bitcast.parity, bf16[544,128]{1,0:T(8,128)(2,1)S(1)} %collective-permute-done.14.got_x.refs_3_, f32[1024,128]{1,0:T(8,128)S(1)} %shard_map.100.base, bf16[1024,512]{1,0:T(8,128)(2,1)S(1)} %get-tuple-element.62.cross, ...), custom_call_target="tpu_custom_call" | custom-call | tf_op jit(solution)/shard_map/pallas_call | solution.py:32
  (47 shorter events, 14.6 us)
Async XLA Ops:
  0.6 1.5 %copy-start = (bf16[1280,16,16]{0,2,1:T(8,128)(2,1)S(1)}, bf16[1280,16,16]{0,2,1:T(8,128)(2,1)}, u32[]{:S(2)}) copy-start(bf16[1280,16,16]{0,2,1:T(8,128)(2,1)} %param.6) | copy-start | bytes 1966084
  2.1 2.0 %copy-start.1 = (f32[64,16,128]{2,1,0:T(8,128)S(1)}, f32[64,16,128]{2,1,0:T(8,128)}, u32[]{:S(2)}) copy-start(f32[64,16,128]{2,1,0:T(8,128)} %param.5) | copy-start | bytes 1572868
  4.7 9.5 %collective-permute-start = (bf16[528,128]{1,0:T(8,128)(2,1)S(1)}, bf16[528,128]{1,0:T(8,128)(2,1)S(1)}, u32[]{:S(2)}, u32[]{:S(2)}) collective-permute-start(bf16[528,128]{1,0:T(8,128)(2,1)S(1)} %get-tuple-element.57), channel_id=1, source_target_pairs={{1,4},{5,8},{9,12},{13,0},{4,1},{8,5},{12,9},{0,13},{3,6},{7,10},{... | collective-permute-start | bytes 405512 | tf_op jit(solution)/shard_map/ppermute | solution.py:304
  9.3 4.5 %collective-permute-start.1 = (bf16[512,128]{1,0:T(8,128)(2,1)S(1)}, bf16[512,128]{1,0:T(8,128)(2,1)S(1)}, u32[]{:S(2)}, u32[]{:S(2)}) collective-permute-start(bf16[512,128]{1,0:T(8,128)(2,1)S(1)} %get-tuple-element.58._), channel_id=1, source_target_pairs={{0,1},{1,0},{2,3},{3,2},{4,5},{5,4},{6,7},{7,6},{8,9},{9,8},{10,11... | collective-permute-start | bytes 393224 | tf_op jit(solution)/shard_map/ppermute | solution.py:305
  14.3 7.1 %collective-permute-start.2 = (bf16[528,128]{1,0:T(8,128)(2,1)S(1)}, bf16[528,128]{1,0:T(8,128)(2,1)S(1)}, u32[]{:S(2)}, u32[]{:S(2)}) collective-permute-start(bf16[528,128]{1,0:T(8,128)(2,1)S(1)} %shard_map.73._), channel_id=1, source_target_pairs={{1,4},{5,8},{9,12},{13,0},{4,1},{8,5},{12,9},{0,13},{3,6},{7,10},{... | collective-permute-start | bytes 405512 | tf_op jit(solution)/shard_map/ppermute | solution.py:304
  16.4 1.4 %collective-permute-start.3 = (bf16[512,128]{1,0:T(8,128)(2,1)S(1)}, bf16[512,128]{1,0:T(8,128)(2,1)S(1)}, u32[]{:S(2)}, u32[]{:S(2)}) collective-permute-start(bf16[512,128]{1,0:T(8,128)(2,1)S(1)} %get-tuple-element.66), channel_id=1, source_target_pairs={{0,1},{1,0},{2,3},{3,2},{4,5},{5,4},{6,7},{7,6},{8,9},{9,8},{10,11... | collective-permute-start | bytes 393224 | tf_op jit(solution)/shard_map/ppermute | solution.py:305
  21.4 6.3 %collective-permute-start.4 = (bf16[528,128]{1,0:T(8,128)(2,1)S(1)}, bf16[528,128]{1,0:T(8,128)(2,1)S(1)}, u32[]{:S(2)}, u32[]{:S(2)}) collective-permute-start(bf16[528,128]{1,0:T(8,128)(2,1)S(1)} %shard_map.77._), channel_id=1, source_target_pairs={{1,4},{5,8},{9,12},{13,0},{4,1},{8,5},{12,9},{0,13},{3,6},{7,10},{... | collective-permute-start | bytes 405512 | tf_op jit(solution)/shard_map/ppermute | solution.py:304
  23.0 1.4 %collective-permute-start.5 = (bf16[512,128]{1,0:T(8,128)(2,1)S(1)}, bf16[512,128]{1,0:T(8,128)(2,1)S(1)}, u32[]{:S(2)}, u32[]{:S(2)}) collective-permute-start(bf16[512,128]{1,0:T(8,128)(2,1)S(1)} %get-tuple-element.73), channel_id=1, source_target_pairs={{0,1},{1,0},{2,3},{3,2},{4,5},{5,4},{6,7},{7,6},{8,9},{9,8},{10,11... | collective-permute-start | bytes 393224 | tf_op jit(solution)/shard_map/ppermute | solution.py:305
  28.0 6.4 %collective-permute-start.6 = (bf16[528,128]{1,0:T(8,128)(2,1)S(1)}, bf16[528,128]{1,0:T(8,128)(2,1)S(1)}, u32[]{:S(2)}, u32[]{:S(2)}) collective-permute-start(bf16[528,128]{1,0:T(8,128)(2,1)S(1)} %shard_map.81._), channel_id=1, source_target_pairs={{1,4},{5,8},{9,12},{13,0},{4,1},{8,5},{12,9},{0,13},{3,6},{7,10},{... | collective-permute-start | bytes 405512 | tf_op jit(solution)/shard_map/ppermute | solution.py:304
  29.7 1.4 %collective-permute-start.7 = (bf16[512,128]{1,0:T(8,128)(2,1)S(1)}, bf16[512,128]{1,0:T(8,128)(2,1)S(1)}, u32[]{:S(2)}, u32[]{:S(2)}) collective-permute-start(bf16[512,128]{1,0:T(8,128)(2,1)S(1)} %get-tuple-element.79), channel_id=1, source_target_pairs={{0,1},{1,0},{2,3},{3,2},{4,5},{5,4},{6,7},{7,6},{8,9},{9,8},{10,11... | collective-permute-start | bytes 393224 | tf_op jit(solution)/shard_map/ppermute | solution.py:305
  34.4 6.5 %collective-permute-start.8 = (bf16[560,128]{1,0:T(8,128)(2,1)S(1)}, bf16[560,128]{1,0:T(8,128)(2,1)S(1)}, u32[]{:S(2)}, u32[]{:S(2)}) collective-permute-start(bf16[560,128]{1,0:T(8,128)(2,1)S(1)} %shard_map.85._), channel_id=1, source_target_pairs={{1,4},{5,8},{9,12},{13,0},{4,1},{8,5},{12,9},{0,13},{3,6},{7,10},{... | collective-permute-start | bytes 430088 | tf_op jit(solution)/shard_map/ppermute | solution.py:304
  36.6 1.4 %collective-permute-start.9 = (bf16[544,128]{1,0:T(8,128)(2,1)S(1)}, bf16[544,128]{1,0:T(8,128)(2,1)S(1)}, u32[]{:S(2)}, u32[]{:S(2)}) collective-permute-start(bf16[544,128]{1,0:T(8,128)(2,1)S(1)} %get-tuple-element.88), channel_id=1, source_target_pairs={{0,1},{1,0},{2,3},{3,2},{4,5},{5,4},{6,7},{7,6},{8,9},{9,8},{10,11... | collective-permute-start | bytes 417800 | tf_op jit(solution)/shard_map/ppermute | solution.py:305
  41.0 6.4 %collective-permute-start.10 = (bf16[544,128]{1,0:T(8,128)(2,1)S(1)}, bf16[544,128]{1,0:T(8,128)(2,1)S(1)}, u32[]{:S(2)}, u32[]{:S(2)}) collective-permute-start(bf16[544,128]{1,0:T(8,128)(2,1)S(1)} %shard_map.89._), channel_id=1, source_target_pairs={{1,4},{5,8},{9,12},{13,0},{4,1},{8,5},{12,9},{0,13},{3,6},{7,10},{... | collective-permute-start | bytes 417800 | tf_op jit(solution)/shard_map/ppermute | solution.py:304
  43.2 1.4 %collective-permute-start.11 = (bf16[512,128]{1,0:T(8,128)(2,1)S(1)}, bf16[512,128]{1,0:T(8,128)(2,1)S(1)}, u32[]{:S(2)}, u32[]{:S(2)}) collective-permute-start(bf16[512,128]{1,0:T(8,128)(2,1)S(1)} %get-tuple-element.93), channel_id=1, source_target_pairs={{0,1},{1,0},{2,3},{3,2},{4,5},{5,4},{6,7},{7,6},{8,9},{9,8},{10,11... | collective-permute-start | bytes 393224 | tf_op jit(solution)/shard_map/ppermute | solution.py:305
  47.5 6.5 %collective-permute-start.12 = (bf16[560,128]{1,0:T(8,128)(2,1)S(1)}, bf16[560,128]{1,0:T(8,128)(2,1)S(1)}, u32[]{:S(2)}, u32[]{:S(2)}) collective-permute-start(bf16[560,128]{1,0:T(8,128)(2,1)S(1)} %shard_map.93._), channel_id=1, source_target_pairs={{1,4},{5,8},{9,12},{13,0},{4,1},{8,5},{12,9},{0,13},{3,6},{7,10},{... | collective-permute-start | bytes 430088 | tf_op jit(solution)/shard_map/ppermute | solution.py:304
  49.9 1.4 %collective-permute-start.13 = (bf16[544,128]{1,0:T(8,128)(2,1)S(1)}, bf16[544,128]{1,0:T(8,128)(2,1)S(1)}, u32[]{:S(2)}, u32[]{:S(2)}) collective-permute-start(bf16[544,128]{1,0:T(8,128)(2,1)S(1)} %get-tuple-element.98), channel_id=1, source_target_pairs={{0,1},{1,0},{2,3},{3,2},{4,5},{5,4},{6,7},{7,6},{8,9},{9,8},{10,11... | collective-permute-start | bytes 417800 | tf_op jit(solution)/shard_map/ppermute | solution.py:305
  54.0 6.3 %collective-permute-start.14 = (bf16[544,128]{1,0:T(8,128)(2,1)S(1)}, bf16[544,128]{1,0:T(8,128)(2,1)S(1)}, u32[]{:S(2)}, u32[]{:S(2)}) collective-permute-start(bf16[544,128]{1,0:T(8,128)(2,1)S(1)} %shard_map.97._), channel_id=1, source_target_pairs={{1,4},{5,8},{9,12},{13,0},{4,1},{8,5},{12,9},{0,13},{3,6},{7,10},{... | collective-permute-start | bytes 417800 | tf_op jit(solution)/shard_map/ppermute | solution.py:304
  56.7 1.4 %collective-permute-start.15 = (bf16[512,128]{1,0:T(8,128)(2,1)S(1)}, bf16[512,128]{1,0:T(8,128)(2,1)S(1)}, u32[]{:S(2)}, u32[]{:S(2)}) collective-permute-start(bf16[512,128]{1,0:T(8,128)(2,1)S(1)} %get-tuple-element.103), channel_id=1, source_target_pairs={{0,1},{1,0},{2,3},{3,2},{4,5},{5,4},{6,7},{7,6},{8,9},{9,8},{10,11... | collective-permute-start | bytes 393224 | tf_op jit(solution)/shard_map/ppermute | solution.py:305

commit v7 on v6

--- a/solution.py
+++ b/solution.py
@@ -286,6 +286,40 @@
     for got in refs[:-2]:
         total = total + get_table(got, edge_size)
     moments[...] = total
+
+
+def halves_body(atoms, orbits, halo, parity, got_x, base, cross, table, *refs):
+    *got, out, moments, full = refs
+    edge_size = orbits * halo
+    near = pl.program_id(0) == 1
+
+    def put(at, make):
+        for o in range(orbits):
+            out[pl.ds(o, halo, stride=orbits), :] = make(o, slice(o * atoms + at, o * atoms + at + halo))
+
+    @pl.when((parity[0] == 0) & ~near)
+    def _():
+        put(halo, lambda o, rows: base[rows, :])
+
+    @pl.when((parity[0] == 0) & near)
+    def _():
+        put(0, lambda o, rows: base[rows, :] + 2.0 * got_x[o * halo : (o + 1) * halo, :].astype(F32))
+
+    @pl.when((parity[0] != 0) & ~near)
+    def _():
+        full[...] = base[...] + 2.0 * times(cross, got_x[:edge_size, :])
+        put(halo, lambda o, rows: full[rows, :])
+
+    @pl.when((parity[0] != 0) & near)
+    def _():
+        put(0, lambda o, rows: full[rows, :])
+
+    @pl.when(~near)
+    def _():
+        total = table[...]
+        for one in got:
+            total = total + get_table(one, edge_size)
+        moments[...] = total
 
 
 def per_device(probes, blocks, block_rows, block_cols, counts):
@@ -383,11 +417,21 @@
             )
         if ride and k >= HALF:
             got.append(got_i if k % 2 == 0 else got_x)
-    last, moments = call(
-        functools.partial(last_body, *dims, STEPS - 1, turn),
-        (whole, ((STEPS + 1, width), F32)),
-        parity, got_x, base, cross, table, *got, smem=1,
-    )
+    operands = (parity, got_x, base, cross, table, *got)
+    if turn:
+        last, moments = pl.pallas_call(
+            functools.partial(halves_body, *dims),
+            grid=(2,),
+            out_shape=(jax.ShapeDtypeStruct(*whole), jax.ShapeDtypeStruct((ROWS, width), F32)),
+            in_specs=[SMEM] + [VMEM] * (len(operands) - 1),
+            out_specs=(pl.BlockSpec((size // 2, width), lambda g: (1 - g, 0)), VMEM),
+            scratch_shapes=[pltpu.VMEM((size, width), F32)],
+            compiler_params=pltpu.CompilerParams(vmem_limit_bytes=16 << 20),
+        )(*operands)
+    else:
+        last, moments = call(
+            functools.partial(last_body, *dims, STEPS - 1, turn), (whole, ((ROWS, width), F32)), *operands, smem=1
+        )
     last = last.reshape(atoms, orbits, width) if turn else last.reshape(orbits, atoms, width).transpose(1, 0, 2)
     return last, moments if ride else lax.psum(moments, RING)
 

time: 61.6 us -> 61.6 us (level)
    pallas_call x0 -> x1, Pallas kernels: none -> 1.02 us  [per_device(): pl.pallas_call(functools.partial(halves_body, *dims), grid=(2,), out_shap...]
    pallas_call x34 -> x33, Pallas kernels: 20.8 us -> 19.8 us  [call(): pl.pallas_call(body, out_shape=tuple((jax.ShapeDtypeStruct(s, t) for s, t...]
where the time goes in v7:
time: 61.6 us; the launch traced here: 61.4 us
  waiting for transfers between devices  21.8 us (35%)
  Pallas kernels  20.8 us (34%)
  starting transfers between devices  16.3 us (26%)
  between operations  1.68 us (3%)
  other arithmetic  0.72 us (1%)
    pallas_call x33, Pallas kernels, call(): pl.pallas_call(body, out_shape=tuple((jax.ShapeDtypeStruct(s, t) for s, t...  19.8 us
    ppermute x8, waiting for transfers between devices, per_device(): across = lambda x: lax.ppermute(x, RING, between)  17.5 us
    ppermute x8, starting transfers between devices, per_device(): across = lambda x: lax.ppermute(x, RING, between)  15.8 us
    ppermute x8, waiting for transfers between devices, per_device(): inside = lambda x: lax.ppermute(x, 'orb', [(0, 1), (1, 0)])  4.34 us
  transfers between devices with their start and end apart: 16, of which 14 were waited for; matrix products, arithmetic and copies ran while one was open for 0% of the time, Pallas kernels for 27%

profile of v7, /device:TPU:0, one launch (start us, length us, event | category | flops | bytes accessed | tf_op | source)
XLA Modules:
  0.0 61.4 jit_solution(5184777038216332113)
XLA Ops:
  1.4 0.7 %add_select_fusion.pair = s32[1280]{0:T(1024)S(1)} fusion(s32[1280]{0:T(1024)} %param.7, s32[1280]{0:T(1024)} %param.8, s32[]{:T(128)} %bitcast.7), kind=kLoop, calls=%fused_computation | loop fusion | flops 5120 | bytes 15364 | tf_op jit(solution)/shard_map/jit(_where)/select_n | solution.py:342
  2.1 1.9 %shard_map.69.crosst = bf16[512,1024]{1,0:T(8,128)(2,1)S(1)} custom-call(bf16[64,1280]{1,0:T(8,128)(2,1)S(1)} %get-tuple-element.55.row_hot, s32[1,1280]{1,0:T(1,128)S(1)} %get-tuple-element.56.cols, bf16[256,1280]{1,0:T(8,128)(2,1)S(1)} %bitcast.8), custom_call_target="tpu_custom_call" | custom-call | flops 1342177280 | bytes 824320 | tf_op jit(solution)/shard_map/pallas_call | solution.py:32
  4.7 4.6 %collective-permute-start = (bf16[528,128]{1,0:T(8,128)(2,1)S(1)}, bf16[528,128]{1,0:T(8,128)(2,1)S(1)}, u32[]{:S(2)}, u32[]{:S(2)}) collective-permute-start(bf16[528,128]{1,0:T(8,128)(2,1)S(1)} %get-tuple-element.57), channel_id=1, source_target_pairs={{1,4},{5,8},{9,12},{13,0},{4,1},{8,5},{12,9},{0,13},{3,6},{7,10},{... | collective-permute-start | bytes 405512 | tf_op jit(solution)/shard_map/ppermute | solution.py:338
  9.3 4.5 %shard_map.71 = (bf16[1024,1024]{1,0:T(8,128)(2,1)S(1)}, bf16[1024,512]{1,0:T(8,128)(2,1)S(1)}, bf16[512,512]{1,0:T(8,128)(2,1)S(1)}, f32[1024,128]{1,0:T(8,128)S(1)}) custom-call(bf16[64,1280]{1,0:T(8,128)(2,1)S(1)} %get-tuple-element.55.row_hot, s32[1,1280]{1,0:T(1,128)S(1)} %get-tuple-element.56.cols, bf16[256,1280]{1,0:T(8,128)(2,1)S(1)} %bitcast.9, ...), custom_call_target="tpu_custom_call" | custom-call | tf_op jit(solution)/shard_map/pallas_call | solution.py:32
  14.3 1.6 %collective-permute-start.2 = (bf16[528,128]{1,0:T(8,128)(2,1)S(1)}, bf16[528,128]{1,0:T(8,128)(2,1)S(1)}, u32[]{:S(2)}, u32[]{:S(2)}) collective-permute-start(bf16[528,128]{1,0:T(8,128)(2,1)S(1)} %shard_map.73._), channel_id=1, source_target_pairs={{1,4},{5,8},{9,12},{13,0},{4,1},{8,5},{12,9},{0,13},{3,6},{7,10},{... | collective-permute-start | bytes 405512 | tf_op jit(solution)/shard_map/ppermute | solution.py:338
  16.5 0.7 %shard_map.75 = (f32[1024,128]{1,0:T(8,128)S(1)}, f32[2,128]{1,0:T(2,128)S(1)}) custom-call(bf16[1024,1024]{1,0:T(8,128)(2,1)S(1)} %get-tuple-element.67.own, bf16[1024,128]{1,0:T(8,128)(2,1)S(1)} %get-tuple-element.68.w, f32[1024,128]{1,0:T(8,128)S(1)} %get-tuple-element.61.previous.refs_0_, f32[1024,128]{1,0:T(8,128)S(1)} %get-tuple-element.69.refs_1_.previous), custom_call_target="tpu_custom_call" | custom-call | tf_op jit(solution)/shard_map/pallas_call | solution.py:32
  18.3 3.1 %collective-permute-done.2.got_x = bf16[528,128]{1,0:T(8,128)(2,1)S(1)} collective-permute-done((bf16[528,128]{1,0:T(8,128)(2,1)S(1)}, bf16[528,128]{1,0:T(8,128)(2,1)S(1)}, u32[]{:S(2)}, u32[]{:S(2)}) %collective-permute-start.2) | collective-permute-done | bytes 135200 | tf_op jit(solution)/shard_map/ppermute | solution.py:338
  21.4 1.1 %collective-permute-start.4 = (bf16[528,128]{1,0:T(8,128)(2,1)S(1)}, bf16[528,128]{1,0:T(8,128)(2,1)S(1)}, u32[]{:S(2)}, u32[]{:S(2)}) collective-permute-start(bf16[528,128]{1,0:T(8,128)(2,1)S(1)} %shard_map.77._), channel_id=1, source_target_pairs={{1,4},{5,8},{9,12},{13,0},{4,1},{8,5},{12,9},{0,13},{3,6},{7,10},{... | collective-permute-start | bytes 405512 | tf_op jit(solution)/shard_map/ppermute | solution.py:338
  23.1 0.7 %shard_map.79 = (f32[1024,128]{1,0:T(8,128)S(1)}, f32[1,128]{1,0:T(1,128)S(1)}) custom-call(bf16[1024,1024]{1,0:T(8,128)(2,1)S(1)} %get-tuple-element.67.own, bf16[1024,128]{1,0:T(8,128)(2,1)S(1)} %get-tuple-element.74.w, f32[1024,128]{1,0:T(8,128)S(1)} %get-tuple-element.61.previous.refs_0_, f32[1024,128]{1,0:T(8,128)S(1)} %get-tuple-element.75.refs_1_.previous), custom_call_target="tpu_custom_call" | custom-call | tf_op jit(solution)/shard_map/pallas_call | solution.py:32
  24.9 2.8 %collective-permute-done.4.got_x = bf16[528,128]{1,0:T(8,128)(2,1)S(1)} collective-permute-done((bf16[528,128]{1,0:T(8,128)(2,1)S(1)}, bf16[528,128]{1,0:T(8,128)(2,1)S(1)}, u32[]{:S(2)}, u32[]{:S(2)}) %collective-permute-start.4) | collective-permute-done | bytes 135200 | tf_op jit(solution)/shard_map/ppermute | solution.py:338
  28.0 1.2 %collective-permute-start.6 = (bf16[528,128]{1,0:T(8,128)(2,1)S(1)}, bf16[528,128]{1,0:T(8,128)(2,1)S(1)}, u32[]{:S(2)}, u32[]{:S(2)}) collective-permute-start(bf16[528,128]{1,0:T(8,128)(2,1)S(1)} %shard_map.81._), channel_id=1, source_target_pairs={{1,4},{5,8},{9,12},{13,0},{4,1},{8,5},{12,9},{0,13},{3,6},{7,10},{... | collective-permute-start | bytes 405512 | tf_op jit(solution)/shard_map/ppermute | solution.py:338
  29.7 0.7 %shard_map.83 = (f32[1024,128]{1,0:T(8,128)S(1)}, f32[3,128]{1,0:T(4,128)S(1)}) custom-call(bf16[1024,1024]{1,0:T(8,128)(2,1)S(1)} %get-tuple-element.67.own, bf16[1024,128]{1,0:T(8,128)(2,1)S(1)} %get-tuple-element.80.w, f32[1024,128]{1,0:T(8,128)S(1)} %get-tuple-element.61.previous.refs_0_, f32[1024,128]{1,0:T(8,128)S(1)} %get-tuple-element.75.refs_1_.previous, ...), custom_call_target="tpu_custom_call" | custom-call | tf_op jit(solution)/shard_map/pallas_call | solution.py:32
  31.5 2.8 %collective-permute-done.6.got_x = bf16[528,128]{1,0:T(8,128)(2,1)S(1)} collective-permute-done((bf16[528,128]{1,0:T(8,128)(2,1)S(1)}, bf16[528,128]{1,0:T(8,128)(2,1)S(1)}, u32[]{:S(2)}, u32[]{:S(2)}) %collective-permute-start.6) | collective-permute-done | bytes 135200 | tf_op jit(solution)/shard_map/ppermute | solution.py:338
  34.4 1.5 %collective-permute-start.8 = (bf16[560,128]{1,0:T(8,128)(2,1)S(1)}, bf16[560,128]{1,0:T(8,128)(2,1)S(1)}, u32[]{:S(2)}, u32[]{:S(2)}) collective-permute-start(bf16[560,128]{1,0:T(8,128)(2,1)S(1)} %shard_map.85._), channel_id=1, source_target_pairs={{1,4},{5,8},{9,12},{13,0},{4,1},{8,5},{12,9},{0,13},{3,6},{7,10},{... | collective-permute-start | bytes 430088 | tf_op jit(solution)/shard_map/ppermute | solution.py:338
  35.9 0.7 %shard_map.86 = (f32[1024,128]{1,0:T(8,128)S(1)}, bf16[1024,128]{1,0:T(8,128)(2,1)S(1)}, bf16[544,128]{1,0:T(8,128)(2,1)S(1)}, f32[9,128]{1,0:T(8,128)S(1)}) custom-call(s32[1]{0:T(128)} %bitcast.parity, bf16[528,128]{1,0:T(8,128)(2,1)S(1)} %collective-permute-done.6.got_x, f32[1024,128]{1,0:T(8,128)S(1)} %get-tuple-element.84.base, ...), custom_call_target="tpu_custom_call" | custom-call | tf_op jit(solution)/shard_map/pallas_call | solution.py:32
  38.4 2.4 %collective-permute-done.8.got_x = bf16[560,128]{1,0:T(8,128)(2,1)S(1)} collective-permute-done((bf16[560,128]{1,0:T(8,128)(2,1)S(1)}, bf16[560,128]{1,0:T(8,128)(2,1)S(1)}, u32[]{:S(2)}, u32[]{:S(2)}) %collective-permute-start.8) | collective-permute-done | bytes 143392 | tf_op jit(solution)/shard_map/ppermute | solution.py:338
  41.0 1.7 %collective-permute-start.10 = (bf16[544,128]{1,0:T(8,128)(2,1)S(1)}, bf16[544,128]{1,0:T(8,128)(2,1)S(1)}, u32[]{:S(2)}, u32[]{:S(2)}) collective-permute-start(bf16[544,128]{1,0:T(8,128)(2,1)S(1)} %shard_map.89._), channel_id=1, source_target_pairs={{1,4},{5,8},{9,12},{13,0},{4,1},{8,5},{12,9},{0,13},{3,6},{7,10},{... | collective-permute-start | bytes 417800 | tf_op jit(solution)/shard_map/ppermute | solution.py:338
  43.3 0.7 %shard_map.91.local = f32[1024,128]{1,0:T(8,128)S(1)} custom-call(bf16[1024,1024]{1,0:T(8,128)(2,1)S(1)} %get-tuple-element.67.own, bf16[1024,128]{1,0:T(8,128)(2,1)S(1)} %get-tuple-element.94.w), custom_call_target="tpu_custom_call" | custom-call | tf_op jit(solution)/shard_map/pallas_call | solution.py:32
  45.1 2.4 %collective-permute-done.10.got_x.refs_1_ = bf16[544,128]{1,0:T(8,128)(2,1)S(1)} collective-permute-done((bf16[544,128]{1,0:T(8,128)(2,1)S(1)}, bf16[544,128]{1,0:T(8,128)(2,1)S(1)}, u32[]{:S(2)}, u32[]{:S(2)}) %collective-permute-start.10) | collective-permute-done | bytes 139296 | tf_op jit(solution)/shard_map/ppermute | solution.py:338
  47.5 2.0 %collective-permute-start.12 = (bf16[560,128]{1,0:T(8,128)(2,1)S(1)}, bf16[560,128]{1,0:T(8,128)(2,1)S(1)}, u32[]{:S(2)}, u32[]{:S(2)}) collective-permute-start(bf16[560,128]{1,0:T(8,128)(2,1)S(1)} %shard_map.93._), channel_id=1, source_target_pairs={{1,4},{5,8},{9,12},{13,0},{4,1},{8,5},{12,9},{0,13},{3,6},{7,10},{... | collective-permute-start | bytes 430088 | tf_op jit(solution)/shard_map/ppermute | solution.py:338
  51.8 2.1 %collective-permute-done.12.got_x = bf16[560,128]{1,0:T(8,128)(2,1)S(1)} collective-permute-done((bf16[560,128]{1,0:T(8,128)(2,1)S(1)}, bf16[560,128]{1,0:T(8,128)(2,1)S(1)}, u32[]{:S(2)}, u32[]{:S(2)}) %collective-permute-start.12) | collective-permute-done | bytes 143392 | tf_op jit(solution)/shard_map/ppermute | solution.py:338
  54.0 2.2 %collective-permute-start.14 = (bf16[544,128]{1,0:T(8,128)(2,1)S(1)}, bf16[544,128]{1,0:T(8,128)(2,1)S(1)}, u32[]{:S(2)}, u32[]{:S(2)}) collective-permute-start(bf16[544,128]{1,0:T(8,128)(2,1)S(1)} %shard_map.97._), channel_id=1, source_target_pairs={{1,4},{5,8},{9,12},{13,0},{4,1},{8,5},{12,9},{0,13},{3,6},{7,10},{... | collective-permute-start | bytes 417800 | tf_op jit(solution)/shard_map/ppermute | solution.py:338
  58.6 1.8 %collective-permute-done.14.got_x.refs_3_ = bf16[544,128]{1,0:T(8,128)(2,1)S(1)} collective-permute-done((bf16[544,128]{1,0:T(8,128)(2,1)S(1)}, bf16[544,128]{1,0:T(8,128)(2,1)S(1)}, u32[]{:S(2)}, u32[]{:S(2)}) %collective-permute-start.14) | collective-permute-done | bytes 139296 | tf_op jit(solution)/shard_map/ppermute | solution.py:338
  60.3 1.0 %shard_map.101 = (f32[1024,128]{1,0:T(8,128)}, f32[9,128]{1,0:T(8,128)}) custom-call(s32[1]{0:T(128)} %bitcast.parity, bf16[544,128]{1,0:T(8,128)(2,1)S(1)} %collective-permute-done.14.got_x.refs_3_, f32[1024,128]{1,0:T(8,128)S(1)} %shard_map.100.base, bf16[1024,512]{1,0:T(8,128)(2,1)S(1)} %get-tuple-element.62.cross, ...), custom_call_target="tpu_custom_call" | custom-call | tf_op jit(solution)/shard_map/pallas_call | solution.py:422
  (47 shorter events, 14.6 us)
Async XLA Ops:
  0.6 1.5 %copy-start = (bf16[1280,16,16]{0,2,1:T(8,128)(2,1)S(1)}, bf16[1280,16,16]{0,2,1:T(8,128)(2,1)}, u32[]{:S(2)}) copy-start(bf16[1280,16,16]{0,2,1:T(8,128)(2,1)} %param.6) | copy-start | bytes 1966084
  2.1 2.0 %copy-start.1 = (f32[64,16,128]{2,1,0:T(8,128)S(1)}, f32[64,16,128]{2,1,0:T(8,128)}, u32[]{:S(2)}) copy-start(f32[64,16,128]{2,1,0:T(8,128)} %param.5) | copy-start | bytes 1572868
  4.7 9.5 %collective-permute-start = (bf16[528,128]{1,0:T(8,128)(2,1)S(1)}, bf16[528,128]{1,0:T(8,128)(2,1)S(1)}, u32[]{:S(2)}, u32[]{:S(2)}) collective-permute-start(bf16[528,128]{1,0:T(8,128)(2,1)S(1)} %get-tuple-element.57), channel_id=1, source_target_pairs={{1,4},{5,8},{9,12},{13,0},{4,1},{8,5},{12,9},{0,13},{3,6},{7,10},{... | collective-permute-start | bytes 405512 | tf_op jit(solution)/shard_map/ppermute | solution.py:338
  9.3 4.5 %collective-permute-start.1 = (bf16[512,128]{1,0:T(8,128)(2,1)S(1)}, bf16[512,128]{1,0:T(8,128)(2,1)S(1)}, u32[]{:S(2)}, u32[]{:S(2)}) collective-permute-start(bf16[512,128]{1,0:T(8,128)(2,1)S(1)} %get-tuple-element.58._), channel_id=1, source_target_pairs={{0,1},{1,0},{2,3},{3,2},{4,5},{5,4},{6,7},{7,6},{8,9},{9,8},{10,11... | collective-permute-start | bytes 393224 | tf_op jit(solution)/shard_map/ppermute | solution.py:339
  14.3 7.1 %collective-permute-start.2 = (bf16[528,128]{1,0:T(8,128)(2,1)S(1)}, bf16[528,128]{1,0:T(8,128)(2,1)S(1)}, u32[]{:S(2)}, u32[]{:S(2)}) collective-permute-start(bf16[528,128]{1,0:T(8,128)(2,1)S(1)} %shard_map.73._), channel_id=1, source_target_pairs={{1,4},{5,8},{9,12},{13,0},{4,1},{8,5},{12,9},{0,13},{3,6},{7,10},{... | collective-permute-start | bytes 405512 | tf_op jit(solution)/shard_map/ppermute | solution.py:338
  16.4 1.4 %collective-permute-start.3 = (bf16[512,128]{1,0:T(8,128)(2,1)S(1)}, bf16[512,128]{1,0:T(8,128)(2,1)S(1)}, u32[]{:S(2)}, u32[]{:S(2)}) collective-permute-start(bf16[512,128]{1,0:T(8,128)(2,1)S(1)} %get-tuple-element.66), channel_id=1, source_target_pairs={{0,1},{1,0},{2,3},{3,2},{4,5},{5,4},{6,7},{7,6},{8,9},{9,8},{10,11... | collective-permute-start | bytes 393224 | tf_op jit(solution)/shard_map/ppermute | solution.py:339
  21.4 6.3 %collective-permute-start.4 = (bf16[528,128]{1,0:T(8,128)(2,1)S(1)}, bf16[528,128]{1,0:T(8,128)(2,1)S(1)}, u32[]{:S(2)}, u32[]{:S(2)}) collective-permute-start(bf16[528,128]{1,0:T(8,128)(2,1)S(1)} %shard_map.77._), channel_id=1, source_target_pairs={{1,4},{5,8},{9,12},{13,0},{4,1},{8,5},{12,9},{0,13},{3,6},{7,10},{... | collective-permute-start | bytes 405512 | tf_op jit(solution)/shard_map/ppermute | solution.py:338
  23.0 1.4 %collective-permute-start.5 = (bf16[512,128]{1,0:T(8,128)(2,1)S(1)}, bf16[512,128]{1,0:T(8,128)(2,1)S(1)}, u32[]{:S(2)}, u32[]{:S(2)}) collective-permute-start(bf16[512,128]{1,0:T(8,128)(2,1)S(1)} %get-tuple-element.73), channel_id=1, source_target_pairs={{0,1},{1,0},{2,3},{3,2},{4,5},{5,4},{6,7},{7,6},{8,9},{9,8},{10,11... | collective-permute-start | bytes 393224 | tf_op jit(solution)/shard_map/ppermute | solution.py:339
  28.0 6.4 %collective-permute-start.6 = (bf16[528,128]{1,0:T(8,128)(2,1)S(1)}, bf16[528,128]{1,0:T(8,128)(2,1)S(1)}, u32[]{:S(2)}, u32[]{:S(2)}) collective-permute-start(bf16[528,128]{1,0:T(8,128)(2,1)S(1)} %shard_map.81._), channel_id=1, source_target_pairs={{1,4},{5,8},{9,12},{13,0},{4,1},{8,5},{12,9},{0,13},{3,6},{7,10},{... | collective-permute-start | bytes 405512 | tf_op jit(solution)/shard_map/ppermute | solution.py:338
  29.7 1.4 %collective-permute-start.7 = (bf16[512,128]{1,0:T(8,128)(2,1)S(1)}, bf16[512,128]{1,0:T(8,128)(2,1)S(1)}, u32[]{:S(2)}, u32[]{:S(2)}) collective-permute-start(bf16[512,128]{1,0:T(8,128)(2,1)S(1)} %get-tuple-element.79), channel_id=1, source_target_pairs={{0,1},{1,0},{2,3},{3,2},{4,5},{5,4},{6,7},{7,6},{8,9},{9,8},{10,11... | collective-permute-start | bytes 393224 | tf_op jit(solution)/shard_map/ppermute | solution.py:339
  34.4 6.5 %collective-permute-start.8 = (bf16[560,128]{1,0:T(8,128)(2,1)S(1)}, bf16[560,128]{1,0:T(8,128)(2,1)S(1)}, u32[]{:S(2)}, u32[]{:S(2)}) collective-permute-start(bf16[560,128]{1,0:T(8,128)(2,1)S(1)} %shard_map.85._), channel_id=1, source_target_pairs={{1,4},{5,8},{9,12},{13,0},{4,1},{8,5},{12,9},{0,13},{3,6},{7,10},{... | collective-permute-start | bytes 430088 | tf_op jit(solution)/shard_map/ppermute | solution.py:338
  36.6 1.4 %collective-permute-start.9 = (bf16[544,128]{1,0:T(8,128)(2,1)S(1)}, bf16[544,128]{1,0:T(8,128)(2,1)S(1)}, u32[]{:S(2)}, u32[]{:S(2)}) collective-permute-start(bf16[544,128]{1,0:T(8,128)(2,1)S(1)} %get-tuple-element.88), channel_id=1, source_target_pairs={{0,1},{1,0},{2,3},{3,2},{4,5},{5,4},{6,7},{7,6},{8,9},{9,8},{10,11... | collective-permute-start | bytes 417800 | tf_op jit(solution)/shard_map/ppermute | solution.py:339
  41.0 6.4 %collective-permute-start.10 = (bf16[544,128]{1,0:T(8,128)(2,1)S(1)}, bf16[544,128]{1,0:T(8,128)(2,1)S(1)}, u32[]{:S(2)}, u32[]{:S(2)}) collective-permute-start(bf16[544,128]{1,0:T(8,128)(2,1)S(1)} %shard_map.89._), channel_id=1, source_target_pairs={{1,4},{5,8},{9,12},{13,0},{4,1},{8,5},{12,9},{0,13},{3,6},{7,10},{... | collective-permute-start | bytes 417800 | tf_op jit(solution)/shard_map/ppermute | solution.py:338
  43.2 1.4 %collective-permute-start.11 = (bf16[512,128]{1,0:T(8,128)(2,1)S(1)}, bf16[512,128]{1,0:T(8,128)(2,1)S(1)}, u32[]{:S(2)}, u32[]{:S(2)}) collective-permute-start(bf16[512,128]{1,0:T(8,128)(2,1)S(1)} %get-tuple-element.93), channel_id=1, source_target_pairs={{0,1},{1,0},{2,3},{3,2},{4,5},{5,4},{6,7},{7,6},{8,9},{9,8},{10,11... | collective-permute-start | bytes 393224 | tf_op jit(solution)/shard_map/ppermute | solution.py:339
  47.5 6.5 %collective-permute-start.12 = (bf16[560,128]{1,0:T(8,128)(2,1)S(1)}, bf16[560,128]{1,0:T(8,128)(2,1)S(1)}, u32[]{:S(2)}, u32[]{:S(2)}) collective-permute-start(bf16[560,128]{1,0:T(8,128)(2,1)S(1)} %shard_map.93._), channel_id=1, source_target_pairs={{1,4},{5,8},{9,12},{13,0},{4,1},{8,5},{12,9},{0,13},{3,6},{7,10},{... | collective-permute-start | bytes 430088 | tf_op jit(solution)/shard_map/ppermute | solution.py:338
  49.9 1.4 %collective-permute-start.13 = (bf16[544,128]{1,0:T(8,128)(2,1)S(1)}, bf16[544,128]{1,0:T(8,128)(2,1)S(1)}, u32[]{:S(2)}, u32[]{:S(2)}) collective-permute-start(bf16[544,128]{1,0:T(8,128)(2,1)S(1)} %get-tuple-element.98), channel_id=1, source_target_pairs={{0,1},{1,0},{2,3},{3,2},{4,5},{5,4},{6,7},{7,6},{8,9},{9,8},{10,11... | collective-permute-start | bytes 417800 | tf_op jit(solution)/shard_map/ppermute | solution.py:339
  54.0 6.3 %collective-permute-start.14 = (bf16[544,128]{1,0:T(8,128)(2,1)S(1)}, bf16[544,128]{1,0:T(8,128)(2,1)S(1)}, u32[]{:S(2)}, u32[]{:S(2)}) collective-permute-start(bf16[544,128]{1,0:T(8,128)(2,1)S(1)} %shard_map.97._), channel_id=1, source_target_pairs={{1,4},{5,8},{9,12},{13,0},{4,1},{8,5},{12,9},{0,13},{3,6},{7,10},{... | collective-permute-start | bytes 417800 | tf_op jit(solution)/shard_map/ppermute | solution.py:338
  56.7 1.4 %collective-permute-start.15 = (bf16[512,128]{1,0:T(8,128)(2,1)S(1)}, bf16[512,128]{1,0:T(8,128)(2,1)S(1)}, u32[]{:S(2)}, u32[]{:S(2)}) collective-permute-start(bf16[512,128]{1,0:T(8,128)(2,1)S(1)} %get-tuple-element.103), channel_id=1, source_target_pairs={{0,1},{1,0},{2,3},{3,2},{4,5},{5,4},{6,7},{7,6},{8,9},{9,8},{10,11... | collective-permute-start | bytes 393224 | tf_op jit(solution)/shard_map/ppermute | solution.py:339

commit v8 on v6

--- a/solution.py
+++ b/solution.py
@@ -91,7 +91,7 @@
 
 def own_body(atoms, orbits, halo, row_hot, cols, blocks, crosst, w, _, own_ref, cross_ref, gram_ref, local_ref, own_f32):
     place(atoms, orbits, 0, atoms, row_hot, cols, blocks, own_f32)
-    gram_ref[...] = lax.dot_general(crosst[...], crosst[...], NT, preferred_element_type=F32).astype(BF16)
+    gram_ref[...] = (2.0 * lax.dot_general(crosst[...], crosst[...], NT, preferred_element_type=F32)).astype(BF16)
     lanes = 2 * atoms
     for p in range(orbits // 2):
         at = slice(p * lanes, (p + 1) * lanes)
@@ -209,7 +209,8 @@
 
     @pl.when(parity[0] != 0)
     def _():
-        out[:edge_size, :] = (pre[...] + factor * times(gram, got_x[:edge_size, :])).astype(BF16)
+        product = times(gram, got_x[:edge_size, :])
+        out[:edge_size, :] = (pre[...] + (0.5 * product if k == 0 else product)).astype(BF16)
 
     if tail == "sum":
         table, got = refs[:-1]

time: 61.6 us -> 61.6 us (level)
  no operation moved by 1% of the time
where the time goes in v8:
time: 61.6 us; the launch traced here: 61.3 us
  waiting for transfers between devices  21.8 us (35%)
  Pallas kernels  20.8 us (34%)
  starting transfers between devices  16.3 us (26%)
  between operations  1.68 us (3%)
  other arithmetic  0.72 us (1%)
    pallas_call x34, Pallas kernels, call(): pl.pallas_call(body, out_shape=tuple((jax.ShapeDtypeStruct(s, t) for s, t...  20.8 us
    ppermute x8, waiting for transfers between devices, per_device(): across = lambda x: lax.ppermute(x, RING, between)  17.5 us
    ppermute x8, starting transfers between devices, per_device(): across = lambda x: lax.ppermute(x, RING, between)  15.8 us
    ppermute x8, waiting for transfers between devices, per_device(): inside = lambda x: lax.ppermute(x, 'orb', [(0, 1), (1, 0)])  4.34 us
  transfers between devices with their start and end apart: 16, of which 14 were waited for; matrix products, arithmetic and copies ran while one was open for 0% of the time, Pallas kernels for 27%

profile of v8, /device:TPU:0, one launch (start us, length us, event | category | flops | bytes accessed | tf_op | source)
XLA Modules:
  0.0 61.3 jit_solution(8684418498153540530)
XLA Ops:
  1.4 0.7 %add_select_fusion.pair = s32[1280]{0:T(1024)S(1)} fusion(s32[1280]{0:T(1024)} %param.7, s32[1280]{0:T(1024)} %param.8, s32[]{:T(128)} %bitcast.7), kind=kLoop, calls=%fused_computation | loop fusion | flops 5120 | bytes 15364 | tf_op jit(solution)/shard_map/jit(_where)/select_n | solution.py:309
  2.1 1.9 %shard_map.69.crosst = bf16[512,1024]{1,0:T(8,128)(2,1)S(1)} custom-call(bf16[64,1280]{1,0:T(8,128)(2,1)S(1)} %get-tuple-element.55.row_hot, s32[1,1280]{1,0:T(1,128)S(1)} %get-tuple-element.56.cols, bf16[256,1280]{1,0:T(8,128)(2,1)S(1)} %bitcast.8), custom_call_target="tpu_custom_call" | custom-call | flops 1342177280 | bytes 824320 | tf_op jit(solution)/shard_map/pallas_call | solution.py:32
  4.7 4.6 %collective-permute-start = (bf16[528,128]{1,0:T(8,128)(2,1)S(1)}, bf16[528,128]{1,0:T(8,128)(2,1)S(1)}, u32[]{:S(2)}, u32[]{:S(2)}) collective-permute-start(bf16[528,128]{1,0:T(8,128)(2,1)S(1)} %get-tuple-element.57), channel_id=1, source_target_pairs={{1,4},{5,8},{9,12},{13,0},{4,1},{8,5},{12,9},{0,13},{3,6},{7,10},{... | collective-permute-start | bytes 405512 | tf_op jit(solution)/shard_map/ppermute | solution.py:305
  9.3 4.5 %shard_map.71 = (bf16[1024,1024]{1,0:T(8,128)(2,1)S(1)}, bf16[1024,512]{1,0:T(8,128)(2,1)S(1)}, bf16[512,512]{1,0:T(8,128)(2,1)S(1)}, f32[1024,128]{1,0:T(8,128)S(1)}) custom-call(bf16[64,1280]{1,0:T(8,128)(2,1)S(1)} %get-tuple-element.55.row_hot, s32[1,1280]{1,0:T(1,128)S(1)} %get-tuple-element.56.cols, bf16[256,1280]{1,0:T(8,128)(2,1)S(1)} %bitcast.9, ...), custom_call_target="tpu_custom_call" | custom-call | tf_op jit(solution)/shard_map/pallas_call | solution.py:32
  14.3 1.6 %collective-permute-start.2 = (bf16[528,128]{1,0:T(8,128)(2,1)S(1)}, bf16[528,128]{1,0:T(8,128)(2,1)S(1)}, u32[]{:S(2)}, u32[]{:S(2)}) collective-permute-start(bf16[528,128]{1,0:T(8,128)(2,1)S(1)} %shard_map.73._), channel_id=1, source_target_pairs={{1,4},{5,8},{9,12},{13,0},{4,1},{8,5},{12,9},{0,13},{3,6},{7,10},{... | collective-permute-start | bytes 405512 | tf_op jit(solution)/shard_map/ppermute | solution.py:305
  16.5 0.7 %shard_map.75 = (f32[1024,128]{1,0:T(8,128)S(1)}, f32[2,128]{1,0:T(2,128)S(1)}) custom-call(bf16[1024,1024]{1,0:T(8,128)(2,1)S(1)} %get-tuple-element.67.own, bf16[1024,128]{1,0:T(8,128)(2,1)S(1)} %get-tuple-element.68.w, f32[1024,128]{1,0:T(8,128)S(1)} %get-tuple-element.61.previous.refs_0_, f32[1024,128]{1,0:T(8,128)S(1)} %get-tuple-element.69.refs_1_.previous), custom_call_target="tpu_custom_call" | custom-call | tf_op jit(solution)/shard_map/pallas_call | solution.py:32
  18.3 3.1 %collective-permute-done.2.got_x = bf16[528,128]{1,0:T(8,128)(2,1)S(1)} collective-permute-done((bf16[528,128]{1,0:T(8,128)(2,1)S(1)}, bf16[528,128]{1,0:T(8,128)(2,1)S(1)}, u32[]{:S(2)}, u32[]{:S(2)}) %collective-permute-start.2) | collective-permute-done | bytes 135200 | tf_op jit(solution)/shard_map/ppermute | solution.py:305
  21.4 1.1 %collective-permute-start.4 = (bf16[528,128]{1,0:T(8,128)(2,1)S(1)}, bf16[528,128]{1,0:T(8,128)(2,1)S(1)}, u32[]{:S(2)}, u32[]{:S(2)}) collective-permute-start(bf16[528,128]{1,0:T(8,128)(2,1)S(1)} %shard_map.77._), channel_id=1, source_target_pairs={{1,4},{5,8},{9,12},{13,0},{4,1},{8,5},{12,9},{0,13},{3,6},{7,10},{... | collective-permute-start | bytes 405512 | tf_op jit(solution)/shard_map/ppermute | solution.py:305
  23.1 0.7 %shard_map.79 = (f32[1024,128]{1,0:T(8,128)S(1)}, f32[1,128]{1,0:T(1,128)S(1)}) custom-call(bf16[1024,1024]{1,0:T(8,128)(2,1)S(1)} %get-tuple-element.67.own, bf16[1024,128]{1,0:T(8,128)(2,1)S(1)} %get-tuple-element.74.w, f32[1024,128]{1,0:T(8,128)S(1)} %get-tuple-element.61.previous.refs_0_, f32[1024,128]{1,0:T(8,128)S(1)} %get-tuple-element.75.refs_1_.previous), custom_call_target="tpu_custom_call" | custom-call | tf_op jit(solution)/shard_map/pallas_call | solution.py:32
  24.9 2.8 %collective-permute-done.4.got_x = bf16[528,128]{1,0:T(8,128)(2,1)S(1)} collective-permute-done((bf16[528,128]{1,0:T(8,128)(2,1)S(1)}, bf16[528,128]{1,0:T(8,128)(2,1)S(1)}, u32[]{:S(2)}, u32[]{:S(2)}) %collective-permute-start.4) | collective-permute-done | bytes 135200 | tf_op jit(solution)/shard_map/ppermute | solution.py:305
  28.0 1.2 %collective-permute-start.6 = (bf16[528,128]{1,0:T(8,128)(2,1)S(1)}, bf16[528,128]{1,0:T(8,128)(2,1)S(1)}, u32[]{:S(2)}, u32[]{:S(2)}) collective-permute-start(bf16[528,128]{1,0:T(8,128)(2,1)S(1)} %shard_map.81._), channel_id=1, source_target_pairs={{1,4},{5,8},{9,12},{13,0},{4,1},{8,5},{12,9},{0,13},{3,6},{7,10},{... | collective-permute-start | bytes 405512 | tf_op jit(solution)/shard_map/ppermute | solution.py:305
  29.7 0.7 %shard_map.83 = (f32[1024,128]{1,0:T(8,128)S(1)}, f32[3,128]{1,0:T(4,128)S(1)}) custom-call(bf16[1024,1024]{1,0:T(8,128)(2,1)S(1)} %get-tuple-element.67.own, bf16[1024,128]{1,0:T(8,128)(2,1)S(1)} %get-tuple-element.80.w, f32[1024,128]{1,0:T(8,128)S(1)} %get-tuple-element.61.previous.refs_0_, f32[1024,128]{1,0:T(8,128)S(1)} %get-tuple-element.75.refs_1_.previous, ...), custom_call_target="tpu_custom_call" | custom-call | tf_op jit(solution)/shard_map/pallas_call | solution.py:32
  31.5 2.8 %collective-permute-done.6.got_x = bf16[528,128]{1,0:T(8,128)(2,1)S(1)} collective-permute-done((bf16[528,128]{1,0:T(8,128)(2,1)S(1)}, bf16[528,128]{1,0:T(8,128)(2,1)S(1)}, u32[]{:S(2)}, u32[]{:S(2)}) %collective-permute-start.6) | collective-permute-done | bytes 135200 | tf_op jit(solution)/shard_map/ppermute | solution.py:305
  34.4 1.5 %collective-permute-start.8 = (bf16[560,128]{1,0:T(8,128)(2,1)S(1)}, bf16[560,128]{1,0:T(8,128)(2,1)S(1)}, u32[]{:S(2)}, u32[]{:S(2)}) collective-permute-start(bf16[560,128]{1,0:T(8,128)(2,1)S(1)} %shard_map.85._), channel_id=1, source_target_pairs={{1,4},{5,8},{9,12},{13,0},{4,1},{8,5},{12,9},{0,13},{3,6},{7,10},{... | collective-permute-start | bytes 430088 | tf_op jit(solution)/shard_map/ppermute | solution.py:305
  35.9 0.7 %shard_map.86 = (f32[1024,128]{1,0:T(8,128)S(1)}, bf16[1024,128]{1,0:T(8,128)(2,1)S(1)}, bf16[544,128]{1,0:T(8,128)(2,1)S(1)}, f32[9,128]{1,0:T(8,128)S(1)}) custom-call(s32[1]{0:T(128)} %bitcast.parity, bf16[528,128]{1,0:T(8,128)(2,1)S(1)} %collective-permute-done.6.got_x, f32[1024,128]{1,0:T(8,128)S(1)} %get-tuple-element.84.base, ...), custom_call_target="tpu_custom_call" | custom-call | tf_op jit(solution)/shard_map/pallas_call | solution.py:32
  38.4 2.5 %collective-permute-done.8.got_x = bf16[560,128]{1,0:T(8,128)(2,1)S(1)} collective-permute-done((bf16[560,128]{1,0:T(8,128)(2,1)S(1)}, bf16[560,128]{1,0:T(8,128)(2,1)S(1)}, u32[]{:S(2)}, u32[]{:S(2)}) %collective-permute-start.8) | collective-permute-done | bytes 143392 | tf_op jit(solution)/shard_map/ppermute | solution.py:305
  41.0 1.7 %collective-permute-start.10 = (bf16[544,128]{1,0:T(8,128)(2,1)S(1)}, bf16[544,128]{1,0:T(8,128)(2,1)S(1)}, u32[]{:S(2)}, u32[]{:S(2)}) collective-permute-start(bf16[544,128]{1,0:T(8,128)(2,1)S(1)} %shard_map.89._), channel_id=1, source_target_pairs={{1,4},{5,8},{9,12},{13,0},{4,1},{8,5},{12,9},{0,13},{3,6},{7,10},{... | collective-permute-start | bytes 417800 | tf_op jit(solution)/shard_map/ppermute | solution.py:305
  43.3 0.7 %shard_map.91.local = f32[1024,128]{1,0:T(8,128)S(1)} custom-call(bf16[1024,1024]{1,0:T(8,128)(2,1)S(1)} %get-tuple-element.67.own, bf16[1024,128]{1,0:T(8,128)(2,1)S(1)} %get-tuple-element.94.w), custom_call_target="tpu_custom_call" | custom-call | tf_op jit(solution)/shard_map/pallas_call | solution.py:32
  45.0 2.4 %collective-permute-done.10.got_x.refs_1_ = bf16[544,128]{1,0:T(8,128)(2,1)S(1)} collective-permute-done((bf16[544,128]{1,0:T(8,128)(2,1)S(1)}, bf16[544,128]{1,0:T(8,128)(2,1)S(1)}, u32[]{:S(2)}, u32[]{:S(2)}) %collective-permute-start.10) | collective-permute-done | bytes 139296 | tf_op jit(solution)/shard_map/ppermute | solution.py:305
  47.5 2.0 %collective-permute-start.12 = (bf16[560,128]{1,0:T(8,128)(2,1)S(1)}, bf16[560,128]{1,0:T(8,128)(2,1)S(1)}, u32[]{:S(2)}, u32[]{:S(2)}) collective-permute-start(bf16[560,128]{1,0:T(8,128)(2,1)S(1)} %shard_map.93._), channel_id=1, source_target_pairs={{1,4},{5,8},{9,12},{13,0},{4,1},{8,5},{12,9},{0,13},{3,6},{7,10},{... | collective-permute-start | bytes 430088 | tf_op jit(solution)/shard_map/ppermute | solution.py:305
  51.8 2.1 %collective-permute-done.12.got_x = bf16[560,128]{1,0:T(8,128)(2,1)S(1)} collective-permute-done((bf16[560,128]{1,0:T(8,128)(2,1)S(1)}, bf16[560,128]{1,0:T(8,128)(2,1)S(1)}, u32[]{:S(2)}, u32[]{:S(2)}) %collective-permute-start.12) | collective-permute-done | bytes 143392 | tf_op jit(solution)/shard_map/ppermute | solution.py:305
  54.0 2.2 %collective-permute-start.14 = (bf16[544,128]{1,0:T(8,128)(2,1)S(1)}, bf16[544,128]{1,0:T(8,128)(2,1)S(1)}, u32[]{:S(2)}, u32[]{:S(2)}) collective-permute-start(bf16[544,128]{1,0:T(8,128)(2,1)S(1)} %shard_map.97._), channel_id=1, source_target_pairs={{1,4},{5,8},{9,12},{13,0},{4,1},{8,5},{12,9},{0,13},{3,6},{7,10},{... | collective-permute-start | bytes 417800 | tf_op jit(solution)/shard_map/ppermute | solution.py:305
  58.6 1.8 %collective-permute-done.14.got_x.refs_3_ = bf16[544,128]{1,0:T(8,128)(2,1)S(1)} collective-permute-done((bf16[544,128]{1,0:T(8,128)(2,1)S(1)}, bf16[544,128]{1,0:T(8,128)(2,1)S(1)}, u32[]{:S(2)}, u32[]{:S(2)}) %collective-permute-start.14) | collective-permute-done | bytes 139296 | tf_op jit(solution)/shard_map/ppermute | solution.py:305
  60.3 1.0 %shard_map.101 = (f32[1024,128]{1,0:T(8,128)}, f32[9,128]{1,0:T(8,128)}) custom-call(s32[1]{0:T(128)} %bitcast.parity, bf16[544,128]{1,0:T(8,128)(2,1)S(1)} %collective-permute-done.14.got_x.refs_3_, f32[1024,128]{1,0:T(8,128)S(1)} %shard_map.100.base, bf16[1024,512]{1,0:T(8,128)(2,1)S(1)} %get-tuple-element.62.cross, ...), custom_call_target="tpu_custom_call" | custom-call | tf_op jit(solution)/shard_map/pallas_call | solution.py:32
  (47 shorter events, 14.7 us)
Async XLA Ops:
  0.6 1.5 %copy-start = (bf16[1280,16,16]{0,2,1:T(8,128)(2,1)S(1)}, bf16[1280,16,16]{0,2,1:T(8,128)(2,1)}, u32[]{:S(2)}) copy-start(bf16[1280,16,16]{0,2,1:T(8,128)(2,1)} %param.6) | copy-start | bytes 1966084
  2.1 2.0 %copy-start.1 = (f32[64,16,128]{2,1,0:T(8,128)S(1)}, f32[64,16,128]{2,1,0:T(8,128)}, u32[]{:S(2)}) copy-start(f32[64,16,128]{2,1,0:T(8,128)} %param.5) | copy-start | bytes 1572868
  4.7 9.5 %collective-permute-start = (bf16[528,128]{1,0:T(8,128)(2,1)S(1)}, bf16[528,128]{1,0:T(8,128)(2,1)S(1)}, u32[]{:S(2)}, u32[]{:S(2)}) collective-permute-start(bf16[528,128]{1,0:T(8,128)(2,1)S(1)} %get-tuple-element.57), channel_id=1, source_target_pairs={{1,4},{5,8},{9,12},{13,0},{4,1},{8,5},{12,9},{0,13},{3,6},{7,10},{... | collective-permute-start | bytes 405512 | tf_op jit(solution)/shard_map/ppermute | solution.py:305
  9.3 4.5 %collective-permute-start.1 = (bf16[512,128]{1,0:T(8,128)(2,1)S(1)}, bf16[512,128]{1,0:T(8,128)(2,1)S(1)}, u32[]{:S(2)}, u32[]{:S(2)}) collective-permute-start(bf16[512,128]{1,0:T(8,128)(2,1)S(1)} %get-tuple-element.58._), channel_id=1, source_target_pairs={{0,1},{1,0},{2,3},{3,2},{4,5},{5,4},{6,7},{7,6},{8,9},{9,8},{10,11... | collective-permute-start | bytes 393224 | tf_op jit(solution)/shard_map/ppermute | solution.py:306
  14.3 7.1 %collective-permute-start.2 = (bf16[528,128]{1,0:T(8,128)(2,1)S(1)}, bf16[528,128]{1,0:T(8,128)(2,1)S(1)}, u32[]{:S(2)}, u32[]{:S(2)}) collective-permute-start(bf16[528,128]{1,0:T(8,128)(2,1)S(1)} %shard_map.73._), channel_id=1, source_target_pairs={{1,4},{5,8},{9,12},{13,0},{4,1},{8,5},{12,9},{0,13},{3,6},{7,10},{... | collective-permute-start | bytes 405512 | tf_op jit(solution)/shard_map/ppermute | solution.py:305
  16.4 1.4 %collective-permute-start.3 = (bf16[512,128]{1,0:T(8,128)(2,1)S(1)}, bf16[512,128]{1,0:T(8,128)(2,1)S(1)}, u32[]{:S(2)}, u32[]{:S(2)}) collective-permute-start(bf16[512,128]{1,0:T(8,128)(2,1)S(1)} %get-tuple-element.66), channel_id=1, source_target_pairs={{0,1},{1,0},{2,3},{3,2},{4,5},{5,4},{6,7},{7,6},{8,9},{9,8},{10,11... | collective-permute-start | bytes 393224 | tf_op jit(solution)/shard_map/ppermute | solution.py:306
  21.4 6.3 %collective-permute-start.4 = (bf16[528,128]{1,0:T(8,128)(2,1)S(1)}, bf16[528,128]{1,0:T(8,128)(2,1)S(1)}, u32[]{:S(2)}, u32[]{:S(2)}) collective-permute-start(bf16[528,128]{1,0:T(8,128)(2,1)S(1)} %shard_map.77._), channel_id=1, source_target_pairs={{1,4},{5,8},{9,12},{13,0},{4,1},{8,5},{12,9},{0,13},{3,6},{7,10},{... | collective-permute-start | bytes 405512 | tf_op jit(solution)/shard_map/ppermute | solution.py:305
  23.0 1.4 %collective-permute-start.5 = (bf16[512,128]{1,0:T(8,128)(2,1)S(1)}, bf16[512,128]{1,0:T(8,128)(2,1)S(1)}, u32[]{:S(2)}, u32[]{:S(2)}) collective-permute-start(bf16[512,128]{1,0:T(8,128)(2,1)S(1)} %get-tuple-element.73), channel_id=1, source_target_pairs={{0,1},{1,0},{2,3},{3,2},{4,5},{5,4},{6,7},{7,6},{8,9},{9,8},{10,11... | collective-permute-start | bytes 393224 | tf_op jit(solution)/shard_map/ppermute | solution.py:306
  28.0 6.4 %collective-permute-start.6 = (bf16[528,128]{1,0:T(8,128)(2,1)S(1)}, bf16[528,128]{1,0:T(8,128)(2,1)S(1)}, u32[]{:S(2)}, u32[]{:S(2)}) collective-permute-start(bf16[528,128]{1,0:T(8,128)(2,1)S(1)} %shard_map.81._), channel_id=1, source_target_pairs={{1,4},{5,8},{9,12},{13,0},{4,1},{8,5},{12,9},{0,13},{3,6},{7,10},{... | collective-permute-start | bytes 405512 | tf_op jit(solution)/shard_map/ppermute | solution.py:305
  29.7 1.4 %collective-permute-start.7 = (bf16[512,128]{1,0:T(8,128)(2,1)S(1)}, bf16[512,128]{1,0:T(8,128)(2,1)S(1)}, u32[]{:S(2)}, u32[]{:S(2)}) collective-permute-start(bf16[512,128]{1,0:T(8,128)(2,1)S(1)} %get-tuple-element.79), channel_id=1, source_target_pairs={{0,1},{1,0},{2,3},{3,2},{4,5},{5,4},{6,7},{7,6},{8,9},{9,8},{10,11... | collective-permute-start | bytes 393224 | tf_op jit(solution)/shard_map/ppermute | solution.py:306
  34.4 6.5 %collective-permute-start.8 = (bf16[560,128]{1,0:T(8,128)(2,1)S(1)}, bf16[560,128]{1,0:T(8,128)(2,1)S(1)}, u32[]{:S(2)}, u32[]{:S(2)}) collective-permute-start(bf16[560,128]{1,0:T(8,128)(2,1)S(1)} %shard_map.85._), channel_id=1, source_target_pairs={{1,4},{5,8},{9,12},{13,0},{4,1},{8,5},{12,9},{0,13},{3,6},{7,10},{... | collective-permute-start | bytes 430088 | tf_op jit(solution)/shard_map/ppermute | solution.py:305
  36.6 1.4 %collective-permute-start.9 = (bf16[544,128]{1,0:T(8,128)(2,1)S(1)}, bf16[544,128]{1,0:T(8,128)(2,1)S(1)}, u32[]{:S(2)}, u32[]{:S(2)}) collective-permute-start(bf16[544,128]{1,0:T(8,128)(2,1)S(1)} %get-tuple-element.88), channel_id=1, source_target_pairs={{0,1},{1,0},{2,3},{3,2},{4,5},{5,4},{6,7},{7,6},{8,9},{9,8},{10,11... | collective-permute-start | bytes 417800 | tf_op jit(solution)/shard_map/ppermute | solution.py:306
  41.0 6.4 %collective-permute-start.10 = (bf16[544,128]{1,0:T(8,128)(2,1)S(1)}, bf16[544,128]{1,0:T(8,128)(2,1)S(1)}, u32[]{:S(2)}, u32[]{:S(2)}) collective-permute-start(bf16[544,128]{1,0:T(8,128)(2,1)S(1)} %shard_map.89._), channel_id=1, source_target_pairs={{1,4},{5,8},{9,12},{13,0},{4,1},{8,5},{12,9},{0,13},{3,6},{7,10},{... | collective-permute-start | bytes 417800 | tf_op jit(solution)/shard_map/ppermute | solution.py:305
  43.2 1.4 %collective-permute-start.11 = (bf16[512,128]{1,0:T(8,128)(2,1)S(1)}, bf16[512,128]{1,0:T(8,128)(2,1)S(1)}, u32[]{:S(2)}, u32[]{:S(2)}) collective-permute-start(bf16[512,128]{1,0:T(8,128)(2,1)S(1)} %get-tuple-element.93), channel_id=1, source_target_pairs={{0,1},{1,0},{2,3},{3,2},{4,5},{5,4},{6,7},{7,6},{8,9},{9,8},{10,11... | collective-permute-start | bytes 393224 | tf_op jit(solution)/shard_map/ppermute | solution.py:306
  47.5 6.5 %collective-permute-start.12 = (bf16[560,128]{1,0:T(8,128)(2,1)S(1)}, bf16[560,128]{1,0:T(8,128)(2,1)S(1)}, u32[]{:S(2)}, u32[]{:S(2)}) collective-permute-start(bf16[560,128]{1,0:T(8,128)(2,1)S(1)} %shard_map.93._), channel_id=1, source_target_pairs={{1,4},{5,8},{9,12},{13,0},{4,1},{8,5},{12,9},{0,13},{3,6},{7,10},{... | collective-permute-start | bytes 430088 | tf_op jit(solution)/shard_map/ppermute | solution.py:305
  49.9 1.4 %collective-permute-start.13 = (bf16[544,128]{1,0:T(8,128)(2,1)S(1)}, bf16[544,128]{1,0:T(8,128)(2,1)S(1)}, u32[]{:S(2)}, u32[]{:S(2)}) collective-permute-start(bf16[544,128]{1,0:T(8,128)(2,1)S(1)} %get-tuple-element.98), channel_id=1, source_target_pairs={{0,1},{1,0},{2,3},{3,2},{4,5},{5,4},{6,7},{7,6},{8,9},{9,8},{10,11... | collective-permute-start | bytes 417800 | tf_op jit(solution)/shard_map/ppermute | solution.py:306
  54.0 6.3 %collective-permute-start.14 = (bf16[544,128]{1,0:T(8,128)(2,1)S(1)}, bf16[544,128]{1,0:T(8,128)(2,1)S(1)}, u32[]{:S(2)}, u32[]{:S(2)}) collective-permute-start(bf16[544,128]{1,0:T(8,128)(2,1)S(1)} %shard_map.97._), channel_id=1, source_target_pairs={{1,4},{5,8},{9,12},{13,0},{4,1},{8,5},{12,9},{0,13},{3,6},{7,10},{... | collective-permute-start | bytes 417800 | tf_op jit(solution)/shard_map/ppermute | solution.py:305
  56.7 1.4 %collective-permute-start.15 = (bf16[512,128]{1,0:T(8,128)(2,1)S(1)}, bf16[512,128]{1,0:T(8,128)(2,1)S(1)}, u32[]{:S(2)}, u32[]{:S(2)}) collective-permute-start(bf16[512,128]{1,0:T(8,128)(2,1)S(1)} %get-tuple-element.103), channel_id=1, source_target_pairs={{0,1},{1,0},{2,3},{3,2},{4,5},{5,4},{6,7},{7,6},{8,9},{9,8},{10,11... | collective-permute-start | bytes 393224 | tf_op jit(solution)/shard_map/ppermute | solution.py:306
